TPU v7x, 256 devices: a whole 4x4x8 slice. The times are simulated.
256 devices in a mesh: section: 16 (over y_lo, z), tensor: 16 (over x, y_hi, core).
Axes of the slice: x: 4, y: 4 (y_hi: 2, y_lo: 2; y = y_hi * 2 + y_lo), z: 8, core: 2. Of those that a mesh axis runs over, the one named last changes fastest.
Arguments:
- initial_stack_inputs: bfloat16 [3072, 8192], P('section', 'tensor'), may hold values from -54 to 54
- initial_sequence_starts: int32 [16], P('section'), may hold values 0 or 1
- arriving_pieces: bfloat16 [384, 8192], P(None, 'tensor'), may hold values from -54 to 54
- recall_embeddings: bfloat16 [64, 8192], P(None, 'tensor'), may hold values from -54 to 54
- rescaling_factors: float32 [16, 8192], P('section'), may hold values from 0.5 to 1.5
- lookup_projection: bfloat16 [16, 8192, 4096], P('section', None, 'tensor'), may hold values from -0.25 to 0.25
- content_projection: bfloat16 [16, 8192, 4096], P('section', None, 'tensor'), may hold values from -0.25 to 0.25
- write_gate_projection: bfloat16 [16, 8192, 32], P('section', None, 'tensor'), may hold values from -0.25 to 0.25
- final_projection: bfloat16 [16, 4096, 8192], P('section', 'tensor'), may hold values from -0.125 to 0.125
- associative_stores: float32 [16, 32, 128, 128], P('section', 'tensor'), may hold values from -7680 to 7680
- denominator_vectors: float32 [16, 32, 128], P('section', 'tensor'), may hold values from 50 to 200
Outputs:
- wave_front: bfloat16 [3072, 8192], P('section', 'tensor')
All inputs are finite; a program needn't handle non-finite values. No bound on the sum of `initial_sequence_starts` on one device may be relied on, other than what follows from the above.
Results may differ from a plain program's by a relative error of at most 0.022.
Values may be sent and summed in bfloat16 or wider, within the bound.
No kernel may reach another device: no remote copies, remote signals or barrier semaphores. Data moves between devices by JAX's collectives and lax.ppermute only.
A program may use at most 64 MiB of HBM per device.

v0:
```python
import jax
import jax.numpy as jnp
from jax import lax
from jax.sharding import PartitionSpec as P

SEG = 128
MEM = 64


EPS = 1e-05


def shifted_2(value, axis, steps):
    count = lax.axis_size(axis)
    leading, last = (max(0, -steps), min(count, count - steps))
    return lax.ppermute(value, axis, [(source, source + steps) for source in range(leading, last)])


def feature_map(values):
    return jax.nn.elu(values) + 1.0


def section_layer(
    rows_local, sequence_begin_flag, layer_weights, memory_matrix, denominator_vectors, write
):
    gain_row, lookup_projection, content_projection, write_gate_projection, final_projection = (
        layer_weights
    )
    retained = (1 - sequence_begin_flag).astype(jnp.float32)
    memory_matrix = memory_matrix * retained
    denominator_vectors = denominator_vectors * retained
    head_count = memory_matrix.shape[0]
    head_size = memory_matrix.shape[1]
    row_count = rows_local.shape[0]
    bounds = ((0, row_count),)
    outputs = []
    for start_row, stop_row in bounds:
        block_rows = stop_row - start_row
        gathered = lax.all_gather(rows_local, "tensor", axis=1, tiled=True).astype(jnp.float32)
        row_scale = lax.rsqrt(jnp.mean(gathered * gathered, axis=1, keepdims=True) + EPS)
        normed = (gathered * row_scale * gain_row).astype(jnp.bfloat16)
        mapped_keys = feature_map(
            jnp.dot(normed, lookup_projection, preferred_element_type=jnp.float32)
        ).reshape(block_rows, head_count, head_size)
        values = jnp.dot(normed, content_projection, preferred_element_type=jnp.float32).reshape(
            block_rows, head_count, head_size
        )
        readout_numerator = jnp.einsum(
            "dyt,ytn->dyn", mapped_keys, memory_matrix, precision=lax.Precision.HIGHEST
        )
        denominator = (
            jnp.einsum(
                "rhk,hk->rh", mapped_keys, denominator_vectors, precision=lax.Precision.HIGHEST
            )
            + 1.0
        )
        readout = readout_numerator / denominator[:, :, None]
        partial_term = jnp.dot(
            readout.astype(jnp.bfloat16).reshape(block_rows, head_count * head_size),
            final_projection,
            preferred_element_type=jnp.float32,
        )
        summed = lax.psum_scatter(
            partial_term.astype(jnp.bfloat16), "tensor", scatter_dimension=1, tiled=True
        ).astype(jnp.float32)
        outputs.append((rows_local.astype(jnp.float32) + summed).astype(jnp.bfloat16))
    result = outputs[0]
    if write:
        trailing_keys = mapped_keys[block_rows - MEM :]
        tail_values = values[block_rows - MEM :]
        tail_read = readout[block_rows - MEM :]
        write_gate = jax.nn.sigmoid(
            jnp.dot(
                normed[block_rows - MEM :],
                write_gate_projection,
                preferred_element_type=jnp.float32,
            )
        )
        memory_update = (tail_values - tail_read) * write_gate[:, :, None]
        memory_matrix = memory_matrix + jnp.einsum(
            "nxz,nxa->xza", trailing_keys, memory_update, precision=lax.Precision.HIGHEST
        )
        denominator_vectors = denominator_vectors + jnp.sum(trailing_keys, axis=0)
    return (result, memory_matrix, denominator_vectors)


def local(
    initial_stack_inputs,
    initial_sequence_starts,
    arriving_pieces,
    recall_embeddings,
    rescaling_factors,
    lookup_projection,
    content_projection,
    write_gate_projection,
    final_projection,
    associative_stores,
    denominator_vectors,
):
    section_zero = lax.axis_index("section") == 0
    layer_weights = (
        rescaling_factors[0],
        lookup_projection[0],
        content_projection[0],
        write_gate_projection[0],
        final_projection[0],
    )
    memory_matrix = associative_stores[0]
    normalizer_state = denominator_vectors[0]
    carried_recurrence = initial_stack_inputs
    sequence_begin_flag = initial_sequence_starts[0]
    step_count = arriving_pieces.shape[0] // SEG + 1
    for wave_step in range(step_count):
        if wave_step > 0:
            shifted, shifted_flag = shifted_2(
                (carried_recurrence, jnp.reshape(sequence_begin_flag, (1,))), "section", 1
            )
            arriving = jnp.concatenate(
                [arriving_pieces[(wave_step - 1) * SEG : wave_step * SEG], recall_embeddings],
                axis=0,
            )
            carried_recurrence = jnp.where(section_zero, arriving, shifted)
            sequence_begin_flag = jnp.where(section_zero, jnp.zeros((), jnp.int32), shifted_flag[0])
        carried_recurrence, memory_matrix, normalizer_state = section_layer(
            carried_recurrence,
            sequence_begin_flag,
            layer_weights,
            memory_matrix,
            normalizer_state,
            wave_step + 1 < step_count,
        )
    return carried_recurrence


def solution(mesh):
    return jax.shard_map(
        local,
        mesh=mesh,
        in_specs=(
            P("section", "tensor"),
            P("section"),
            P(None, "tensor"),
            P(None, "tensor"),
            P("section", None),
            P("section", None, "tensor"),
            P("section", None, "tensor"),
            P("section", None, "tensor"),
            P("section", "tensor", None),
            P("section", "tensor", None, None),
            P("section", "tensor", None),
        ),
        out_specs=P("section", "tensor"),
        check_vma=False,
    )
```

profile of v0, /device:TPU:8, one launch (start us, length us, event | category | flops | bytes accessed | tf_op | source)
XLA Modules:
  0.0 661.6 jit_solution(10295347878264558927)
XLA Ops:
  7.3 3.8 collective-permute-start.1
  11.8 4.7 collective-permute-done.1
  17.2 54.0 %all-gather.5.cloned.1.call-done = bf16[192,8192]{1,0:T(8,128)(2,1)} async-done(((bf16[192,512]{1,0:T(8,128)(2,1)}), bf16[192,8192]{1,0:T(8,128)(2,1)}) %all-gather.5.cloned.1.call-update) | async-done | bytes 3145744 | tf_op jit(solution)/shard_map/all_gather | solution.py:39
  71.2 2.8 fusion
  73.9 2.8 fusion.2
  76.7 1.1 fusion.69
  79.3 2.6 convolution_convert_fusion.3
  82.0 81.8 %reduce-scatter.5.cloned.1.call-done = bf16[192,512]{1,0:T(8,128)(2,1)} async-done(((bf16[192,8192]{1,0:T(8,128)(2,1)}), bf16[192,512]{1,0:T(8,128)(2,1)}) %reduce-scatter.5.cloned.1.call-update) | async-done | bytes 196624 | tf_op jit(solution)/shard_map/reduce_scatter | solution.py:63
  163.8 1.0 add_convert_fusion.3
  164.8 3.5 collective-permute-start
  168.3 1.8 fusion.168
  170.1 4.6 collective-permute-done
  175.9 3.0 fusion.39
  178.9 1.4 convolution_add_fusion.2
  180.3 52.4 %all-gather.7.cloned.1.call-done = bf16[192,8192]{1,0:T(8,128)(2,1)} async-done(((bf16[192,512]{1,0:T(8,128)(2,1)}), bf16[192,8192]{1,0:T(8,128)(2,1)}) %all-gather.7.cloned.1.call-update) | async-done | bytes 3145744 | tf_op jit(solution)/shard_map/all_gather | solution.py:39
  232.7 2.8 fusion.3
  235.5 2.7 fusion.5
  238.2 1.1 fusion.75
  241.0 2.6 convolution_convert_fusion.2
  243.7 81.8 %reduce-scatter.7.cloned.1.call-done = bf16[192,512]{1,0:T(8,128)(2,1)} async-done(((bf16[192,8192]{1,0:T(8,128)(2,1)}), bf16[192,512]{1,0:T(8,128)(2,1)}) %reduce-scatter.7.cloned.1.call-update) | async-done | bytes 196624 | tf_op jit(solution)/shard_map/reduce_scatter | solution.py:63
  325.5 1.0 add_convert_fusion.2
  326.5 3.5 collective-permute-start.2
  330.0 6.3 collective-permute-done.2
  336.3 1.6 fusion.64
  338.0 3.2 collective-permute-start.3
  341.2 4.3 collective-permute-done.3
  346.2 3.2 collective-permute-start.5
  349.4 4.3 collective-permute-done.5
  354.7 3.7 fusion.42
  358.3 36.9 %all-gather.9.cloned.1.call-done = bf16[192,8192]{1,0:T(8,128)(2,1)} async-done(((bf16[192,512]{1,0:T(8,128)(2,1)}), bf16[192,8192]{1,0:T(8,128)(2,1)}) %all-gather.9.cloned.1.call-update) | async-done | bytes 3145744 | tf_op jit(solution)/shard_map/all_gather | solution.py:39
  395.3 2.8 fusion.6
  398.0 2.7 fusion.8
  400.8 1.1 fusion.81
  401.9 1.1 slice_bitcast_fusion
  403.5 1.3 convolution_add_fusion.1
  406.4 2.6 convolution_convert_fusion.1
  409.1 81.8 %reduce-scatter.9.cloned.1.call-done = bf16[192,512]{1,0:T(8,128)(2,1)} async-done(((bf16[192,8192]{1,0:T(8,128)(2,1)}), bf16[192,512]{1,0:T(8,128)(2,1)}) %reduce-scatter.9.cloned.1.call-update) | async-done | bytes 196624 | tf_op jit(solution)/shard_map/reduce_scatter | solution.py:63
  491.9 3.6 collective-permute-start.4
  495.5 6.3 collective-permute-done.4
  501.9 1.6 fusion.63
  504.0 3.0 fusion.45
  507.0 1.3 convolution_add_fusion
  508.3 52.5 %all-gather.11.cloned.1.call-done = bf16[192,8192]{1,0:T(8,128)(2,1)} async-done(((bf16[192,512]{1,0:T(8,128)(2,1)}), bf16[192,8192]{1,0:T(8,128)(2,1)}) %all-gather.11.cloned.1.call-update) | async-done | bytes 3145744 | tf_op jit(solution)/shard_map/all_gather | solution.py:39
  560.8 2.6 fusion.9
  563.4 4.4 fusion.94
  568.6 2.6 convolution_convert_fusion
  571.2 81.9 %reduce-scatter.11.cloned.1.call-done = bf16[192,512]{1,0:T(8,128)(2,1)} async-done(((bf16[192,8192]{1,0:T(8,128)(2,1)}), bf16[192,512]{1,0:T(8,128)(2,1)}) %reduce-scatter.11.cloned.1.call-update) | async-done | bytes 196624 | tf_op jit(solution)/shard_map/reduce_scatter | solution.py:63
  653.1 1.7 add_convert_fusion
  (90 shorter events, 10.0 us)
Async XLA Ops:
  6.5 169.0 %copy-start = (bf16[1,8192,2]{1,2,0:T(2,128)(2,1)S(1)}, bf16[1,8192,2]{1,2,0:T(2,128)(2,1)}, u32[]{:S(2)}) copy-start(bf16[1,8192,2]{1,2,0:T(2,128)(2,1)} %param.18) | copy-start | bytes 98308
  6.5 64.6 %all-gather.5.cloned.1.call-start = ((), (), s32[]{:S(2)}) async-start(), calls=%async_computation.4 | async-start | bytes 3342336 | tf_op jit(solution)/shard_map/all_gather | solution.py:39
  7.3 156.6 %reduce-scatter.5.cloned.1.call-start = ((), (), s32[]{:S(2)}) async-start(), calls=%async_computation.5 | async-start | bytes 3342336 | tf_op jit(solution)/shard_map/reduce_scatter | solution.py:63
  7.3 9.3 %collective-permute-start.1 = (s32[1]{0:T(128)}, s32[1]{0:T(128)}, u32[]{:S(2)}, u32[]{:S(2)}) collective-permute-start(s32[1]{0:T(128)} %param.12), channel_id=1, source_target_pairs={{0,16},{16,32},{32,48},{48,64},{64,80},{80,96},{96,112},{112,128},... | collective-permute-start | bytes 20 | tf_op jit(solution)/shard_map/ppermute | solution.py:16
  71.2 5.5 copy-start.1
  76.7 1.1 copy-start.24
  76.7 1.6 copy-start.23
  76.7 2.6 copy-start.4
  78.6 0.7 copy-start.15
  79.3 84.5 %copy-start.12 = (bf16[192,512]{1,0:T(8,128)(2,1)S(1)}, bf16[192,512]{1,0:T(8,128)(2,1)}, u32[]{:S(2)}) copy-start(bf16[192,512]{1,0:T(8,128)(2,1)} %param.11) | copy-start | bytes 589828
  81.9 92.7 %copy-start.13 = (bf16[64,512]{1,0:T(8,128)(2,1)S(1)}, bf16[64,512]{1,0:T(8,128)(2,1)}, u32[]{:S(2)}) copy-start(bf16[64,512]{1,0:T(8,128)(2,1)} %param.14) | copy-start | bytes 196612
  82.0 150.7 %all-gather.7.cloned.1.call-start = ((), (), s32[]{:S(2)}) async-start(), calls=%async_computation.6 | async-start | bytes 3342336 | tf_op jit(solution)/shard_map/all_gather | solution.py:39
  164.8 9.8 %collective-permute-start = (bf16[192,512]{1,0:T(8,128)(2,1)S(1)}, bf16[192,512]{1,0:T(8,128)(2,1)S(1)}, u32[]{:S(2)}, u32[]{:S(2)}) collective-permute-start(bf16[192,512]{1,0:T(8,128)(2,1)S(1)} %add_convert_fusion.3), channel_id=1, source_target_pairs={{0,16},{16,32},{32,48},{48,64},{64,80},{80,96},{96,112},{112,128},... | collective-permute-start | bytes 589832 | tf_op jit(solution)/shard_map/ppermute | solution.py:16
  175.4 150.1 %reduce-scatter.7.cloned.1.call-start = ((), (), s32[]{:S(2)}) async-start(), calls=%async_computation.7 | async-start | bytes 3342336 | tf_op jit(solution)/shard_map/reduce_scatter | solution.py:63
  175.9 59.6 %copy-start.21 = (f32[1,8192]{1,0:T(1,128)S(1)}, f32[1,8192]{1,0:T(1,128)}, u32[]{:S(2)}) copy-start(f32[1,8192]{1,0:T(1,128)} %param.15) | copy-start | bytes 98308
  180.3 59.5 %copy-start.17 = (f32[2,128,128]{2,1,0:T(8,128)}, f32[2,128,128]{2,1,0:T(8,128)S(1)}, u32[]{:S(2)}) copy-start(f32[2,128,128]{2,1,0:T(8,128)S(1)} %convolution_add_fusion.2) | copy-start | bytes 393220
  232.7 5.5 copy-start.2
  238.2 2.8 copy-start.5
  239.3 0.7 copy-start.11
  240.3 0.7 copy-start.14
  241.0 84.5 %copy-start.10 = (bf16[192,512]{1,0:T(8,128)(2,1)S(1)}, bf16[192,512]{1,0:T(8,128)(2,1)}, u32[]{:S(2)}) copy-start(bf16[192,512]{1,0:T(8,128)(2,1)} %fusion.65) | copy-start | bytes 589828
  243.6 151.6 %all-gather.9.cloned.1.call-start = ((), (), s32[]{:S(2)}) async-start(), calls=%async_computation.8 | async-start | bytes 3342336 | tf_op jit(solution)/shard_map/all_gather | solution.py:39
  326.5 9.8 %collective-permute-start.2 = (bf16[192,512]{1,0:T(8,128)(2,1)S(1)}, bf16[192,512]{1,0:T(8,128)(2,1)S(1)}, u32[]{:S(2)}, u32[]{:S(2)}) collective-permute-start(bf16[192,512]{1,0:T(8,128)(2,1)S(1)} %add_convert_fusion.2), channel_id=1, source_target_pairs={{0,16},{16,32},{32,48},{48,64},{64,80},{80,96},{96,112},{112,128},... | collective-permute-start | bytes 589832 | tf_op jit(solution)/shard_map/ppermute | solution.py:16
  338.0 153.0 %reduce-scatter.9.cloned.1.call-start = ((), (), s32[]{:S(2)}) async-start(), calls=%async_computation.9 | async-start | bytes 3342336 | tf_op jit(solution)/shard_map/reduce_scatter | solution.py:63
  338.0 7.5 %collective-permute-start.3 = (s32[1]{0:T(128)}, s32[1]{0:T(128)}, u32[]{:S(2)}, u32[]{:S(2)}) collective-permute-start(s32[1]{0:T(128)} %bitcast.20), channel_id=1, source_target_pairs={{0,16},{16,32},{32,48},{48,64},{64,80},{80,96},{96,112},{112,128},... | collective-permute-start | bytes 20 | tf_op jit(solution)/shard_map/ppermute | solution.py:16
  346.2 7.5 %collective-permute-start.5 = (s32[1]{0:T(128)}, s32[1]{0:T(128)}, u32[]{:S(2)}, u32[]{:S(2)}) collective-permute-start(s32[1]{0:T(128)} %bitcast.28), channel_id=1, source_target_pairs={{0,16},{16,32},{32,48},{48,64},{64,80},{80,96},{96,112},{112,128},... | collective-permute-start | bytes 20 | tf_op jit(solution)/shard_map/ppermute | solution.py:16
  395.3 5.5 copy-start.3
  400.8 2.7 copy-start.18
  400.8 2.7 copy-start.22
  400.8 5.6 copy-start.6
  404.8 0.7 copy-start.19
  405.7 0.7 copy-start.16
  406.4 84.5 %copy-start.8 = (bf16[192,512]{1,0:T(8,128)(2,1)S(1)}, bf16[192,512]{1,0:T(8,128)(2,1)}, u32[]{:S(2)}) copy-start(bf16[192,512]{1,0:T(8,128)(2,1)} %fusion.64) | copy-start | bytes 589828
  409.1 151.8 %all-gather.11.cloned.1.call-start = ((), (), s32[]{:S(2)}) async-start(), calls=%async_computation.10 | async-start | bytes 3342336 | tf_op jit(solution)/shard_map/all_gather | solution.py:39
  491.9 15.1 %copy-start.20 = (f32[2,128,128]{2,1,0:T(8,128)S(1)}, f32[2,128,128]{2,1,0:T(8,128)}, u32[]{:S(2)}) copy-start(f32[2,128,128]{2,1,0:T(8,128)} %copy-done.19) | copy-start | bytes 393220
  491.9 10.0 %collective-permute-start.4 = (bf16[192,512]{1,0:T(8,128)(2,1)S(1)}, bf16[192,512]{1,0:T(8,128)(2,1)S(1)}, u32[]{:S(2)}, u32[]{:S(2)}) collective-permute-start(bf16[192,512]{1,0:T(8,128)(2,1)S(1)} %add_convert_fusion.1), channel_id=1, source_target_pairs={{0,16},{16,32},{32,48},{48,64},{64,80},{80,96},{96,112},{112,128},... | collective-permute-start | bytes 589832 | tf_op jit(solution)/shard_map/ppermute | solution.py:16
  503.5 149.6 %reduce-scatter.11.cloned.1.call-start = ((), (), s32[]{:S(2)}) async-start(), calls=%async_computation.11 | async-start | bytes 3342336 | tf_op jit(solution)/shard_map/reduce_scatter | solution.py:63
  563.4 5.1 copy-start.7
  568.6 84.5 %copy-start.9 = (bf16[192,512]{1,0:T(8,128)(2,1)S(1)}, bf16[192,512]{1,0:T(8,128)(2,1)}, u32[]{:S(2)}) copy-start(bf16[192,512]{1,0:T(8,128)(2,1)} %fusion.63) | copy-start | bytes 589828
Sparse Core Ops, SparseCore 0:
  9.9 61.2 all-gather.4
  82.1 81.7 reduce-scatter.4
  175.6 57.0 all-gather.6
  243.8 81.7 reduce-scatter.6
  338.1 57.1 all-gather.8
  409.2 81.7 reduce-scatter.8
  503.7 57.0 all-gather.10
  571.4 81.7 reduce-scatter.10
where the time goes:
time: 663 us; the launch traced here: 662 us
  waiting for transfers between devices  555 us (84%)
  matrix products  35.7 us (5%)
  other arithmetic  28.9 us (4%)
  starting transfers between devices  21.1 us (3%)
  between operations  16.5 us (2%)
    reduce_scatter x4, waiting for transfers between devices, section_layer(): lax.psum_scatter(partial_term.astype(jnp.bfloat16), 'tensor', scatter_dim...  327 us
    all_gather x4, waiting for transfers between devices, section_layer(): lax.all_gather(rows_local, 'tensor', axis=1, tiled=True).astype(jnp.float32)  196 us
    ppermute x6, waiting for transfers between devices, shifted_2(): lax.ppermute(value, axis, [(source, source + steps) for source in range(l...  30.6 us
    ppermute x6, starting transfers between devices, shifted_2(): lax.ppermute(value, axis, [(source, source + steps) for source in range(l...  20.8 us
  transfers between devices with their start and end apart: 14, of which 14 were waited for; matrix products, arithmetic and copies ran while one was open for 2% of the time, Pallas kernels for 0%

commit v1 on v0

v1 whole, which is shorter than its diff:
```python
import functools

import jax
import jax.numpy as jnp
from jax import lax
from jax.experimental import pallas as pl
from jax.experimental.pallas import tpu as pltpu
from jax.sharding import Mesh
from jax.sharding import PartitionSpec as P

SEG = 128
MEM = 64
EPS = 1e-05
AXES = ("y_lo", "z", "x", "y_hi", "core")
SECTION = ("y_lo", "z")
TENSOR = ("x", "y_hi", "core")
CHIPS = ("x", "y_hi")
N_CHIPS = 8
BLOCK = 512
HEADS = 2
HD = 128
WIDE = HEADS * HD
SIDE = 128
HALF = 2 * WIDE + SIDE
HIDDEN = 8192
VMEM_LIMIT = 48 * 2**20
HIGHEST = lax.Precision.HIGHEST


def swap(value, axis):
    return lax.ppermute(value, axis, [(0, 1), (1, 0)])


def next_section(value, steps=1):
    return lax.ppermute(value, SECTION, [(i, i + steps) for i in range(16 - steps)])


def pick_kernel(core_ref, k_ref, v_ref, f_ref, w_out, f_out):
    w_out[0, :, :WIDE] = k_ref[0]
    w_out[0, :, WIDE:] = v_ref[0]
    f_out[...] = f_ref[...]


def pick(core, wk, wv, f):
    def theirs(b, core_ref):
        return (2 * b + 1 - core_ref[0], 0, 0)

    return pl.pallas_call(
        pick_kernel,
        grid_spec=pltpu.PrefetchScalarGridSpec(
            num_scalar_prefetch=1,
            grid=(N_CHIPS,),
            in_specs=[
                pl.BlockSpec((1, BLOCK, WIDE), theirs),
                pl.BlockSpec((1, BLOCK, WIDE), theirs),
                pl.BlockSpec((WIDE, BLOCK), lambda b, core_ref: (0, 2 * b + 1 - core_ref[0])),
            ],
            out_specs=[
                pl.BlockSpec((1, BLOCK, 2 * WIDE), lambda b, core_ref: (b, 0, 0)),
                pl.BlockSpec((WIDE, BLOCK), lambda b, core_ref: (0, b)),
            ],
        ),
        out_shape=[
            jax.ShapeDtypeStruct((N_CHIPS, BLOCK, 2 * WIDE), jnp.bfloat16),
            jax.ShapeDtypeStruct((WIDE, N_CHIPS * BLOCK), jnp.bfloat16),
        ],
        compiler_params=pltpu.CompilerParams(vmem_limit_bytes=16 * 2**20),
        cost_estimate=pl.CostEstimate(flops=0, bytes_accessed=12 * 2**20, transcendentals=0),
    )(core, wk, wv, f)


def project_kernel(
    write, core_ref, x_ref, gain_ref, k_ref, v_ref, got_ref, gate_ref, theirs_ref, mine_out, other_out
):
    core = core_ref[0]
    rows = x_ref.shape[1]
    dot = functools.partial(jnp.dot, preferred_element_type=jnp.float32)
    turned = functools.partial(
        lax.dot_general,
        dimension_numbers=(((1,), (1,)), ((), ())),
        preferred_element_type=jnp.float32,
    )
    k, v, other, squares, gate, theirs = 0.0, 0.0, 0.0, 0.0, 0.0, 0.0
    for b in range(N_CHIPS):
        wide = x_ref[b].astype(jnp.float32)
        squares += wide * wide
        scaled = (wide * gain_ref[b]).astype(jnp.bfloat16)
        k += dot(scaled, k_ref[2 * b + core])
        v += dot(scaled, v_ref[2 * b + core])
        other += dot(scaled, got_ref[b])
        if write:
            gate += turned(scaled[rows - MEM :], gate_ref[b])
            theirs += turned(scaled[rows - MEM :], theirs_ref[b])
    squares = jnp.sum(squares, axis=1, keepdims=True)
    mine_out[:, :WIDE] = k
    mine_out[:, WIDE : 2 * WIDE] = v
    other_out[:, : 2 * WIDE] = other
    lane = lax.broadcasted_iota(jnp.int32, (rows, SIDE), 1)
    side = jnp.where(lane == HEADS, squares, 0.0)
    mine_out[:, 2 * WIDE :] = side
    other_out[:, 2 * WIDE :] = side
    if write:
        mine_out[rows - MEM :, 2 * WIDE :] = side[rows - MEM :] + gate
        other_out[rows - MEM :, 2 * WIDE :] = side[rows - MEM :] + theirs


def project(core, x, gain, wk, wv, got, gate, theirs, write):
    rows = x.shape[1]
    out = jax.ShapeDtypeStruct((rows, HALF), jnp.float32)
    vmem = pl.BlockSpec(memory_space=pltpu.VMEM)
    return pl.pallas_call(
        functools.partial(project_kernel, write),
        in_specs=[pl.BlockSpec(memory_space=pltpu.SMEM)] + [vmem] * 7,
        out_specs=[vmem] * 2,
        out_shape=[out, out],
        compiler_params=pltpu.CompilerParams(vmem_limit_bytes=VMEM_LIMIT),
        cost_estimate=pl.CostEstimate(
            flops=2 * rows * 4096 * 1280, bytes_accessed=12 * 2**20, transcendentals=0
        ),
    )(core, x, gain, wk, wv, got, gate, theirs)


def memory_kernel(write, mine_ref, got_ref, keep_ref, a_ref, z_ref, read_ref, a_out, z_out):
    both = mine_ref[...] + got_ref[...]
    rows = both.shape[0]
    side = both[:, 2 * WIDE :]
    scale = lax.rsqrt(side[:, HEADS : HEADS + 1] * (1.0 / HIDDEN) + EPS)
    keep = keep_ref[0, 0]
    for h in range(HEADS):
        a = a_ref[h] * keep
        z = z_ref[h : h + 1] * keep
        k = both[:, h * HD : (h + 1) * HD] * scale
        k = jnp.where(k > 0, k + 1.0, jnp.exp(jnp.minimum(k, 0.0)))
        v = both[:, WIDE + h * HD : WIDE + (h + 1) * HD] * scale
        top = jnp.dot(k, a, precision=HIGHEST, preferred_element_type=jnp.float32)
        bottom = jnp.sum(k * z, axis=1, keepdims=True) + 1.0
        read = top / bottom
        read_ref[:, h * HD : (h + 1) * HD] = read.astype(jnp.bfloat16)
        if write:
            logit = side[rows - MEM :, h : h + 1] * scale[rows - MEM :]
            gate = 1.0 / (1.0 + jnp.exp(-logit))
            change = (v[rows - MEM :] - read[rows - MEM :]) * gate
            tail = k[rows - MEM :]
            a_out[h] = a + lax.dot_general(
                tail,
                change,
                (((0,), (0,)), ((), ())),
                precision=HIGHEST,
                preferred_element_type=jnp.float32,
            )
            z_out[h : h + 1] = z + jnp.sum(tail, axis=0, keepdims=True)
        else:
            a_out[h] = a
            z_out[h : h + 1] = z


def memory(mine, got, keep, a, z, write):
    rows = mine.shape[0]
    vmem = pl.BlockSpec(memory_space=pltpu.VMEM)
    return pl.pallas_call(
        functools.partial(memory_kernel, write),
        in_specs=[vmem, vmem, pl.BlockSpec(memory_space=pltpu.SMEM), vmem, vmem],
        out_specs=[vmem] * 3,
        out_shape=[
            jax.ShapeDtypeStruct((rows, WIDE), jnp.bfloat16),
            jax.ShapeDtypeStruct(a.shape, a.dtype),
            jax.ShapeDtypeStruct(z.shape, z.dtype),
        ],
        compiler_params=pltpu.CompilerParams(vmem_limit_bytes=16 * 2**20),
        cost_estimate=pl.CostEstimate(
            flops=2 * rows * WIDE * HD * 6, bytes_accessed=rows * HALF * 8, transcendentals=0
        ),
    )(mine, got, keep, a, z)


def output_kernel(core_ref, near_ref, far_ref, f_ref, got_ref, p_ref):
    core = core_ref[0]
    near, far = near_ref[...], far_ref[...]
    for b in range(N_CHIPS):
        columns = pl.ds(pl.multiple_of((2 * b + core) * BLOCK, BLOCK), BLOCK)
        part = jnp.dot(near, f_ref[:, columns], preferred_element_type=jnp.float32)
        part += jnp.dot(
            far, got_ref[:, b * BLOCK : (b + 1) * BLOCK], preferred_element_type=jnp.float32
        )
        p_ref[b] = part.astype(jnp.bfloat16)


def output(core, near, far, f, got):
    rows = near.shape[0]
    vmem = pl.BlockSpec(memory_space=pltpu.VMEM)
    return pl.pallas_call(
        output_kernel,
        in_specs=[pl.BlockSpec(memory_space=pltpu.SMEM)] + [vmem] * 4,
        out_specs=vmem,
        out_shape=jax.ShapeDtypeStruct((N_CHIPS, rows, BLOCK), jnp.bfloat16),
        compiler_params=pltpu.CompilerParams(vmem_limit_bytes=VMEM_LIMIT),
        cost_estimate=pl.CostEstimate(
            flops=2 * rows * 2 * WIDE * 4096, bytes_accessed=4096 * 2 * WIDE * 2, transcendentals=0
        ),
    )(core, near, far, f, got)


def gather_chips(x):
    return lax.all_to_all(
        jnp.broadcast_to(x[None], (N_CHIPS,) + x.shape), CHIPS, 0, 0, tiled=True
    )


def scatter_chips(p, x):
    parts = lax.all_to_all(p, CHIPS, 0, 0, tiled=True)
    total = jnp.sum(parts.astype(jnp.float32), axis=0)
    return (x.astype(jnp.float32) + total).astype(jnp.bfloat16)


def local(
    initial_stack_inputs,
    initial_sequence_starts,
    arriving_pieces,
    recall_embeddings,
    rescaling_factors,
    lookup_projection,
    content_projection,
    write_gate_projection,
    final_projection,
    associative_stores,
    denominator_vectors,
):
    core = lax.axis_index("core")
    which = core.astype(jnp.int32).reshape(1)
    section_zero = (lax.axis_index("y_lo") == 0) & (lax.axis_index("z") == 0)
    steps = arriving_pieces.shape[0] // SEG + 1

    x = initial_stack_inputs
    gathered = gather_chips(x)
    flags = [initial_sequence_starts]
    for t in range(1, steps):
        flags.append(next_section(initial_sequence_starts, t))

    wk = lookup_projection[0].reshape(2 * N_CHIPS, BLOCK, WIDE)
    wv = content_projection[0].reshape(2 * N_CHIPS, BLOCK, WIDE)
    f = final_projection[0]
    w_sent, f_sent = pick(which, wk, wv, f)
    w_got = swap(w_sent, "core")
    f_got = swap(f_sent, "core")
    gain = lax.dynamic_index_in_dim(
        rescaling_factors.reshape(N_CHIPS, 2, 1, BLOCK), core, 1, keepdims=False
    )
    gates = write_gate_projection[0].T.reshape(HEADS, N_CHIPS, 2, BLOCK).transpose(2, 1, 0, 3)
    fill = ((0, 0), (0, SIDE - HEADS), (0, 0))
    gate = jnp.pad(lax.dynamic_index_in_dim(gates, core, 0, keepdims=False), fill)
    theirs = swap(lax.dynamic_index_in_dim(gates, 1 - core, 0, keepdims=False), "core")
    theirs = jnp.pad(theirs, fill)

    a = associative_stores[0]
    z = denominator_vectors[0]
    a, flags = lax.optimization_barrier((a, flags))
    for t in range(steps):
        write = t + 1 < steps
        if t > 0:
            moved = next_section(x)
            entering = jnp.concatenate(
                [arriving_pieces[(t - 1) * SEG : t * SEG], recall_embeddings], axis=0
            )
            x = jnp.where(section_zero, entering, moved)
            gathered = gather_chips(x)
        keep = (1 - flags[t]).astype(jnp.float32).reshape(1, 1)
        mine, other = project(which, gathered, gain, wk, wv, w_got, gate, theirs, write)
        read, a, z = memory(mine, swap(other, "core"), keep, a, z, write)
        p = output(which, read, swap(read, "core"), f, f_got)
        x = scatter_chips(p, x)
    return x


def solution(mesh):
    fine = Mesh(mesh.devices.reshape(2, 8, 4, 2, 2), AXES)
    return jax.shard_map(
        local,
        mesh=fine,
        in_specs=(
            P(SECTION, TENSOR),
            P(SECTION),
            P(None, TENSOR),
            P(None, TENSOR),
            P(SECTION, None),
            P(SECTION, None, TENSOR),
            P(SECTION, None, TENSOR),
            P(SECTION, None, TENSOR),
            P(SECTION, TENSOR, None),
            P(SECTION, TENSOR, None, None),
            P(SECTION, TENSOR, None),
        ),
        out_specs=P(SECTION, TENSOR),
        check_vma=False,
    )
```

time: 663 us -> 337 us (0.51)
  waiting for transfers between devices: 555 us -> 80.7 us
  blocking collectives: 0 us -> 149 us
  Pallas kernels: 0 us -> 49.3 us
  matrix products: 35.7 us -> 0 us
  other arithmetic: 28.9 us -> 4.12 us
  starting transfers between devices: 21.1 us -> 37 us
  between operations: 16.5 us -> 2.94 us
  local copies, waits for them, and re-layouts: 4.75 us -> 13.1 us
    reduce_scatter x4 -> x0, waiting for transfers between devices: 327 us -> none  [section_layer(): lax.psum_scatter(partial_term.astype(jnp.bfloat16), 'tensor', scatter_dim...]
    all_gather x4 -> x0, waiting for transfers between devices: 196 us -> none  [section_layer(): lax.all_gather(rows_local, 'tensor', axis=1, tiled=True).astype(jnp.float32)]
    all_to_all x0 -> x6, blocking collectives: none -> 149 us  [the longest x3 77.1 us: scatter_chips(): parts = lax.all_to_all(p, CHIPS, 0, 0, tiled=True)]
    pallas_call x0 -> x13, Pallas kernels: none -> 49.3 us  [the longest x4 29 us: project(): pl.pallas_call(functools.partial(project_kernel, write), in_specs=[pl.Blo...]
    all_to_all x0 -> x2, waiting for transfers between devices: none -> 44.1 us  [the longest x1 24.8 us: scatter_chips(): parts = lax.all_to_all(p, CHIPS, 0, 0, tiled=True)]
    dot_general x25 -> x0, matrix products: 35.7 us -> none  [the longest x4 10.5 us: section_layer(): jnp.dot(readout.astype(jnp.bfloat16).reshape(block_rows, head_count * hea...]
    convert_element_type x7 -> x4, other arithmetic: 12.8 us -> 0.87 us  [scatter_chips(): return (x.astype(jnp.float32) + total).astype(jnp.bfloat16)]
    all_to_all x0 -> x2, starting transfers between devices: none -> 10.3 us  [the longest x1 6.03 us: gather_chips(): lax.all_to_all(jnp.broadcast_to(x[None], (N_CHIPS,) + x.shape), CHIPS, 0,...]
  transfers between devices with their start and end apart: 14 -> 19, of which waited for: 14 -> 14; matrix products, arithmetic and copies ran while one was open for 2% -> 1% of each run, Pallas kernels for 0% -> 3%
where the time goes in v1:
time: 337 us; the launch traced here: 336 us
  blocking collectives  149 us (44%)
  waiting for transfers between devices  80.7 us (24%)
  Pallas kernels  49.3 us (15%)
  starting transfers between devices  37 us (11%)
  local copies, waits for them, and re-layouts  13.1 us (4%)
  other arithmetic  4.12 us (1%)
    all_to_all x3, blocking collectives, scatter_chips(): parts = lax.all_to_all(p, CHIPS, 0, 0, tiled=True)  77.1 us
    all_to_all x3, blocking collectives, gather_chips(): lax.all_to_all(jnp.broadcast_to(x[None], (N_CHIPS,) + x.shape), CHIPS, 0,...  71.8 us
    pallas_call x4, Pallas kernels, project(): pl.pallas_call(functools.partial(project_kernel, write), in_specs=[pl.Blo...  29 us
    ppermute x6, waiting for transfers between devices, next_section(): lax.ppermute(value, SECTION, [(i, i + steps) for i in range(16 - steps)])  26.5 us
    ppermute x6, starting transfers between devices, next_section(): lax.ppermute(value, SECTION, [(i, i + steps) for i in range(16 - steps)])  24.9 us
    all_to_all x1, waiting for transfers between devices, scatter_chips(): parts = lax.all_to_all(p, CHIPS, 0, 0, tiled=True)  24.8 us
    all_to_all x1, waiting for transfers between devices, gather_chips(): lax.all_to_all(jnp.broadcast_to(x[None], (N_CHIPS,) + x.shape), CHIPS, 0,...  19.3 us
    pallas_call x4, Pallas kernels, output(): pl.pallas_call(output_kernel, in_specs=[pl.BlockSpec(memory_space=pltpu.S...  12.8 us
  transfers between devices with their start and end apart: 19, of which 14 were waited for; matrix products, arithmetic and copies ran while one was open for 1% of the time, Pallas kernels for 3%

profile of v1, /device:TPU:8, one launch (start us, length us, event | category | flops | bytes accessed | tf_op | source)
XLA Modules:
  0.0 336.1 jit_solution(9138412684119273094)
XLA Ops:
  0.0 2.2 copy-done
  2.2 2.2 copy-done.1
  4.4 2.2 copy-done.2
  6.6 3.9 %shard_map.109 = (bf16[8,512,512]{2,1,0:T(8,128)(2,1)}, bf16[256,4096]{1,0:T(8,128)(2,1)S(1)}) custom-call(s32[1]{0:T(128)} %bitcast.core_ref, bf16[16,512,256]{2,1,0:T(8,128)(2,1)S(1)} %bitcast.35, bf16[16,512,256]{2,1,0:T(8,128)(2,1)S(1)} %bitcast.40, bf16[256,8192]{1,0:T(8,128)(2,1)S(1)} %bitcast.30), custom_call_target="tpu_custom_call" | custom-call | bytes 12582912 | tf_op jit(solution)/shard_map/pallas_call | solution.py:48
  10.4 1.4 broadcast_in_dim.8
  12.3 6.0 %all-to-all-start = ((bf16[8,192,512]{2,1,0:T(8,128)(2,1)}), bf16[8,192,512]{2,1,0:T(8,128)(2,1)}, u32[]{:S(2)}, u32[]{:S(2)}) async-start(bf16[8,192,512]{2,1,0:T(8,128)(2,1)} %broadcast_in_dim.8), calls=%async_computation | async-start | bytes 3145728 | tf_op jit(solution)/shard_map/all_to_all | solution.py:204
  20.5 1.7 collective-permute-done.1
  22.2 1.1 pad.8.theirs_ref
  23.2 19.3 %all-to-all-done.x_ref = bf16[8,192,512]{2,1,0:T(8,128)(2,1)} async-done(((bf16[8,192,512]{2,1,0:T(8,128)(2,1)}), bf16[8,192,512]{2,1,0:T(8,128)(2,1)}, u32[]{:S(2)}, u32[]{:S(2)}) %all-to-all-start) | async-done | bytes 1572896 | tf_op jit(solution)/shard_map/all_to_all | solution.py:204
  42.6 1.2 copy-done.3
  43.8 7.8 %shard_map.110 = (f32[192,640]{1,0:T(8,128)S(1)}, f32[192,640]{1,0:T(8,128)S(1)}) custom-call(s32[1]{0:T(128)} %bitcast.core_ref, bf16[8,192,512]{2,1,0:T(8,128)(2,1)} %all-to-all-done.x_ref, f32[8,1,512]{2,1,0:T(1,128)S(1)} %dynamic-slice_bitcast_fusion.gain_ref, bf16[16,512,256]{2,1,0:T(8,128)(2,1)} %bitcast.31, bf16[16,512,256]{2,1,0:T(8,128)(2,1)} %bitcast.36, ...), custom_call_target="tpu_custom_call" | custom-call | flops 2013265920 | bytes 12582912 | tf_op jit(solution)/shard_map/pallas_call | solution.py:111
  51.7 3.8 %collective-permute-start.3 = (s32[1]{0:T(128)}, s32[1]{0:T(128)}, u32[]{:S(2)}, u32[]{:S(2)}) collective-permute-start(s32[1]{0:T(128)} %param.12), channel_id=1, source_target_pairs={{0,16},{16,32},{32,48},{48,64},{64,80},{80,96},{96,112},{112,128},... | collective-permute-start | bytes 20 | tf_op jit(solution)/shard_map/ppermute | solution.py:35
  55.5 5.2 %collective-permute-start.4 = (s32[1]{0:T(128)}, s32[1]{0:T(128)}, u32[]{:S(2)}, u32[]{:S(2)}) collective-permute-start(s32[1]{0:T(128)} %param.12), channel_id=1, source_target_pairs={{0,32},{16,48},{32,64},{48,80},{64,96},{80,112},{96,128},{112,144}... | collective-permute-start | bytes 20 | tf_op jit(solution)/shard_map/ppermute | solution.py:35
  60.7 5.9 %collective-permute-start.5 = (s32[1]{0:T(128)}, s32[1]{0:T(128)}, u32[]{:S(2)}, u32[]{:S(2)}) collective-permute-start(s32[1]{0:T(128)} %param.12), channel_id=1, source_target_pairs={{0,48},{16,64},{32,80},{48,96},{64,112},{80,128},{96,144},{112,160... | collective-permute-start | bytes 20 | tf_op jit(solution)/shard_map/ppermute | solution.py:35
  67.4 2.9 collective-permute-done.5
  70.3 1.0 shard_map.111
  71.4 1.3 collective-permute-done.6.far_ref
  72.7 3.2 shard_map.112
  75.9 1.1 copy-done.5
  77.1 4.3 %all-to-all-start.1 = ((bf16[8,192,512]{2,1,0:T(8,128)(2,1)}), bf16[8,192,512]{2,1,0:T(8,128)(2,1)}, u32[]{:S(2)}, u32[]{:S(2)}) async-start(bf16[8,192,512]{2,1,0:T(8,128)(2,1)} %copy-done.5), calls=%async_computation.1 | async-start | bytes 3145728 | tf_op jit(solution)/shard_map/all_to_all | solution.py:210
  81.4 24.8 %all-to-all-done.1 = bf16[8,192,512]{2,1,0:T(8,128)(2,1)} async-done(((bf16[8,192,512]{2,1,0:T(8,128)(2,1)}), bf16[8,192,512]{2,1,0:T(8,128)(2,1)}, u32[]{:S(2)}, u32[]{:S(2)}) %all-to-all-start.1) | async-done | bytes 1572896 | tf_op jit(solution)/shard_map/all_to_all | solution.py:210
  106.2 1.7 convert_reduce_fusion.3
  108.0 5.0 %collective-permute-start.8 = (bf16[192,512]{1,0:T(8,128)(2,1)S(1)}, bf16[192,512]{1,0:T(8,128)(2,1)S(1)}, u32[]{:S(2)}, u32[]{:S(2)}) collective-permute-start(bf16[192,512]{1,0:T(8,128)(2,1)S(1)} %add_convert_fusion.3), channel_id=1, source_target_pairs={{0,16},{16,32},{32,48},{48,64},{64,80},{80,96},{96,112},{112,128},... | collective-permute-start | bytes 589832 | tf_op jit(solution)/shard_map/ppermute | solution.py:35
  113.1 5.2 %collective-permute-done.8 = bf16[192,512]{1,0:T(8,128)(2,1)S(1)} collective-permute-done((bf16[192,512]{1,0:T(8,128)(2,1)S(1)}, bf16[192,512]{1,0:T(8,128)(2,1)S(1)}, u32[]{:S(2)}, u32[]{:S(2)}) %collective-permute-start.8) | collective-permute-done | bytes 196640 | tf_op jit(solution)/shard_map/ppermute | solution.py:35
  118.4 24.9 %all_to_all.40.x_ref = bf16[8,192,512]{2,1,0:T(8,128)(2,1)S(1)} all-to-all(bf16[8,192,512]{2,1,0:T(8,128)(2,1)S(1)} %broadcast_in_dim.9), channel_id=1, replica_groups=mesh['y_lo'=2,'z'=8,'x'=4,'y_hi'=2,'core'=2] {'x','y_hi'}, dimensions={0} | all-to-all | bytes 3145728 | tf_op jit(solution)/shard_map/all_to_all | solution.py:204
  143.4 7.3 %shard_map.113 = (f32[192,640]{1,0:T(8,128)S(1)}, f32[192,640]{1,0:T(8,128)S(1)}) custom-call(s32[1]{0:T(128)} %bitcast.core_ref, bf16[8,192,512]{2,1,0:T(8,128)(2,1)S(1)} %all_to_all.40.x_ref, f32[8,1,512]{2,1,0:T(1,128)S(1)} %dynamic-slice_bitcast_fusion.gain_ref, bf16[16,512,256]{2,1,0:T(8,128)(2,1)} %bitcast.32, bf16[16,512,256]{2,1,0:T(8,128)(2,1)} %bitcast.37, ...), custom_call_target="tpu_custom_call" | custom-call | flops 2013265920 | bytes 12582912 | tf_op jit(solution)/shard_map/pallas_call | solution.py:111
  151.3 1.3 collective-permute-done.9.got_ref
  152.6 1.0 shard_map.114
  154.0 1.2 collective-permute-done.10.far_ref
  155.2 3.2 shard_map.115
  158.4 25.7 %all_to_all.41 = bf16[8,192,512]{2,1,0:T(8,128)(2,1)S(1)} all-to-all(bf16[8,192,512]{2,1,0:T(8,128)(2,1)S(1)} %shard_map.115), channel_id=1, replica_groups=mesh['y_lo'=2,'z'=8,'x'=4,'y_hi'=2,'core'=2] {'x','y_hi'}, dimensions={0} | all-to-all | bytes 3145728 | tf_op jit(solution)/shard_map/all_to_all | solution.py:210
  184.4 2.9 collective-permute-start.11
  187.3 7.9 %collective-permute-done.11 = bf16[192,512]{1,0:T(8,128)(2,1)S(1)} collective-permute-done((bf16[192,512]{1,0:T(8,128)(2,1)S(1)}, bf16[192,512]{1,0:T(8,128)(2,1)S(1)}, u32[]{:S(2)}, u32[]{:S(2)}) %collective-permute-start.11) | collective-permute-done | bytes 196640 | tf_op jit(solution)/shard_map/ppermute | solution.py:35
  195.4 23.9 %all_to_all.42.x_ref = bf16[8,192,512]{2,1,0:T(8,128)(2,1)S(1)} all-to-all(bf16[8,192,512]{2,1,0:T(8,128)(2,1)S(1)} %broadcast_in_dim.10), channel_id=1, replica_groups=mesh['y_lo'=2,'z'=8,'x'=4,'y_hi'=2,'core'=2] {'x','y_hi'}, dimensions={0} | all-to-all | bytes 3145728 | tf_op jit(solution)/shard_map/all_to_all | solution.py:204
  219.3 7.3 %shard_map.116 = (f32[192,640]{1,0:T(8,128)S(1)}, f32[192,640]{1,0:T(8,128)S(1)}) custom-call(s32[1]{0:T(128)} %bitcast.core_ref, bf16[8,192,512]{2,1,0:T(8,128)(2,1)S(1)} %all_to_all.42.x_ref, f32[8,1,512]{2,1,0:T(1,128)S(1)} %dynamic-slice_bitcast_fusion.gain_ref, bf16[16,512,256]{2,1,0:T(8,128)(2,1)} %bitcast.33, bf16[16,512,256]{2,1,0:T(8,128)(2,1)} %bitcast.38, ...), custom_call_target="tpu_custom_call" | custom-call | flops 2013265920 | bytes 12582912 | tf_op jit(solution)/shard_map/pallas_call | solution.py:111
  227.4 1.2 collective-permute-done.12.got_ref
  228.5 1.0 shard_map.117
  229.8 1.2 collective-permute-done.13.far_ref
  230.9 3.2 shard_map.118
  234.1 25.7 %all_to_all.43 = bf16[8,192,512]{2,1,0:T(8,128)(2,1)S(1)} all-to-all(bf16[8,192,512]{2,1,0:T(8,128)(2,1)S(1)} %shard_map.118), channel_id=1, replica_groups=mesh['y_lo'=2,'z'=8,'x'=4,'y_hi'=2,'core'=2] {'x','y_hi'}, dimensions={0} | all-to-all | bytes 3145728 | tf_op jit(solution)/shard_map/all_to_all | solution.py:210
  260.1 1.9 collective-permute-start.14
  262.0 10.5 %collective-permute-done.14 = bf16[192,512]{1,0:T(8,128)(2,1)S(1)} collective-permute-done((bf16[192,512]{1,0:T(8,128)(2,1)S(1)}, bf16[192,512]{1,0:T(8,128)(2,1)S(1)}, u32[]{:S(2)}, u32[]{:S(2)}) %collective-permute-start.14) | collective-permute-done | bytes 196640 | tf_op jit(solution)/shard_map/ppermute | solution.py:35
  272.7 23.0 %all_to_all.44.x_ref = bf16[8,192,512]{2,1,0:T(8,128)(2,1)S(1)} all-to-all(bf16[8,192,512]{2,1,0:T(8,128)(2,1)S(1)} %broadcast_in_dim.11), channel_id=1, replica_groups=mesh['y_lo'=2,'z'=8,'x'=4,'y_hi'=2,'core'=2] {'x','y_hi'}, dimensions={0} | all-to-all | bytes 3145728 | tf_op jit(solution)/shard_map/all_to_all | solution.py:204
  295.7 6.5 %shard_map.119 = (f32[192,640]{1,0:T(8,128)S(1)}, f32[192,640]{1,0:T(8,128)S(1)}) custom-call(s32[1]{0:T(128)} %bitcast.core_ref, bf16[8,192,512]{2,1,0:T(8,128)(2,1)S(1)} %all_to_all.44.x_ref, f32[8,1,512]{2,1,0:T(1,128)S(1)} %dynamic-slice_bitcast_fusion.gain_ref, bf16[16,512,256]{2,1,0:T(8,128)(2,1)} %bitcast.34, bf16[16,512,256]{2,1,0:T(8,128)(2,1)} %bitcast.39, ...), custom_call_target="tpu_custom_call" | custom-call | flops 2013265920 | bytes 12582912 | tf_op jit(solution)/shard_map/pallas_call | solution.py:111
  303.0 1.2 collective-permute-done.15.got_ref
  305.0 1.2 collective-permute-done.16.far_ref
  306.2 3.2 shard_map.121
  309.4 25.8 %all_to_all.45 = bf16[8,192,512]{2,1,0:T(8,128)(2,1)S(1)} all-to-all(bf16[8,192,512]{2,1,0:T(8,128)(2,1)S(1)} %shard_map.121), channel_id=1, replica_groups=mesh['y_lo'=2,'z'=8,'x'=4,'y_hi'=2,'core'=2] {'x','y_hi'}, dimensions={0} | all-to-all | bytes 3145728 | tf_op jit(solution)/shard_map/all_to_all | solution.py:210
  (65 shorter events, 6.6 us)
Async XLA Ops:
  0.0 2.2 copy-start
  2.2 2.2 copy-start.1
  4.4 2.2 copy-start.2
  6.6 3.9 %copy-start.9 = (bf16[192,512]{1,0:T(8,128)(2,1)S(1)}, bf16[192,512]{1,0:T(8,128)(2,1)}, u32[]{:S(2)}) copy-start(bf16[192,512]{1,0:T(8,128)(2,1)} %param.11) | copy-start | bytes 589828
  10.4 1.9 copy-start.8
  10.4 32.2 %collective-permute-start = (bf16[8,512,512]{2,1,0:T(8,128)(2,1)}, bf16[8,512,512]{2,1,0:T(8,128)(2,1)}, u32[]{:S(2)}, u32[]{:S(2)}) collective-permute-start(bf16[8,512,512]{2,1,0:T(8,128)(2,1)} %get-tuple-element.30), channel_id=1, source_target_pairs={{0,1},{1,0},{2,3},{3,2},{4,5},{5,4},{6,7},{7,6},{8,9},{9,8},{10,11... | collective-permute-start | bytes 12582920 | tf_op jit(solution)/shard_map/ppermute | solution.py:31
  11.9 6.5 %copy-start.13 = (bf16[1,8192,2]{1,2,0:T(2,128)(2,1)S(1)}, bf16[1,8192,2]{1,2,0:T(2,128)(2,1)}, u32[]{:S(2)}) copy-start(bf16[1,8192,2]{1,2,0:T(2,128)(2,1)} %param.18) | copy-start | bytes 98308
  11.9 7.7 %copy-start.14 = (f32[1,8192]{1,0:T(1,128)S(1)}, f32[1,8192]{1,0:T(1,128)}, u32[]{:S(2)}) copy-start(f32[1,8192]{1,0:T(1,128)} %param.15) | copy-start | bytes 98308
  12.3 30.3 %all-to-all-start = ((bf16[8,192,512]{2,1,0:T(8,128)(2,1)}), bf16[8,192,512]{2,1,0:T(8,128)(2,1)}, u32[]{:S(2)}, u32[]{:S(2)}) async-start(bf16[8,192,512]{2,1,0:T(8,128)(2,1)} %broadcast_in_dim.8), calls=%async_computation | async-start | bytes 3145728 | tf_op jit(solution)/shard_map/all_to_all | solution.py:204
  18.3 53.1 %collective-permute-start.7 = (bf16[256,4096]{1,0:T(8,128)(2,1)}, bf16[256,4096]{1,0:T(8,128)(2,1)S(1)}, u32[]{:S(2)}, u32[]{:S(2)}) collective-permute-start(bf16[256,4096]{1,0:T(8,128)(2,1)} %copy-done.8), channel_id=1, source_target_pairs={{0,1},{1,0},{2,3},{3,2},{4,5},{5,4},{6,7},{7,6},{8,9},{9,8},{10,11... | collective-permute-start | bytes 6291464 | tf_op jit(solution)/shard_map/ppermute | solution.py:31
  18.5 3.7 %collective-permute-start.1 = (bf16[8,2,512]{2,1,0:T(2,128)(2,1)S(1)}, bf16[8,2,512]{2,1,0:T(2,128)(2,1)S(1)}, u32[]{:S(2)}, u32[]{:S(2)}) collective-permute-start(bf16[8,2,512]{2,1,0:T(2,128)(2,1)S(1)} %bitcast.46), channel_id=1, source_target_pairs={{0,1},{1,0},{2,3},{3,2},{4,5},{5,4},{6,7},{7,6},{8,9},{9,8},{10,11... | collective-permute-start | bytes 49160 | tf_op jit(solution)/shard_map/ppermute | solution.py:31
  22.2 48.2 %copy-start.6 = (f32[1,2,128,128]{3,2,1,0:T(8,128)S(1)}, f32[1,2,128,128]{3,2,1,0:T(8,128)}, u32[]{:S(2)}) copy-start(f32[1,2,128,128]{3,2,1,0:T(8,128)} %param.20) | copy-start | bytes 393220
  22.2 48.2 %copy-start.7 = (f32[1,2,128]{2,1,0:T(2,128)S(1)}, f32[1,2,128]{2,1,0:T(2,128)}, u32[]{:S(2)}) copy-start(f32[1,2,128]{2,1,0:T(2,128)} %param.21) | copy-start | bytes 3076
  42.6 1.2 copy-start.3
  51.6 18.7 %collective-permute-start.2 = (f32[192,640]{1,0:T(8,128)S(1)}, f32[192,640]{1,0:T(8,128)S(1)}, u32[]{:S(2)}, u32[]{:S(2)}) collective-permute-start(f32[192,640]{1,0:T(8,128)S(1)} %get-tuple-element.32), channel_id=1, source_target_pairs={{0,1},{1,0},{2,3},{3,2},{4,5},{5,4},{6,7},{7,6},{8,9},{9,8},{10,11... | collective-permute-start | bytes 1474568 | tf_op jit(solution)/shard_map/ppermute | solution.py:31
  51.7 15.7 %collective-permute-start.3 = (s32[1]{0:T(128)}, s32[1]{0:T(128)}, u32[]{:S(2)}, u32[]{:S(2)}) collective-permute-start(s32[1]{0:T(128)} %param.12), channel_id=1, source_target_pairs={{0,16},{16,32},{32,48},{48,64},{64,80},{80,96},{96,112},{112,128},... | collective-permute-start | bytes 20 | tf_op jit(solution)/shard_map/ppermute | solution.py:35
  55.5 11.8 %collective-permute-start.4 = (s32[1]{0:T(128)}, s32[1]{0:T(128)}, u32[]{:S(2)}, u32[]{:S(2)}) collective-permute-start(s32[1]{0:T(128)} %param.12), channel_id=1, source_target_pairs={{0,32},{16,48},{32,64},{48,80},{64,96},{80,112},{96,128},{112,144}... | collective-permute-start | bytes 20 | tf_op jit(solution)/shard_map/ppermute | solution.py:35
  60.7 9.6 %collective-permute-start.5 = (s32[1]{0:T(128)}, s32[1]{0:T(128)}, u32[]{:S(2)}, u32[]{:S(2)}) collective-permute-start(s32[1]{0:T(128)} %param.12), channel_id=1, source_target_pairs={{0,48},{16,64},{32,80},{48,96},{64,112},{80,128},{96,144},{112,160... | collective-permute-start | bytes 20 | tf_op jit(solution)/shard_map/ppermute | solution.py:35
  71.3 1.4 collective-permute-start.6
  75.9 1.1 copy-start.5
  77.1 29.1 %all-to-all-start.1 = ((bf16[8,192,512]{2,1,0:T(8,128)(2,1)}), bf16[8,192,512]{2,1,0:T(8,128)(2,1)}, u32[]{:S(2)}, u32[]{:S(2)}) async-start(bf16[8,192,512]{2,1,0:T(8,128)(2,1)} %copy-done.5), calls=%async_computation.1 | async-start | bytes 3145728 | tf_op jit(solution)/shard_map/all_to_all | solution.py:210
  81.4 26.6 %copy-start.10 = (bf16[192,512]{1,0:T(8,128)(2,1)S(1)}, bf16[192,512]{1,0:T(8,128)(2,1)}, u32[]{:S(2)}) copy-start(bf16[192,512]{1,0:T(8,128)(2,1)} %param.11) | copy-start | bytes 589828
  106.2 6.8 %copy-start.12 = (bf16[384,512]{1,0:T(8,128)(2,1)S(1)}, bf16[384,512]{1,0:T(8,128)(2,1)}, u32[]{:S(2)}) copy-start(bf16[384,512]{1,0:T(8,128)(2,1)} %param.13) | copy-start | bytes 1179652
  106.2 12.0 %copy-start.11 = (bf16[64,512]{1,0:T(8,128)(2,1)S(1)}, bf16[64,512]{1,0:T(8,128)(2,1)}, u32[]{:S(2)}) copy-start(bf16[64,512]{1,0:T(8,128)(2,1)} %param.14) | copy-start | bytes 196612
  108.0 10.3 %collective-permute-start.8 = (bf16[192,512]{1,0:T(8,128)(2,1)S(1)}, bf16[192,512]{1,0:T(8,128)(2,1)S(1)}, u32[]{:S(2)}, u32[]{:S(2)}) collective-permute-start(bf16[192,512]{1,0:T(8,128)(2,1)S(1)} %add_convert_fusion.3), channel_id=1, source_target_pairs={{0,16},{16,32},{32,48},{48,64},{64,80},{80,96},{96,112},{112,128},... | collective-permute-start | bytes 589832 | tf_op jit(solution)/shard_map/ppermute | solution.py:35
  118.4 24.9 %copy-start.4 = (bf16[8,128,512]{2,1,0:T(8,128)(2,1)S(1)}, bf16[8,128,512]{2,1,0:T(8,128)(2,1)}, u32[]{:S(2)}) copy-start(bf16[8,128,512]{2,1,0:T(8,128)(2,1)} %pad.8.theirs_ref) | copy-start | bytes 3145732
  150.7 1.9 collective-permute-start.9
  153.6 1.6 collective-permute-start.10
  184.4 10.8 %collective-permute-start.11 = (bf16[192,512]{1,0:T(8,128)(2,1)S(1)}, bf16[192,512]{1,0:T(8,128)(2,1)S(1)}, u32[]{:S(2)}, u32[]{:S(2)}) collective-permute-start(bf16[192,512]{1,0:T(8,128)(2,1)S(1)} %add_convert_fusion.2), channel_id=1, source_target_pairs={{0,16},{16,32},{32,48},{48,64},{64,80},{80,96},{96,112},{112,128},... | collective-permute-start | bytes 589832 | tf_op jit(solution)/shard_map/ppermute | solution.py:35
  226.6 1.9 collective-permute-start.12
  229.5 1.4 collective-permute-start.13
  260.1 12.4 %collective-permute-start.14 = (bf16[192,512]{1,0:T(8,128)(2,1)S(1)}, bf16[192,512]{1,0:T(8,128)(2,1)S(1)}, u32[]{:S(2)}, u32[]{:S(2)}) collective-permute-start(bf16[192,512]{1,0:T(8,128)(2,1)S(1)} %add_convert_fusion.1), channel_id=1, source_target_pairs={{0,16},{16,32},{32,48},{48,64},{64,80},{80,96},{96,112},{112,128},... | collective-permute-start | bytes 589832 | tf_op jit(solution)/shard_map/ppermute | solution.py:35
  302.2 1.9 collective-permute-start.15
  304.9 1.3 collective-permute-start.16

commit v2 on v1

v2 whole, which is shorter than its diff:
```python
import functools

import jax
import jax.numpy as jnp
from jax import lax
from jax.experimental import pallas as pl
from jax.experimental.pallas import tpu as pltpu
from jax.sharding import Mesh
from jax.sharding import PartitionSpec as P

SEG = 128
PIECE = 192
MEM = 64
EPS = 1e-05
AXES = ("y_lo", "z", "x", "y_hi", "core")
SECTION = ("y_lo", "z")
TENSOR = ("x", "y_hi", "core")
CHIPS = ("x", "y_hi")
N_CHIPS = 8
FLAG_ROWS = 16
PARTS = 4
BLOCK = 512
HEADS = 2
HD = 128
WIDE = HEADS * HD
SIDE = 128
HALF = 2 * WIDE + SIDE
HIDDEN = 8192
VMEM_LIMIT = 14 * 2**20
HIGHEST = lax.Precision.HIGHEST


VMEM = pl.BlockSpec(memory_space=pltpu.VMEM)
SMEM = pl.BlockSpec(memory_space=pltpu.SMEM)


def swap(value, axis):
    return lax.ppermute(value, axis, [(0, 1), (1, 0)])


def next_section(value):
    return lax.ppermute(value, SECTION, [(i, i + 1) for i in range(15)])


def pick_kernel(core_ref, k_ref, v_ref, f_ref, w_keep, w_sent, f_keep, f_sent):
    core = core_ref[0]
    w_keep[0, :, :WIDE] = k_ref[core]
    w_keep[0, :, WIDE:] = v_ref[core]
    w_sent[0, :, :WIDE] = k_ref[1 - core]
    w_sent[0, :, WIDE:] = v_ref[1 - core]
    f_keep[0] = f_ref[:, pl.ds(pl.multiple_of(core * BLOCK, BLOCK), BLOCK)]
    f_sent[0] = f_ref[:, pl.ds(pl.multiple_of((1 - core) * BLOCK, BLOCK), BLOCK)]


def pick(core, wk, wv, f, part):
    count = N_CHIPS // PARTS
    pair = pl.BlockSpec((2, BLOCK, WIDE), lambda b: (part * count + b, 0, 0))
    w_block = pl.BlockSpec((1, BLOCK, 2 * WIDE), lambda b: (b, 0, 0))
    f_block = pl.BlockSpec((1, WIDE, BLOCK), lambda b: (b, 0, 0))
    w_shape = jax.ShapeDtypeStruct((count, BLOCK, 2 * WIDE), jnp.bfloat16)
    f_shape = jax.ShapeDtypeStruct((count, WIDE, BLOCK), jnp.bfloat16)
    return pl.pallas_call(
        pick_kernel,
        grid=(count,),
        in_specs=[SMEM, pair, pair, pl.BlockSpec((WIDE, 2 * BLOCK), lambda b: (0, part * count + b))],
        out_specs=[w_block, w_block, f_block, f_block],
        out_shape=[w_shape, w_shape, f_shape, f_shape],
        compiler_params=pltpu.CompilerParams(vmem_limit_bytes=VMEM_LIMIT),
        cost_estimate=pl.CostEstimate(flops=0, bytes_accessed=0, transcendentals=0),
    )(core, wk, wv, f)


def project_kernel(write, x_ref, gain_ref, gate_ref, *refs):
    keep_refs, got_refs, (mine_out, other_out) = refs[:PARTS], refs[PARTS : 2 * PARTS], refs[-2:]
    rows = x_ref.shape[1]
    dot = functools.partial(jnp.dot, preferred_element_type=jnp.float32)
    squares, gate, mine, other = 0.0, 0.0, 0.0, 0.0
    for b in range(N_CHIPS):
        part, at = divmod(b, N_CHIPS // PARTS)
        wide = x_ref[b].astype(jnp.float32)
        squares += wide * wide
        scaled = (wide * gain_ref[b]).astype(jnp.bfloat16)
        mine += dot(scaled, keep_refs[part][at])
        other += dot(scaled, got_refs[part][at])
        if write:
            gate += dot(scaled[rows - MEM :], gate_ref[b])
    squares = jnp.sum(squares, axis=1, keepdims=True)
    lane = lax.broadcasted_iota(jnp.int32, (rows, SIDE), 1)
    side = jnp.where(lane == 2 * HEADS, squares, 0.0)
    mine_out[:, : 2 * WIDE] = mine
    other_out[:, : 2 * WIDE] = other
    mine_out[:, 2 * WIDE :] = side
    other_out[:, 2 * WIDE :] = side
    if write:
        mine_out[rows - MEM :, 2 * WIDE :] = side[rows - MEM :] + gate
        other_out[rows - MEM :, 2 * WIDE :] = side[rows - MEM :] + gate


def project(x, gain, gate, keep, got, write):
    rows = x.shape[1]
    out = jax.ShapeDtypeStruct((rows, HALF), jnp.float32)
    return pl.pallas_call(
        functools.partial(project_kernel, write),
        in_specs=[VMEM] * (3 + 2 * PARTS),
        out_specs=[VMEM] * 2,
        out_shape=[out, out],
        compiler_params=pltpu.CompilerParams(vmem_limit_bytes=VMEM_LIMIT),
        cost_estimate=pl.CostEstimate(
            flops=2 * rows * 4096 * 1024, bytes_accessed=0, transcendentals=0
        ),
    )(x, gain, gate, *keep, *got)


def memory_kernel(write, mine_ref, got_ref, keep_ref, a_ref, z_ref, read_ref, *state):
    both = mine_ref[:, : 2 * WIDE] + got_ref[:, : 2 * WIDE]
    rows = both.shape[0]
    side, got_side = mine_ref[:, 2 * WIDE :], got_ref[:, 2 * WIDE :]
    total = side[:, 2 * HEADS : 2 * HEADS + 1] + got_side[:, 2 * HEADS : 2 * HEADS + 1]
    scale = lax.rsqrt(total * (1.0 / HIDDEN) + EPS)
    keep = keep_ref[0, 0]
    for h in range(HEADS):
        a = a_ref[h] * keep
        z = z_ref[h : h + 1] * keep
        k = both[:, h * HD : (h + 1) * HD] * scale
        k = jnp.where(k > 0, k + 1.0, jnp.exp(jnp.minimum(k, 0.0)))
        v = both[:, WIDE + h * HD : WIDE + (h + 1) * HD] * scale
        top = jnp.dot(k, a, precision=HIGHEST, preferred_element_type=jnp.float32)
        bottom = jnp.sum(k * z, axis=1, keepdims=True) + 1.0
        read = top / bottom
        read_ref[:, h * HD : (h + 1) * HD] = read.astype(jnp.bfloat16)
        if write:
            logit = side[rows - MEM :, h : h + 1] + got_side[rows - MEM :, HEADS + h : HEADS + h + 1]
            logit = logit * scale[rows - MEM :]
            gate = 1.0 / (1.0 + jnp.exp(-logit))
            change = (v[rows - MEM :] - read[rows - MEM :]) * gate
            tail = k[rows - MEM :]
            state[0][h] = a + lax.dot_general(
                tail,
                change,
                (((0,), (0,)), ((), ())),
                precision=HIGHEST,
                preferred_element_type=jnp.float32,
            )
            state[1][h : h + 1] = z + jnp.sum(tail, axis=0, keepdims=True)


def memory(mine, got, keep, a, z, write):
    rows = mine.shape[0]
    shapes = [jax.ShapeDtypeStruct((rows, WIDE), jnp.bfloat16)]
    if write:
        shapes += [jax.ShapeDtypeStruct(a.shape, a.dtype), jax.ShapeDtypeStruct(z.shape, z.dtype)]
    return pl.pallas_call(
        functools.partial(memory_kernel, write),
        in_specs=[VMEM, VMEM, SMEM, VMEM, VMEM],
        out_specs=[VMEM] * len(shapes),
        out_shape=shapes,
        compiler_params=pltpu.CompilerParams(vmem_limit_bytes=16 * 2**20),
        cost_estimate=pl.CostEstimate(
            flops=2 * rows * WIDE * HD * 6, bytes_accessed=rows * HALF * 8, transcendentals=0
        ),
    )(mine, got, keep, a, z)


def output_kernel(near_ref, far_ref, *refs):
    keep_refs, got_refs, p_ref = refs[:PARTS], refs[PARTS : 2 * PARTS], refs[-1]
    near, far = near_ref[...], far_ref[...]
    for b in range(N_CHIPS):
        i, at = divmod(b, N_CHIPS // PARTS)
        part = jnp.dot(near, keep_refs[i][at], preferred_element_type=jnp.float32)
        part += jnp.dot(far, got_refs[i][at], preferred_element_type=jnp.float32)
        p_ref[b] = part.astype(jnp.bfloat16)


def output(near, far, keep, got):
    rows = near.shape[0]
    return pl.pallas_call(
        output_kernel,
        in_specs=[VMEM] * (2 + 2 * PARTS),
        out_specs=VMEM,
        out_shape=jax.ShapeDtypeStruct((N_CHIPS, rows, BLOCK), jnp.bfloat16),
        compiler_params=pltpu.CompilerParams(vmem_limit_bytes=VMEM_LIMIT),
        cost_estimate=pl.CostEstimate(
            flops=2 * rows * 2 * WIDE * 4096, bytes_accessed=0, transcendentals=0
        ),
    )(near, far, *keep, *got)


def copies(x):
    return jnp.broadcast_to(x[None], (N_CHIPS,) + x.shape)


def exchange(blocks):
    return lax.all_to_all(blocks, CHIPS, 0, 0, tiled=True)


def local(
    initial_stack_inputs,
    initial_sequence_starts,
    arriving_pieces,
    recall_embeddings,
    rescaling_factors,
    lookup_projection,
    content_projection,
    write_gate_projection,
    final_projection,
    associative_stores,
    denominator_vectors,
):
    core = lax.axis_index("core")
    which = core.astype(jnp.int32).reshape(1)
    section_zero = (lax.axis_index("y_lo") == 0) & (lax.axis_index("z") == 0)
    steps = arriving_pieces.shape[0] // SEG + 1

    x = initial_stack_inputs
    outgoing, which = lax.optimization_barrier((copies(x), which))
    flag = (initial_sequence_starts[0] > 0).astype(jnp.bfloat16)

    wk = lookup_projection[0].reshape(2 * N_CHIPS, BLOCK, WIDE)
    wv = content_projection[0].reshape(2 * N_CHIPS, BLOCK, WIDE)
    picked = [pick(which, wk, wv, final_projection[0], part) for part in range(PARTS)]
    w_keep, w_sent, f_keep, f_sent = zip(*picked)
    w_got = [swap(w, "core") for w in w_sent]
    f_got = [swap(f, "core") for f in f_sent]
    gain = lax.dynamic_index_in_dim(
        rescaling_factors.reshape(N_CHIPS, 2, 1, BLOCK), core, 1, keepdims=False
    )
    gates = write_gate_projection[0].T.reshape(HEADS, N_CHIPS, 2, BLOCK)
    gate = lax.dynamic_index_in_dim(gates, core, 2, keepdims=False)
    theirs = swap(lax.dynamic_index_in_dim(gates, 1 - core, 2, keepdims=False), "core")
    gate = jnp.concatenate([gate, theirs], axis=0).transpose(1, 2, 0)
    gate = jnp.pad(gate, ((0, 0), (0, 0), (0, SIDE - 2 * HEADS)))

    a = associative_stores[0]
    z = denominator_vectors[0]
    for t in range(steps):
        write = t + 1 < steps
        if t > 0:
            sent = jnp.concatenate([x, jnp.broadcast_to(flag, (FLAG_ROWS, BLOCK))], axis=0)
            moved = next_section(sent)
            entering = jnp.concatenate(
                [arriving_pieces[(t - 1) * SEG : t * SEG], recall_embeddings], axis=0
            )
            x = jnp.where(section_zero, entering, moved[:PIECE])
            flag = jnp.where(section_zero, jnp.zeros((), jnp.bfloat16), moved[PIECE, 0])
            outgoing = copies(x)
        keep = (1.0 - flag.astype(jnp.float32)).reshape(1, 1)
        mine, other = project(exchange(outgoing), gain, gate, w_keep, w_got, write)
        read, *state = memory(mine, swap(other, "core"), keep, a, z, write)
        if write:
            a, z = state
        p = exchange(output(read, swap(read, "core"), f_keep, f_got))
        total = jnp.sum(p.astype(jnp.float32), axis=0)
        x = (x.astype(jnp.float32) + total).astype(jnp.bfloat16)
    return x


def solution(mesh):
    fine = Mesh(mesh.devices.reshape(2, 8, 4, 2, 2), AXES)
    return jax.shard_map(
        local,
        mesh=fine,
        in_specs=(
            P(SECTION, TENSOR),
            P(SECTION),
            P(None, TENSOR),
            P(None, TENSOR),
            P(SECTION, None),
            P(SECTION, None, TENSOR),
            P(SECTION, None, TENSOR),
            P(SECTION, None, TENSOR),
            P(SECTION, TENSOR, None),
            P(SECTION, TENSOR, None, None),
            P(SECTION, TENSOR, None),
        ),
        out_specs=P(SECTION, TENSOR),
        check_vma=False,
    )
```

time: 337 us -> 339 us (level)
  local copies, waits for them, and re-layouts: 13.1 us -> 52.2 us
  waiting for transfers between devices: 80.7 us -> 59.5 us
  starting transfers between devices: 37 us -> 24.7 us
  Pallas kernels: 49.3 us -> 42.1 us
    unnamed x33 -> x135, local copies, waits for them, and re-layouts: 9.93 us -> 44.2 us
    all_to_all x2, waiting for transfers between devices: 44.1 us -> 24.6 us  [exchange(): return lax.all_to_all(blocks, CHIPS, 0, 0, tiled=True)]
    ppermute x6 -> x3, starting transfers between devices: 24.9 us -> 7.84 us  [next_section(): return lax.ppermute(value, SECTION, [(i, i + 1) for i in range(15)])]
    pallas_call x13 -> x16, Pallas kernels: 49.3 us -> 42.1 us  [the longest x4 20 us: project(): pl.pallas_call(functools.partial(project_kernel, write), in_specs=[VMEM]...]
    ppermute x11 -> x17, waiting for transfers between devices: 10.1 us -> 8.33 us  [swap(): return lax.ppermute(value, axis, [(0, 1), (1, 0)])]
    ppermute x6 -> x3, waiting for transfers between devices: 26.5 us -> 26.5 us  [next_section(): return lax.ppermute(value, SECTION, [(i, i + 1) for i in range(15)])]
  transfers between devices with their start and end apart: 19 -> 22, of which waited for: 14 -> 13; matrix products, arithmetic and copies ran while one was open for 1% -> 2% of each run, Pallas kernels for 3% -> 2%
where the time goes in v2:
time: 339 us; the launch traced here: 337 us
  blocking collectives  152 us (45%)
  waiting for transfers between devices  59.5 us (18%)
  local copies, waits for them, and re-layouts  52.2 us (15%)
  Pallas kernels  42.1 us (12%)
  starting transfers between devices  24.7 us (7%)
  other arithmetic  4.11 us (1%)
    all_to_all x6, blocking collectives, exchange(): return lax.all_to_all(blocks, CHIPS, 0, 0, tiled=True)  152 us
    unnamed x135, local copies, waits for them, and re-layouts  44.2 us
    ppermute x3, waiting for transfers between devices, next_section(): return lax.ppermute(value, SECTION, [(i, i + 1) for i in range(15)])  26.5 us
    all_to_all x2, waiting for transfers between devices, exchange(): return lax.all_to_all(blocks, CHIPS, 0, 0, tiled=True)  24.6 us
    pallas_call x4, Pallas kernels, project(): pl.pallas_call(functools.partial(project_kernel, write), in_specs=[VMEM]...  20 us
    all_to_all x2, starting transfers between devices, exchange(): return lax.all_to_all(blocks, CHIPS, 0, 0, tiled=True)  13.3 us
    pallas_call x4, Pallas kernels, output(): pl.pallas_call(output_kernel, in_specs=[VMEM] * (2 + 2 * PARTS), out_spec...  9.99 us
    ppermute x17, waiting for transfers between devices, swap(): return lax.ppermute(value, axis, [(0, 1), (1, 0)])  8.33 us
  transfers between devices with their start and end apart: 22, of which 13 were waited for; matrix products, arithmetic and copies ran while one was open for 2% of the time, Pallas kernels for 2%

profile of v2, /device:TPU:8, one launch (start us, length us, event | category | flops | bytes accessed | tf_op | source)
XLA Modules:
  0.0 337.3 jit_solution(8792845232472222282)
XLA Ops:
  0.0 2.2 broadcast_in_dim.8
  2.2 6.0 %all-to-all-start = ((bf16[8,192,512]{2,1,0:T(8,128)(2,1)}), bf16[8,192,512]{2,1,0:T(8,128)(2,1)}, u32[]{:S(2)}, u32[]{:S(2)}) async-start(bf16[8,192,512]{2,1,0:T(8,128)(2,1)} %broadcast_in_dim.8), calls=%async_computation | async-start | bytes 3145728 | tf_op jit(solution)/shard_map/all_to_all | solution.py:193
  8.2 2.2 copy-done
  10.4 2.2 copy-done.1
  12.6 2.2 copy-done.2
  14.8 1.4 shard_map.112
  17.0 1.4 shard_map.111
  20.6 1.4 shard_map.110
  22.1 1.1 copy-done.8
  23.9 1.4 shard_map.109
  29.9 1.4 copy.18
  31.3 1.5 pad.7.gate_ref
  32.9 1.2 copy-done.4
  34.1 1.2 copy-done.9
  35.3 1.2 copy-done.14
  36.5 5.5 %shard_map.113 = (f32[192,640]{1,0:T(8,128)S(1)}, f32[192,640]{1,0:T(8,128)}) custom-call(bf16[8,192,512]{2,1,0:T(8,128)(2,1)} %all-to-all-done.x_ref, f32[8,1,512]{2,1,0:T(1,128)S(1)} %dynamic-slice_bitcast_fusion.gain_ref, bf16[8,512,128]{2,1,0:T(8,128)(2,1)S(1)} %pad.7.gate_ref, bf16[2,512,512]{2,1,0:T(8,128)(2,1)S(1)} %copy-done.14, ...), custom_call_target="tpu_custom_call" | custom-call | flops 1610612736 | tf_op jit(solution)/shard_map/pallas_call | solution.py:102
  46.0 2.0 shard_map.114
  49.5 1.0 copy-done.19
  53.7 2.5 shard_map.115
  56.2 1.1 copy-done.38
  57.3 7.2 %all-to-all-start.1 = ((bf16[8,192,512]{2,1,0:T(8,128)(2,1)}), bf16[8,192,512]{2,1,0:T(8,128)(2,1)}, u32[]{:S(2)}, u32[]{:S(2)}) async-start(bf16[8,192,512]{2,1,0:T(8,128)(2,1)} %copy-done.38), calls=%async_computation.1 | async-start | bytes 3145728 | tf_op jit(solution)/shard_map/all_to_all | solution.py:193
  64.6 24.6 %all-to-all-done.1 = bf16[8,192,512]{2,1,0:T(8,128)(2,1)} async-done(((bf16[8,192,512]{2,1,0:T(8,128)(2,1)}), bf16[8,192,512]{2,1,0:T(8,128)(2,1)}, u32[]{:S(2)}, u32[]{:S(2)}) %all-to-all-start.1) | async-done | bytes 1572896 | tf_op jit(solution)/shard_map/all_to_all | solution.py:193
  89.2 1.7 convert_reduce_fusion.3
  91.0 4.0 %collective-permute-start.11 = (bf16[208,512]{1,0:T(8,128)(2,1)S(1)}, bf16[208,512]{1,0:T(8,128)(2,1)S(1)}, u32[]{:S(2)}, u32[]{:S(2)}) collective-permute-start(bf16[208,512]{1,0:T(8,128)(2,1)S(1)} %concatenate.25), channel_id=1, source_target_pairs={{0,16},{16,32},{32,48},{48,64},{64,80},{80,96},{96,112},{112,128},... | collective-permute-start | bytes 638984 | tf_op jit(solution)/shard_map/ppermute | solution.py:42
  95.8 8.4 %collective-permute-done.11 = bf16[208,512]{1,0:T(8,128)(2,1)S(1)} collective-permute-done((bf16[208,512]{1,0:T(8,128)(2,1)S(1)}, bf16[208,512]{1,0:T(8,128)(2,1)S(1)}, u32[]{:S(2)}, u32[]{:S(2)}) %collective-permute-start.11) | collective-permute-done | bytes 213024 | tf_op jit(solution)/shard_map/ppermute | solution.py:42
  105.1 25.6 %all_to_all.40.x_ref = bf16[8,192,512]{2,1,0:T(8,128)(2,1)S(1)} all-to-all(bf16[8,192,512]{2,1,0:T(8,128)(2,1)S(1)} %broadcast_in_dim.9), channel_id=1, replica_groups=mesh['y_lo'=2,'z'=8,'x'=4,'y_hi'=2,'core'=2] {'x','y_hi'}, dimensions={0} | all-to-all | bytes 3145728 | tf_op jit(solution)/shard_map/all_to_all | solution.py:193
  130.7 5.0 %shard_map.116 = (f32[192,640]{1,0:T(8,128)S(1)}, f32[192,640]{1,0:T(8,128)}) custom-call(bf16[8,192,512]{2,1,0:T(8,128)(2,1)S(1)} %all_to_all.40.x_ref, f32[8,1,512]{2,1,0:T(1,128)S(1)} %dynamic-slice_bitcast_fusion.gain_ref, bf16[8,512,128]{2,1,0:T(8,128)(2,1)S(1)} %pad.7.gate_ref, bf16[2,512,512]{2,1,0:T(8,128)(2,1)S(1)} %copy-done.15, ...), custom_call_target="tpu_custom_call" | custom-call | flops 1610612736 | tf_op jit(solution)/shard_map/pallas_call | solution.py:102
  137.6 1.1 collective-permute-done.12.got_ref
  139.7 2.0 shard_map.117
  142.0 1.2 collective-permute-done.13.far_ref
  147.4 2.5 shard_map.118
  149.9 25.7 %all_to_all.41 = bf16[8,192,512]{2,1,0:T(8,128)(2,1)S(1)} all-to-all(bf16[8,192,512]{2,1,0:T(8,128)(2,1)S(1)} %shard_map.118), channel_id=1, replica_groups=mesh['y_lo'=2,'z'=8,'x'=4,'y_hi'=2,'core'=2] {'x','y_hi'}, dimensions={0} | all-to-all | bytes 3145728 | tf_op jit(solution)/shard_map/all_to_all | solution.py:193
  176.6 1.9 collective-permute-start.14
  178.5 8.4 %collective-permute-done.14 = bf16[208,512]{1,0:T(8,128)(2,1)S(1)} collective-permute-done((bf16[208,512]{1,0:T(8,128)(2,1)S(1)}, bf16[208,512]{1,0:T(8,128)(2,1)S(1)}, u32[]{:S(2)}, u32[]{:S(2)}) %collective-permute-start.14) | collective-permute-done | bytes 213024 | tf_op jit(solution)/shard_map/ppermute | solution.py:42
  187.8 25.1 %all_to_all.42.x_ref = bf16[8,192,512]{2,1,0:T(8,128)(2,1)S(1)} all-to-all(bf16[8,192,512]{2,1,0:T(8,128)(2,1)S(1)} %broadcast_in_dim.10), channel_id=1, replica_groups=mesh['y_lo'=2,'z'=8,'x'=4,'y_hi'=2,'core'=2] {'x','y_hi'}, dimensions={0} | all-to-all | bytes 3145728 | tf_op jit(solution)/shard_map/all_to_all | solution.py:193
  212.8 5.0 %shard_map.119 = (f32[192,640]{1,0:T(8,128)S(1)}, f32[192,640]{1,0:T(8,128)}) custom-call(bf16[8,192,512]{2,1,0:T(8,128)(2,1)S(1)} %all_to_all.42.x_ref, f32[8,1,512]{2,1,0:T(1,128)S(1)} %dynamic-slice_bitcast_fusion.gain_ref, bf16[8,512,128]{2,1,0:T(8,128)(2,1)S(1)} %pad.7.gate_ref, bf16[2,512,512]{2,1,0:T(8,128)(2,1)S(1)} %copy-done.16, ...), custom_call_target="tpu_custom_call" | custom-call | flops 1610612736 | tf_op jit(solution)/shard_map/pallas_call | solution.py:102
  221.9 2.0 shard_map.120
  224.1 1.2 collective-permute-done.16.far_ref
  229.5 2.5 shard_map.121
  232.0 25.7 %all_to_all.43 = bf16[8,192,512]{2,1,0:T(8,128)(2,1)S(1)} all-to-all(bf16[8,192,512]{2,1,0:T(8,128)(2,1)S(1)} %shard_map.121), channel_id=1, replica_groups=mesh['y_lo'=2,'z'=8,'x'=4,'y_hi'=2,'core'=2] {'x','y_hi'}, dimensions={0} | all-to-all | bytes 3145728 | tf_op jit(solution)/shard_map/all_to_all | solution.py:193
  258.7 1.9 collective-permute-start.17
  260.6 9.7 %collective-permute-done.17 = bf16[208,512]{1,0:T(8,128)(2,1)S(1)} collective-permute-done((bf16[208,512]{1,0:T(8,128)(2,1)S(1)}, bf16[208,512]{1,0:T(8,128)(2,1)S(1)}, u32[]{:S(2)}, u32[]{:S(2)}) %collective-permute-start.17) | collective-permute-done | bytes 213024 | tf_op jit(solution)/shard_map/ppermute | solution.py:42
  271.2 23.8 %all_to_all.44.x_ref = bf16[8,192,512]{2,1,0:T(8,128)(2,1)S(1)} all-to-all(bf16[8,192,512]{2,1,0:T(8,128)(2,1)S(1)} %broadcast_in_dim.11), channel_id=1, replica_groups=mesh['y_lo'=2,'z'=8,'x'=4,'y_hi'=2,'core'=2] {'x','y_hi'}, dimensions={0} | all-to-all | bytes 3145728 | tf_op jit(solution)/shard_map/all_to_all | solution.py:193
  295.1 4.5 %shard_map.122 = (f32[192,640]{1,0:T(8,128)S(1)}, f32[192,640]{1,0:T(8,128)}) custom-call(bf16[8,192,512]{2,1,0:T(8,128)(2,1)S(1)} %all_to_all.44.x_ref, f32[8,1,512]{2,1,0:T(1,128)S(1)} %dynamic-slice_bitcast_fusion.gain_ref, bf16[8,512,128]{2,1,0:T(8,128)(2,1)S(1)} %pad.7.gate_ref, bf16[2,512,512]{2,1,0:T(8,128)(2,1)S(1)} %copy-done.17, ...), custom_call_target="tpu_custom_call" | custom-call | flops 1610612736 | tf_op jit(solution)/shard_map/pallas_call | solution.py:102
  304.2 1.2 collective-permute-done.19.far_ref
  305.4 1.0 copy-done.32
  307.5 2.5 shard_map.124
  310.0 25.7 %all_to_all.45 = bf16[8,192,512]{2,1,0:T(8,128)(2,1)S(1)} all-to-all(bf16[8,192,512]{2,1,0:T(8,128)(2,1)S(1)} %shard_map.124), channel_id=1, replica_groups=mesh['y_lo'=2,'z'=8,'x'=4,'y_hi'=2,'core'=2] {'x','y_hi'}, dimensions={0} | all-to-all | bytes 3145728 | tf_op jit(solution)/shard_map/all_to_all | solution.py:193
  (183 shorter events, 42.8 us)
Async XLA Ops:
  2.2 30.6 %all-to-all-start = ((bf16[8,192,512]{2,1,0:T(8,128)(2,1)}), bf16[8,192,512]{2,1,0:T(8,128)(2,1)}, u32[]{:S(2)}, u32[]{:S(2)}) async-start(bf16[8,192,512]{2,1,0:T(8,128)(2,1)} %broadcast_in_dim.8), calls=%async_computation | async-start | bytes 3145728 | tf_op jit(solution)/shard_map/all_to_all | solution.py:193
  8.2 2.2 copy-start
  10.4 2.2 copy-start.1
  12.6 2.2 copy-start.2
  17.0 15.8 %collective-permute-start.4 = (bf16[2,512,512]{2,1,0:T(8,128)(2,1)}, bf16[2,512,512]{2,1,0:T(8,128)(2,1)S(1)}, u32[]{:S(2)}, u32[]{:S(2)}) collective-permute-start(bf16[2,512,512]{2,1,0:T(8,128)(2,1)} %get-tuple-element.49), channel_id=1, source_target_pairs={{0,1},{1,0},{2,3},{3,2},{4,5},{5,4},{6,7},{7,6},{8,9},{9,8},{10,11... | collective-permute-start | bytes 3145736 | tf_op jit(solution)/shard_map/ppermute | solution.py:38
  20.1 12.7 %collective-permute-start.3 = (bf16[2,512,512]{2,1,0:T(8,128)(2,1)}, bf16[2,512,512]{2,1,0:T(8,128)(2,1)}, u32[]{:S(2)}, u32[]{:S(2)}) collective-permute-start(bf16[2,512,512]{2,1,0:T(8,128)(2,1)} %get-tuple-element.48), channel_id=1, source_target_pairs={{0,1},{1,0},{2,3},{3,2},{4,5},{5,4},{6,7},{7,6},{8,9},{9,8},{10,11... | collective-permute-start | bytes 3145736 | tf_op jit(solution)/shard_map/ppermute | solution.py:38
  23.9 3.7 %copy-start.64 = (bf16[1,8192,2]{1,2,0:T(2,128)(2,1)S(1)}, bf16[1,8192,2]{1,2,0:T(2,128)(2,1)}, u32[]{:S(2)}) copy-start(bf16[1,8192,2]{1,2,0:T(2,128)(2,1)} %param.18) | copy-start | bytes 98308
  23.9 4.4 %copy-start.65 = (f32[1,8192]{1,0:T(1,128)S(1)}, f32[1,8192]{1,0:T(1,128)}, u32[]{:S(2)}) copy-start(f32[1,8192]{1,0:T(1,128)} %param.15) | copy-start | bytes 98308
  23.9 8.9 %collective-permute-start.2 = (bf16[2,512,512]{2,1,0:T(8,128)(2,1)}, bf16[2,512,512]{2,1,0:T(8,128)(2,1)}, u32[]{:S(2)}, u32[]{:S(2)}) collective-permute-start(bf16[2,512,512]{2,1,0:T(8,128)(2,1)} %get-tuple-element.47), channel_id=1, source_target_pairs={{0,1},{1,0},{2,3},{3,2},{4,5},{5,4},{6,7},{7,6},{8,9},{9,8},{10,11... | collective-permute-start | bytes 3145736 | tf_op jit(solution)/shard_map/ppermute | solution.py:38
  27.1 5.7 %collective-permute-start.1 = (bf16[2,512,512]{2,1,0:T(8,128)(2,1)}, bf16[2,512,512]{2,1,0:T(8,128)(2,1)}, u32[]{:S(2)}, u32[]{:S(2)}) collective-permute-start(bf16[2,512,512]{2,1,0:T(8,128)(2,1)} %get-tuple-element.46), channel_id=1, source_target_pairs={{0,1},{1,0},{2,3},{3,2},{4,5},{5,4},{6,7},{7,6},{8,9},{9,8},{10,11... | collective-permute-start | bytes 3145736 | tf_op jit(solution)/shard_map/ppermute | solution.py:38
  27.7 2.2 collective-permute-start
  36.5 8.5 %copy-start.47 = (f32[1,2,128,128]{3,2,1,0:T(8,128)S(1)}, f32[1,2,128,128]{3,2,1,0:T(8,128)}, u32[]{:S(2)}) copy-start(f32[1,2,128,128]{3,2,1,0:T(8,128)} %param.20) | copy-start | bytes 393220
  36.5 8.5 %copy-start.48 = (f32[1,2,128]{2,1,0:T(2,128)S(1)}, f32[1,2,128]{2,1,0:T(2,128)}, u32[]{:S(2)}) copy-start(f32[1,2,128]{2,1,0:T(2,128)} %param.21) | copy-start | bytes 3076
  42.8 2.2 collective-permute-start.5
  43.2 5.4 %collective-permute-start.10 = (bf16[2,256,512]{2,1,0:T(8,128)(2,1)}, bf16[2,256,512]{2,1,0:T(8,128)(2,1)}, u32[]{:S(2)}, u32[]{:S(2)}) collective-permute-start(bf16[2,256,512]{2,1,0:T(8,128)(2,1)} %get-tuple-element.60), channel_id=1, source_target_pairs={{0,1},{1,0},{2,3},{3,2},{4,5},{5,4},{6,7},{7,6},{8,9},{9,8},{10,11... | collective-permute-start | bytes 1572872 | tf_op jit(solution)/shard_map/ppermute | solution.py:38
  43.3 5.2 %collective-permute-start.9 = (bf16[2,256,512]{2,1,0:T(8,128)(2,1)}, bf16[2,256,512]{2,1,0:T(8,128)(2,1)}, u32[]{:S(2)}, u32[]{:S(2)}) collective-permute-start(bf16[2,256,512]{2,1,0:T(8,128)(2,1)} %get-tuple-element.59), channel_id=1, source_target_pairs={{0,1},{1,0},{2,3},{3,2},{4,5},{5,4},{6,7},{7,6},{8,9},{9,8},{10,11... | collective-permute-start | bytes 1572872 | tf_op jit(solution)/shard_map/ppermute | solution.py:38
  43.7 4.9 %collective-permute-start.8 = (bf16[2,256,512]{2,1,0:T(8,128)(2,1)}, bf16[2,256,512]{2,1,0:T(8,128)(2,1)}, u32[]{:S(2)}, u32[]{:S(2)}) collective-permute-start(bf16[2,256,512]{2,1,0:T(8,128)(2,1)} %get-tuple-element.58), channel_id=1, source_target_pairs={{0,1},{1,0},{2,3},{3,2},{4,5},{5,4},{6,7},{7,6},{8,9},{9,8},{10,11... | collective-permute-start | bytes 1572872 | tf_op jit(solution)/shard_map/ppermute | solution.py:38
  43.8 4.7 %collective-permute-start.7 = (bf16[2,256,512]{2,1,0:T(8,128)(2,1)}, bf16[2,256,512]{2,1,0:T(8,128)(2,1)}, u32[]{:S(2)}, u32[]{:S(2)}) collective-permute-start(bf16[2,256,512]{2,1,0:T(8,128)(2,1)} %get-tuple-element.57), channel_id=1, source_target_pairs={{0,1},{1,0},{2,3},{3,2},{4,5},{5,4},{6,7},{7,6},{8,9},{9,8},{10,11... | collective-permute-start | bytes 1572872 | tf_op jit(solution)/shard_map/ppermute | solution.py:38
  48.1 1.4 collective-permute-start.6
  57.3 31.9 %all-to-all-start.1 = ((bf16[8,192,512]{2,1,0:T(8,128)(2,1)}), bf16[8,192,512]{2,1,0:T(8,128)(2,1)}, u32[]{:S(2)}, u32[]{:S(2)}) async-start(bf16[8,192,512]{2,1,0:T(8,128)(2,1)} %copy-done.38), calls=%async_computation.1 | async-start | bytes 3145728 | tf_op jit(solution)/shard_map/all_to_all | solution.py:193
  64.6 26.4 %copy-start.59 = (bf16[192,512]{1,0:T(8,128)(2,1)S(1)}, bf16[192,512]{1,0:T(8,128)(2,1)}, u32[]{:S(2)}) copy-start(bf16[192,512]{1,0:T(8,128)(2,1)} %param.11) | copy-start | bytes 589828
  64.6 39.7 %copy-start.60 = (bf16[64,512]{1,0:T(8,128)(2,1)S(1)}, bf16[64,512]{1,0:T(8,128)(2,1)}, u32[]{:S(2)}) copy-start(bf16[64,512]{1,0:T(8,128)(2,1)} %param.14) | copy-start | bytes 196612
  89.2 5.8 %copy-start.63 = (bf16[384,512]{1,0:T(8,128)(2,1)S(1)}, bf16[384,512]{1,0:T(8,128)(2,1)}, u32[]{:S(2)}) copy-start(bf16[384,512]{1,0:T(8,128)(2,1)} %param.13) | copy-start | bytes 1179652
  91.0 13.2 %collective-permute-start.11 = (bf16[208,512]{1,0:T(8,128)(2,1)S(1)}, bf16[208,512]{1,0:T(8,128)(2,1)S(1)}, u32[]{:S(2)}, u32[]{:S(2)}) collective-permute-start(bf16[208,512]{1,0:T(8,128)(2,1)S(1)} %concatenate.25), channel_id=1, source_target_pairs={{0,16},{16,32},{32,48},{48,64},{64,80},{80,96},{96,112},{112,128},... | collective-permute-start | bytes 638984 | tf_op jit(solution)/shard_map/ppermute | solution.py:42
  105.1 25.6 %copy-start.5 = (bf16[2,512,512]{2,1,0:T(8,128)(2,1)S(1)}, bf16[2,512,512]{2,1,0:T(8,128)(2,1)}, u32[]{:S(2)}) copy-start(bf16[2,512,512]{2,1,0:T(8,128)(2,1)} %copy-done.3) | copy-start | bytes 3145732
  105.1 25.6 %copy-start.10 = (bf16[2,512,512]{2,1,0:T(8,128)(2,1)S(1)}, bf16[2,512,512]{2,1,0:T(8,128)(2,1)}, u32[]{:S(2)}) copy-start(bf16[2,512,512]{2,1,0:T(8,128)(2,1)} %copy-done.8) | copy-start | bytes 3145732
  105.1 25.6 %copy-start.15 = (bf16[2,512,512]{2,1,0:T(8,128)(2,1)S(1)}, bf16[2,512,512]{2,1,0:T(8,128)(2,1)}, u32[]{:S(2)}) copy-start(bf16[2,512,512]{2,1,0:T(8,128)(2,1)} %copy-done.13) | copy-start | bytes 3145732
  130.7 8.0 %copy-start.50 = (f32[2,128]{1,0:T(2,128)S(1)}, f32[2,128]{1,0:T(2,128)}, u32[]{:S(2)}) copy-start(f32[2,128]{1,0:T(2,128)} %copy-done.49) | copy-start | bytes 3076
  136.5 2.2 collective-permute-start.12
  141.8 8.1 %copy-start.51 = (f32[2,128]{1,0:T(2,128)}, f32[2,128]{1,0:T(2,128)S(1)}, u32[]{:S(2)}) copy-start(f32[2,128]{1,0:T(2,128)S(1)} %get-tuple-element.69.z_ref) | copy-start | bytes 3076
  141.8 1.4 collective-permute-start.13
  175.6 11.3 %copy-start.62 = (bf16[128,512]{1,0:T(8,128)(2,1)S(1)}, bf16[128,512]{1,0:T(8,128)(2,1)}, u32[]{:S(2)}) copy-start(bf16[128,512]{1,0:T(8,128)(2,1)} %get-tuple-element.77) | copy-start | bytes 393220
  176.6 10.3 %collective-permute-start.14 = (bf16[208,512]{1,0:T(8,128)(2,1)S(1)}, bf16[208,512]{1,0:T(8,128)(2,1)S(1)}, u32[]{:S(2)}, u32[]{:S(2)}) collective-permute-start(bf16[208,512]{1,0:T(8,128)(2,1)S(1)} %concatenate.26), channel_id=1, source_target_pairs={{0,16},{16,32},{32,48},{48,64},{64,80},{80,96},{96,112},{112,128},... | collective-permute-start | bytes 638984 | tf_op jit(solution)/shard_map/ppermute | solution.py:42
  187.7 25.1 %copy-start.6 = (bf16[2,512,512]{2,1,0:T(8,128)(2,1)S(1)}, bf16[2,512,512]{2,1,0:T(8,128)(2,1)}, u32[]{:S(2)}) copy-start(bf16[2,512,512]{2,1,0:T(8,128)(2,1)} %copy-done.3) | copy-start | bytes 3145732
  187.7 25.1 %copy-start.11 = (bf16[2,512,512]{2,1,0:T(8,128)(2,1)S(1)}, bf16[2,512,512]{2,1,0:T(8,128)(2,1)}, u32[]{:S(2)}) copy-start(bf16[2,512,512]{2,1,0:T(8,128)(2,1)} %copy-done.8) | copy-start | bytes 3145732
  187.8 25.1 %copy-start.16 = (bf16[2,512,512]{2,1,0:T(8,128)(2,1)S(1)}, bf16[2,512,512]{2,1,0:T(8,128)(2,1)}, u32[]{:S(2)}) copy-start(bf16[2,512,512]{2,1,0:T(8,128)(2,1)} %copy-done.13) | copy-start | bytes 3145732
  212.8 8.0 %copy-start.52 = (f32[2,128]{1,0:T(2,128)S(1)}, f32[2,128]{1,0:T(2,128)}, u32[]{:S(2)}) copy-start(f32[2,128]{1,0:T(2,128)} %copy-done.51) | copy-start | bytes 3076
  218.6 2.2 collective-permute-start.15
  223.9 1.4 collective-permute-start.16
  257.7 12.7 %copy-start.61 = (bf16[128,512]{1,0:T(8,128)(2,1)S(1)}, bf16[128,512]{1,0:T(8,128)(2,1)}, u32[]{:S(2)}) copy-start(bf16[128,512]{1,0:T(8,128)(2,1)} %get-tuple-element.75) | copy-start | bytes 393220
  258.7 11.7 %collective-permute-start.17 = (bf16[208,512]{1,0:T(8,128)(2,1)S(1)}, bf16[208,512]{1,0:T(8,128)(2,1)S(1)}, u32[]{:S(2)}, u32[]{:S(2)}) collective-permute-start(bf16[208,512]{1,0:T(8,128)(2,1)S(1)} %concatenate.27), channel_id=1, source_target_pairs={{0,16},{16,32},{32,48},{48,64},{64,80},{80,96},{96,112},{112,128},... | collective-permute-start | bytes 638984 | tf_op jit(solution)/shard_map/ppermute | solution.py:42
  271.2 23.9 %copy-start.7 = (bf16[2,512,512]{2,1,0:T(8,128)(2,1)S(1)}, bf16[2,512,512]{2,1,0:T(8,128)(2,1)}, u32[]{:S(2)}) copy-start(bf16[2,512,512]{2,1,0:T(8,128)(2,1)} %copy-done.3) | copy-start | bytes 3145732
  271.2 23.9 %copy-start.12 = (bf16[2,512,512]{2,1,0:T(8,128)(2,1)S(1)}, bf16[2,512,512]{2,1,0:T(8,128)(2,1)}, u32[]{:S(2)}) copy-start(bf16[2,512,512]{2,1,0:T(8,128)(2,1)} %copy-done.8) | copy-start | bytes 3145732
  271.2 23.9 %copy-start.17 = (bf16[2,512,512]{2,1,0:T(8,128)(2,1)S(1)}, bf16[2,512,512]{2,1,0:T(8,128)(2,1)}, u32[]{:S(2)}) copy-start(bf16[2,512,512]{2,1,0:T(8,128)(2,1)} %copy-done.13) | copy-start | bytes 3145732
  300.4 4.9 %copy-start.22 = (bf16[2,256,512]{2,1,0:T(8,128)(2,1)S(1)}, bf16[2,256,512]{2,1,0:T(8,128)(2,1)}, u32[]{:S(2)}) copy-start(bf16[2,256,512]{2,1,0:T(8,128)(2,1)} %copy-done.18) | copy-start | bytes 1572868
  300.5 4.9 %copy-start.27 = (bf16[2,256,512]{2,1,0:T(8,128)(2,1)S(1)}, bf16[2,256,512]{2,1,0:T(8,128)(2,1)}, u32[]{:S(2)}) copy-start(bf16[2,256,512]{2,1,0:T(8,128)(2,1)} %copy-done.23) | copy-start | bytes 1572868
  300.5 2.1 collective-permute-start.18
  304.0 1.4 collective-permute-start.19
  (40 other events, 39.2 us)

commit v3 on v2

v3 whole, which is shorter than its diff:
```python
import functools

import jax
import jax.numpy as jnp
from jax import lax
from jax.experimental import pallas as pl
from jax.experimental.pallas import tpu as pltpu
from jax.sharding import Mesh
from jax.sharding import PartitionSpec as P

SEG = 128
PIECE = 192
MEM = 64
EPS = 1e-05
AXES = ("y_lo", "z", "x", "y_hi", "core")
SECTION = ("y_lo", "z")
TENSOR = ("x", "y_hi", "core")
CHIPS = ("x", "y_hi")
N_CHIPS = 8
FLAG_ROWS = 16
BLOCK = 512
HEADS = 2
SIDE = 128
GATE_ROWS = 16
HD = 128
WIDE = HEADS * HD
HIDDEN = 8192
VMEM_LIMIT = 48 * 2**20
HIGHEST = lax.Precision.HIGHEST


VMEM = pl.BlockSpec(memory_space=pltpu.VMEM)
SMEM = pl.BlockSpec(memory_space=pltpu.SMEM)


def swap(value, axis):
    return lax.ppermute(value, axis, [(0, 1), (1, 0)])


def next_section(value):
    return lax.ppermute(value, SECTION, [(i, i + 1) for i in range(15)])


ANY = pl.BlockSpec(memory_space=pl.ANY)


def pick_kernel(core_ref, f_ref, keep_ref, sent_ref):
    core = core_ref[0]
    keep_ref[0] = f_ref[:, pl.ds(pl.multiple_of(core * BLOCK, BLOCK), BLOCK)]
    sent_ref[0] = f_ref[:, pl.ds(pl.multiple_of((1 - core) * BLOCK, BLOCK), BLOCK)]


def pick(core, f):
    block = pl.BlockSpec((1, WIDE, BLOCK), lambda b: (b, 0, 0))
    shape = jax.ShapeDtypeStruct((N_CHIPS, WIDE, BLOCK), jnp.bfloat16)
    return pl.pallas_call(
        pick_kernel,
        grid=(N_CHIPS,),
        in_specs=[SMEM, pl.BlockSpec((WIDE, 2 * BLOCK), lambda b: (0, b))],
        out_specs=[block, block],
        out_shape=[shape, shape],
        compiler_params=pltpu.CompilerParams(vmem_limit_bytes=VMEM_LIMIT),
        cost_estimate=pl.CostEstimate(flops=0, bytes_accessed=0, transcendentals=0),
    )(core, f)


def project_half(write, offset, x_ref, gain_ref, wk_ref, wv_ref, gate_ref, bufs, sems):
    x_buf, k_buf, v_buf = bufs
    rows = x_ref.shape[1]
    copies = []
    for b in range(N_CHIPS):
        place = 2 * b + offset
        group = []
        for i, (source, target) in enumerate(
            (
                (x_ref.at[b], x_buf.at[b]),
                (wk_ref.at[place], k_buf.at[b]),
                (wv_ref.at[place], v_buf.at[b]),
            )
        ):
            copy = pltpu.make_async_copy(source, target, sems.at[i, b])
            copy.start()
            group.append(copy)
        copies.append(group)
    dot = functools.partial(jnp.dot, preferred_element_type=jnp.float32)
    squares, gates, keys, values = 0.0, 0.0, 0.0, 0.0
    for b in range(N_CHIPS):
        place = 2 * b + offset
        for copy in copies[b]:
            copy.wait()
        wide = x_buf[b].astype(jnp.float32)
        squares += wide * wide
        scaled = (wide * gain_ref[place]).astype(jnp.bfloat16)
        keys += dot(scaled, k_buf[b])
        values += dot(scaled, v_buf[b])
        if write:
            gates += lax.dot_general(
                scaled[rows - MEM :],
                gate_ref[place],
                (((1,), (1,)), ((), ())),
                preferred_element_type=jnp.float32,
            )
    return keys, values, jnp.sum(squares, axis=1, keepdims=True), gates


def first_kernel(write, core_ref, x_ref, gain_ref, wk_ref, wv_ref, gate_ref, sum_ref, *rest):
    *bufs, sems = rest
    rows = x_ref.shape[1]
    keys, values, squares, gates = project_half(
        write, core_ref[0], x_ref, gain_ref, wk_ref, wv_ref, gate_ref, bufs, sems
    )
    sum_ref[:, :WIDE] = keys
    sum_ref[:, WIDE : 2 * WIDE] = values
    lane = lax.broadcasted_iota(jnp.int32, (rows, SIDE), 1)
    side = jnp.where(lane == GATE_ROWS, squares, 0.0)
    sum_ref[:, 2 * WIDE :] = side
    if write:
        sum_ref[rows - MEM :, 2 * WIDE : 2 * WIDE + GATE_ROWS] = gates


def read_kernel(
    write, core_ref, keep_ref, sum_ref, x_ref, gain_ref, wk_ref, wv_ref, gate_ref, a_ref, z_ref,
    read_ref, *rest,
):
    *state, x_buf, k_buf, v_buf, sems = rest
    rows = x_ref.shape[1]
    keys, values, squares, gates = project_half(
        write, 1 - core_ref[0], x_ref, gain_ref, wk_ref, wv_ref, gate_ref,
        (x_buf, k_buf, v_buf), sems,
    )
    keys += sum_ref[:, :WIDE]
    values += sum_ref[:, WIDE : 2 * WIDE]
    side = sum_ref[:, 2 * WIDE :]
    squares += side[:, GATE_ROWS : GATE_ROWS + 1]
    scale = lax.rsqrt(squares * (1.0 / HIDDEN) + EPS)
    keep = keep_ref[0, 0]
    for h in range(HEADS):
        a = a_ref[h] * keep
        z = z_ref[h : h + 1] * keep
        k = keys[:, h * HD : (h + 1) * HD] * scale
        k = jnp.where(k > 0, k + 1.0, jnp.exp(jnp.minimum(k, 0.0)))
        top = jnp.dot(k, a, precision=HIGHEST, preferred_element_type=jnp.float32)
        bottom = jnp.sum(k * z, axis=1, keepdims=True) + 1.0
        read = top / bottom
        read_ref[:, h * HD : (h + 1) * HD] = read.astype(jnp.bfloat16)
        if write:
            v = values[rows - MEM :, h * HD : (h + 1) * HD] * scale[rows - MEM :]
            logit = (side[rows - MEM :, h : h + 1] + gates[:, h : h + 1]) * scale[rows - MEM :]
            gate = 1.0 / (1.0 + jnp.exp(-logit))
            tail = k[rows - MEM :]
            state[0][h] = a + lax.dot_general(
                tail,
                (v - read[rows - MEM :]) * gate,
                (((0,), (0,)), ((), ())),
                precision=HIGHEST,
                preferred_element_type=jnp.float32,
            )
            state[1][h : h + 1] = z + jnp.sum(tail, axis=0, keepdims=True)


def half_scratch(rows):
    weights = pltpu.VMEM((N_CHIPS, BLOCK, WIDE), jnp.bfloat16)
    x = pltpu.VMEM((N_CHIPS, rows, BLOCK), jnp.bfloat16)
    return [x, weights, weights, pltpu.SemaphoreType.DMA((3, N_CHIPS))]


def project_first(core, own, gain, wk, wv, gate, write):
    rows = own.shape[1]
    return pl.pallas_call(
        functools.partial(first_kernel, write),
        in_specs=[SMEM, ANY, VMEM, ANY, ANY, VMEM],
        out_specs=VMEM,
        out_shape=jax.ShapeDtypeStruct((rows, 2 * WIDE + SIDE), jnp.float32),
        scratch_shapes=half_scratch(rows),
        compiler_params=pltpu.CompilerParams(vmem_limit_bytes=VMEM_LIMIT),
        cost_estimate=pl.CostEstimate(
            flops=rows * HIDDEN * 2 * WIDE, bytes_accessed=6 * 2**20, transcendentals=0
        ),
    )(core, own, gain, wk, wv, gate)


def read_memory(core, keep, begun, got, gain, wk, wv, gate, a, z, write):
    rows = got.shape[1]
    shapes = [jax.ShapeDtypeStruct((rows, WIDE), jnp.bfloat16)]
    if write:
        shapes += [jax.ShapeDtypeStruct(a.shape, a.dtype), jax.ShapeDtypeStruct(z.shape, z.dtype)]
    return pl.pallas_call(
        functools.partial(read_kernel, write),
        in_specs=[SMEM, SMEM, VMEM, ANY, VMEM, ANY, ANY, VMEM, VMEM, VMEM],
        out_specs=[VMEM] * len(shapes),
        out_shape=shapes,
        scratch_shapes=half_scratch(rows),
        compiler_params=pltpu.CompilerParams(vmem_limit_bytes=VMEM_LIMIT),
        cost_estimate=pl.CostEstimate(
            flops=rows * HIDDEN * 2 * WIDE, bytes_accessed=6 * 2**20, transcendentals=0
        ),
    )(core, keep, begun, got, gain, wk, wv, gate, a, z)


def output_kernel(near_ref, far_ref, keep_ref, got_ref, p_ref, got_buf, sems):
    copies = []
    for b in range(N_CHIPS):
        copies.append(pltpu.make_async_copy(got_ref.at[b], got_buf.at[b], sems.at[b]))
        copies[-1].start()
    near, far = near_ref[...], far_ref[...]
    for b in range(N_CHIPS):
        part = jnp.dot(near, keep_ref[b], preferred_element_type=jnp.float32)
        copies[b].wait()
        part += jnp.dot(far, got_buf[b], preferred_element_type=jnp.float32)
        p_ref[b] = part.astype(jnp.bfloat16)


def output(near, far, keep, got):
    rows = near.shape[0]
    return pl.pallas_call(
        output_kernel,
        in_specs=[VMEM, VMEM, VMEM, ANY],
        out_specs=VMEM,
        out_shape=jax.ShapeDtypeStruct((N_CHIPS, rows, BLOCK), jnp.bfloat16),
        scratch_shapes=[
            pltpu.VMEM((N_CHIPS, WIDE, BLOCK), jnp.bfloat16),
            pltpu.SemaphoreType.DMA((N_CHIPS,)),
        ],
        compiler_params=pltpu.CompilerParams(vmem_limit_bytes=VMEM_LIMIT),
        cost_estimate=pl.CostEstimate(
            flops=2 * rows * 2 * WIDE * 4096, bytes_accessed=2 * 2**20, transcendentals=0
        ),
    )(near, far, keep, got)


def copies(x):
    return jnp.broadcast_to(x[None], (N_CHIPS,) + x.shape)


def exchange(blocks):
    return lax.all_to_all(blocks, CHIPS, 0, 0, tiled=True)


def local(
    initial_stack_inputs,
    initial_sequence_starts,
    arriving_pieces,
    recall_embeddings,
    rescaling_factors,
    lookup_projection,
    content_projection,
    write_gate_projection,
    final_projection,
    associative_stores,
    denominator_vectors,
):
    core = lax.axis_index("core")
    which = core.astype(jnp.int32).reshape(1)
    section_zero = (lax.axis_index("y_lo") == 0) & (lax.axis_index("z") == 0)
    steps = arriving_pieces.shape[0] // SEG + 1

    x = initial_stack_inputs
    outgoing, which = lax.optimization_barrier((copies(x), which))
    flag = (initial_sequence_starts[0] > 0).astype(jnp.bfloat16)

    wk = lookup_projection[0].reshape(2 * N_CHIPS, BLOCK, WIDE)
    wv = content_projection[0].reshape(2 * N_CHIPS, BLOCK, WIDE)
    f_keep, f_sent = pick(which, final_projection[0])
    f_got = swap(f_sent, "core")
    gain = rescaling_factors.reshape(2 * N_CHIPS, 1, BLOCK)
    gate = write_gate_projection[0].T.reshape(HEADS, 2 * N_CHIPS, BLOCK).transpose(1, 0, 2)
    gate = jnp.pad(gate, ((0, 0), (0, GATE_ROWS - HEADS), (0, 0)))

    a = associative_stores[0]
    z = denominator_vectors[0]
    for t in range(steps):
        write = t + 1 < steps
        if t > 0:
            sent = jnp.concatenate([x, jnp.broadcast_to(flag, (FLAG_ROWS, BLOCK))], axis=0)
            moved = next_section(sent)
            entering = jnp.concatenate(
                [arriving_pieces[(t - 1) * SEG : t * SEG], recall_embeddings], axis=0
            )
            x = jnp.where(section_zero, entering, moved[:PIECE])
            flag = jnp.where(section_zero, jnp.zeros((), jnp.bfloat16), moved[PIECE, 0])
            outgoing = copies(x)
        keep = (1.0 - flag.astype(jnp.float32)).reshape(1, 1)
        own = exchange(outgoing)
        got = swap(own, "core")
        begun = project_first(which, own, gain, wk, wv, gate, write)
        read, *state = read_memory(which, keep, begun, got, gain, wk, wv, gate, a, z, write)
        if write:
            a, z = state
        p = exchange(output(read, swap(read, "core"), f_keep, f_got))
        total = jnp.sum(p.astype(jnp.float32), axis=0)
        x = (x.astype(jnp.float32) + total).astype(jnp.bfloat16)
    return x


def solution(mesh):
    fine = Mesh(mesh.devices.reshape(2, 8, 4, 2, 2), AXES)
    return jax.shard_map(
        local,
        mesh=fine,
        in_specs=(
            P(SECTION, TENSOR),
            P(SECTION),
            P(None, TENSOR),
            P(None, TENSOR),
            P(SECTION, None),
            P(SECTION, None, TENSOR),
            P(SECTION, None, TENSOR),
            P(SECTION, None, TENSOR),
            P(SECTION, TENSOR, None),
            P(SECTION, TENSOR, None, None),
            P(SECTION, TENSOR, None),
        ),
        out_specs=P(SECTION, TENSOR),
        check_vma=False,
    )
```

time: 339 us -> 309 us (0.912)
  local copies, waits for them, and re-layouts: 52.2 us -> 5.48 us
  waiting for transfers between devices: 59.5 us -> 77.3 us
  Pallas kernels: 42.1 us -> 49.9 us
  starting transfers between devices: 24.7 us -> 20.6 us
    unnamed x135 -> x16, local copies, waits for them, and re-layouts: 44.2 us -> 1.19 us
    all_to_all x2, waiting for transfers between devices: 24.6 us -> 42.8 us  [exchange(): return lax.all_to_all(blocks, CHIPS, 0, 0, tiled=True)]
    pallas_call x16 -> x13, Pallas kernels: 42.1 us -> 49.9 us  [the longest x4 17.6 us: read_memory(): pl.pallas_call(functools.partial(read_kernel, write), in_specs=[SMEM, SME...]
    ppermute x17 -> x9, waiting for transfers between devices: 8.33 us -> 3.79 us  [swap(): return lax.ppermute(value, axis, [(0, 1), (1, 0)])]
    ppermute x3, waiting for transfers between devices: 26.5 us -> 30.7 us  [next_section(): return lax.ppermute(value, SECTION, [(i, i + 1) for i in range(15)])]
  transfers between devices with their start and end apart: 22 -> 14, of which waited for: 13 -> 9; matrix products, arithmetic and copies ran while one was open for 2% -> 1% of each run, Pallas kernels for 2% -> 8%
where the time goes in v3:
time: 309 us; the launch traced here: 308 us
  blocking collectives  149 us (48%)
  waiting for transfers between devices  77.3 us (25%)
  Pallas kernels  49.9 us (16%)
  starting transfers between devices  20.6 us (7%)
  local copies, waits for them, and re-layouts  5.48 us (2%)
  other arithmetic  3.4 us (1%)
    all_to_all x6, blocking collectives, exchange(): return lax.all_to_all(blocks, CHIPS, 0, 0, tiled=True)  149 us
    all_to_all x2, waiting for transfers between devices, exchange(): return lax.all_to_all(blocks, CHIPS, 0, 0, tiled=True)  42.8 us
    ppermute x3, waiting for transfers between devices, next_section(): return lax.ppermute(value, SECTION, [(i, i + 1) for i in range(15)])  30.7 us
    pallas_call x4, Pallas kernels, read_memory(): pl.pallas_call(functools.partial(read_kernel, write), in_specs=[SMEM, SME...  17.6 us
    pallas_call x4, Pallas kernels, output(): pl.pallas_call(output_kernel, in_specs=[VMEM, VMEM, VMEM, ANY], out_specs...  13.2 us
    pallas_call x4, Pallas kernels, project_first(): pl.pallas_call(functools.partial(first_kernel, write), in_specs=[SMEM, AN...  12.9 us
    all_to_all x2, starting transfers between devices, exchange(): return lax.all_to_all(blocks, CHIPS, 0, 0, tiled=True)  10.3 us
    ppermute x3, starting transfers between devices, next_section(): return lax.ppermute(value, SECTION, [(i, i + 1) for i in range(15)])  7.66 us
  transfers between devices with their start and end apart: 14, of which 9 were waited for; matrix products, arithmetic and copies ran while one was open for 1% of the time, Pallas kernels for 8%

profile of v3, /device:TPU:8, one launch (start us, length us, event | category | flops | bytes accessed | tf_op | source)
XLA Modules:
  0.0 308.2 jit_solution(10585992569705751095)
XLA Ops:
  0.0 2.2 broadcast_in_dim.8
  2.2 6.0 %all-to-all-start = ((bf16[8,192,512]{2,1,0:T(8,128)(2,1)}), bf16[8,192,512]{2,1,0:T(8,128)(2,1)}, u32[]{:S(2)}, u32[]{:S(2)}) async-start(bf16[8,192,512]{2,1,0:T(8,128)(2,1)} %broadcast_in_dim.8), calls=%async_computation | async-start | bytes 3145728 | tf_op jit(solution)/shard_map/all_to_all | solution.py:236
  8.3 6.1 %shard_map.111 = (bf16[8,256,512]{2,1,0:T(8,128)(2,1)S(1)}, bf16[8,256,512]{2,1,0:T(8,128)(2,1)}) custom-call(s32[1]{0:T(128)} %bitcast.core_ref, bf16[256,8192]{1,0:T(8,128)(2,1)} %bitcast.48), custom_call_target="tpu_custom_call" | custom-call | tf_op jit(solution)/shard_map/pallas_call | solution.py:56
  14.4 17.6 %all-to-all-done.x_ref = bf16[8,192,512]{2,1,0:T(8,128)(2,1)} async-done(((bf16[8,192,512]{2,1,0:T(8,128)(2,1)}), bf16[8,192,512]{2,1,0:T(8,128)(2,1)}, u32[]{:S(2)}, u32[]{:S(2)}) %all-to-all-start) | async-done | bytes 1572896 | tf_op jit(solution)/shard_map/all_to_all | solution.py:236
  32.8 3.3 %shard_map.109.sum_ref = f32[192,640]{1,0:T(8,128)S(1)} custom-call(s32[1]{0:T(128)} %bitcast.core_ref, bf16[8,192,512]{2,1,0:T(8,128)(2,1)} %all-to-all-done.x_ref, f32[16,1,512]{2,1,0:T(1,128)S(1)} %bitcast.22, bf16[16,512,256]{2,1,0:T(8,128)(2,1)} %bitcast.32, bf16[16,512,256]{2,1,0:T(8,128)(2,1)} %bitcast.40, bf16[16,16,512]{2,1,0:T(8,128)(2,1)S(1)} %pad.7.gate_ref), custom_call_target="tpu_custom_call" | custom-call | flops 805306368 | bytes 6291456 | tf_op jit(solution)/shard_map/pallas_call | solution.py:169
  36.2 4.7 %shard_map.110 = (bf16[192,256]{1,0:T(8,128)(2,1)S(1)}, f32[2,128,128]{2,1,0:T(8,128)S(1)}, f32[2,128]{1,0:T(2,128)S(1)}) custom-call(s32[1]{0:T(128)} %bitcast.core_ref, f32[1,1]{1,0:T(1,128)} %bitcast.2.keep_ref, f32[192,640]{1,0:T(8,128)S(1)} %shard_map.109.sum_ref, bf16[8,192,512]{2,1,0:T(8,128)(2,1)} %collective-permute-done.x_ref, ...), custom_call_target="tpu_custom_call" | custom-call | flops 805306368 | bytes 6291456 | tf_op jit(solution)/shard_map/pallas_call | solution.py:187
  40.9 0.6 collective-permute-start.1
  41.5 0.9 collective-permute-done.1.far_ref
  42.4 3.3 %shard_map.112 = bf16[8,192,512]{2,1,0:T(8,128)(2,1)S(1)} custom-call(bf16[192,256]{1,0:T(8,128)(2,1)S(1)} %get-tuple-element.20.near_ref, bf16[192,256]{1,0:T(8,128)(2,1)S(1)} %collective-permute-done.1.far_ref, bf16[8,256,512]{2,1,0:T(8,128)(2,1)S(1)} %get-tuple-element.21.keep_ref, bf16[8,256,512]{2,1,0:T(8,128)(2,1)} %collective-permute-done.2.got_ref), custom_call_target="tpu_custom_call" | custom-call | flops 805306368 | bytes 2097152 | tf_op jit(solution)/shard_map/pallas_call | solution.py:215
  45.7 1.1 copy-done
  46.9 4.3 %all-to-all-start.1 = ((bf16[8,192,512]{2,1,0:T(8,128)(2,1)}), bf16[8,192,512]{2,1,0:T(8,128)(2,1)}, u32[]{:S(2)}, u32[]{:S(2)}) async-start(bf16[8,192,512]{2,1,0:T(8,128)(2,1)} %copy-done), calls=%async_computation.1 | async-start | bytes 3145728 | tf_op jit(solution)/shard_map/all_to_all | solution.py:236
  51.2 25.2 %all-to-all-done.1 = bf16[8,192,512]{2,1,0:T(8,128)(2,1)} async-done(((bf16[8,192,512]{2,1,0:T(8,128)(2,1)}), bf16[8,192,512]{2,1,0:T(8,128)(2,1)}, u32[]{:S(2)}, u32[]{:S(2)}) %all-to-all-start.1) | async-done | bytes 1572896 | tf_op jit(solution)/shard_map/all_to_all | solution.py:236
  76.4 1.7 convert_reduce_fusion.3
  78.2 3.8 %collective-permute-start.3 = (bf16[208,512]{1,0:T(8,128)(2,1)S(1)}, bf16[208,512]{1,0:T(8,128)(2,1)S(1)}, u32[]{:S(2)}, u32[]{:S(2)}) collective-permute-start(bf16[208,512]{1,0:T(8,128)(2,1)S(1)} %concatenate.21), channel_id=1, source_target_pairs={{0,16},{16,32},{32,48},{48,64},{64,80},{80,96},{96,112},{112,128},... | collective-permute-start | bytes 638984 | tf_op jit(solution)/shard_map/ppermute | solution.py:41
  82.0 9.7 %collective-permute-done.3 = bf16[208,512]{1,0:T(8,128)(2,1)S(1)} collective-permute-done((bf16[208,512]{1,0:T(8,128)(2,1)S(1)}, bf16[208,512]{1,0:T(8,128)(2,1)S(1)}, u32[]{:S(2)}, u32[]{:S(2)}) %collective-permute-start.3) | collective-permute-done | bytes 213024 | tf_op jit(solution)/shard_map/ppermute | solution.py:41
  92.0 25.1 %all_to_all.40.x_ref = bf16[8,192,512]{2,1,0:T(8,128)(2,1)} all-to-all(bf16[8,192,512]{2,1,0:T(8,128)(2,1)S(1)} %broadcast_in_dim.9), channel_id=1, replica_groups=mesh['y_lo'=2,'z'=8,'x'=4,'y_hi'=2,'core'=2] {'x','y_hi'}, dimensions={0} | all-to-all | bytes 3145728 | tf_op jit(solution)/shard_map/all_to_all | solution.py:236
  117.1 0.5 slice.37
  118.2 3.2 %shard_map.113.sum_ref = f32[192,640]{1,0:T(8,128)S(1)} custom-call(s32[1]{0:T(128)} %bitcast.core_ref, bf16[8,192,512]{2,1,0:T(8,128)(2,1)} %all_to_all.40.x_ref, f32[16,1,512]{2,1,0:T(1,128)S(1)} %bitcast.24, bf16[16,512,256]{2,1,0:T(8,128)(2,1)} %bitcast.34, bf16[16,512,256]{2,1,0:T(8,128)(2,1)} %bitcast.42, bf16[16,16,512]{2,1,0:T(8,128)(2,1)S(1)} %pad.7.gate_ref), custom_call_target="tpu_custom_call" | custom-call | flops 805306368 | bytes 6291456 | tf_op jit(solution)/shard_map/pallas_call | solution.py:169
  121.5 4.7 %shard_map.114 = (bf16[192,256]{1,0:T(8,128)(2,1)S(1)}, f32[2,128,128]{2,1,0:T(8,128)S(1)}, f32[2,128]{1,0:T(2,128)S(1)}) custom-call(s32[1]{0:T(128)} %bitcast.core_ref, f32[1,1]{1,0:T(1,128)} %bitcast.14.keep_ref, f32[192,640]{1,0:T(8,128)S(1)} %shard_map.113.sum_ref, bf16[8,192,512]{2,1,0:T(8,128)(2,1)} %collective-permute-done.4.x_ref, ...), custom_call_target="tpu_custom_call" | custom-call | flops 805306368 | bytes 6291456 | tf_op jit(solution)/shard_map/pallas_call | solution.py:187
  126.2 0.6 collective-permute-start.5
  126.8 0.9 collective-permute-done.5.far_ref
  127.7 3.3 %shard_map.115 = bf16[8,192,512]{2,1,0:T(8,128)(2,1)S(1)} custom-call(bf16[192,256]{1,0:T(8,128)(2,1)S(1)} %get-tuple-element.25.near_ref, bf16[192,256]{1,0:T(8,128)(2,1)S(1)} %collective-permute-done.5.far_ref, bf16[8,256,512]{2,1,0:T(8,128)(2,1)S(1)} %get-tuple-element.21.keep_ref, bf16[8,256,512]{2,1,0:T(8,128)(2,1)} %collective-permute-done.2.got_ref), custom_call_target="tpu_custom_call" | custom-call | flops 805306368 | bytes 2097152 | tf_op jit(solution)/shard_map/pallas_call | solution.py:215
  131.0 25.9 %all_to_all.41 = bf16[8,192,512]{2,1,0:T(8,128)(2,1)S(1)} all-to-all(bf16[8,192,512]{2,1,0:T(8,128)(2,1)S(1)} %shard_map.115), channel_id=1, replica_groups=mesh['y_lo'=2,'z'=8,'x'=4,'y_hi'=2,'core'=2] {'x','y_hi'}, dimensions={0} | all-to-all | bytes 3145728 | tf_op jit(solution)/shard_map/all_to_all | solution.py:236
  156.9 0.2 convert_reduce_fusion.2
  157.2 1.9 collective-permute-start.6
  159.1 9.3 %collective-permute-done.6 = bf16[208,512]{1,0:T(8,128)(2,1)S(1)} collective-permute-done((bf16[208,512]{1,0:T(8,128)(2,1)S(1)}, bf16[208,512]{1,0:T(8,128)(2,1)S(1)}, u32[]{:S(2)}, u32[]{:S(2)}) %collective-permute-start.6) | collective-permute-done | bytes 213024 | tf_op jit(solution)/shard_map/ppermute | solution.py:41
  168.5 0.1 broadcast_in_dim.10
  168.6 23.9 %all_to_all.42.x_ref = bf16[8,192,512]{2,1,0:T(8,128)(2,1)} all-to-all(bf16[8,192,512]{2,1,0:T(8,128)(2,1)S(1)} %broadcast_in_dim.10), channel_id=1, replica_groups=mesh['y_lo'=2,'z'=8,'x'=4,'y_hi'=2,'core'=2] {'x','y_hi'}, dimensions={0} | all-to-all | bytes 3145728 | tf_op jit(solution)/shard_map/all_to_all | solution.py:236
  192.5 0.5 slice.39
  193.7 3.2 %shard_map.116.sum_ref = f32[192,640]{1,0:T(8,128)S(1)} custom-call(s32[1]{0:T(128)} %bitcast.core_ref, bf16[8,192,512]{2,1,0:T(8,128)(2,1)} %all_to_all.42.x_ref, f32[16,1,512]{2,1,0:T(1,128)S(1)} %bitcast.26, bf16[16,512,256]{2,1,0:T(8,128)(2,1)} %bitcast.36, bf16[16,512,256]{2,1,0:T(8,128)(2,1)} %bitcast.44, bf16[16,16,512]{2,1,0:T(8,128)(2,1)S(1)} %pad.7.gate_ref), custom_call_target="tpu_custom_call" | custom-call | flops 805306368 | bytes 6291456 | tf_op jit(solution)/shard_map/pallas_call | solution.py:169
  196.9 4.7 %shard_map.117 = (bf16[192,256]{1,0:T(8,128)(2,1)S(1)}, f32[2,128,128]{2,1,0:T(8,128)S(1)}, f32[2,128]{1,0:T(2,128)S(1)}) custom-call(s32[1]{0:T(128)} %bitcast.core_ref, f32[1,1]{1,0:T(1,128)} %bitcast.16.keep_ref, f32[192,640]{1,0:T(8,128)S(1)} %shard_map.116.sum_ref, bf16[8,192,512]{2,1,0:T(8,128)(2,1)} %collective-permute-done.7.x_ref, ...), custom_call_target="tpu_custom_call" | custom-call | flops 805306368 | bytes 6291456 | tf_op jit(solution)/shard_map/pallas_call | solution.py:187
  201.6 0.8 collective-permute-start.8
  202.4 0.9 collective-permute-done.8.far_ref
  203.4 3.3 %shard_map.118 = bf16[8,192,512]{2,1,0:T(8,128)(2,1)S(1)} custom-call(bf16[192,256]{1,0:T(8,128)(2,1)S(1)} %get-tuple-element.28.near_ref, bf16[192,256]{1,0:T(8,128)(2,1)S(1)} %collective-permute-done.8.far_ref, bf16[8,256,512]{2,1,0:T(8,128)(2,1)S(1)} %get-tuple-element.21.keep_ref, bf16[8,256,512]{2,1,0:T(8,128)(2,1)} %collective-permute-done.2.got_ref), custom_call_target="tpu_custom_call" | custom-call | flops 805306368 | bytes 2097152 | tf_op jit(solution)/shard_map/pallas_call | solution.py:215
  206.7 25.9 %all_to_all.43 = bf16[8,192,512]{2,1,0:T(8,128)(2,1)S(1)} all-to-all(bf16[8,192,512]{2,1,0:T(8,128)(2,1)S(1)} %shard_map.118), channel_id=1, replica_groups=mesh['y_lo'=2,'z'=8,'x'=4,'y_hi'=2,'core'=2] {'x','y_hi'}, dimensions={0} | all-to-all | bytes 3145728 | tf_op jit(solution)/shard_map/all_to_all | solution.py:236
  232.6 0.2 convert_reduce_fusion.1
  232.9 1.9 collective-permute-start.9
  234.8 11.7 %collective-permute-done.9 = bf16[208,512]{1,0:T(8,128)(2,1)S(1)} collective-permute-done((bf16[208,512]{1,0:T(8,128)(2,1)S(1)}, bf16[208,512]{1,0:T(8,128)(2,1)S(1)}, u32[]{:S(2)}, u32[]{:S(2)}) %collective-permute-start.9) | collective-permute-done | bytes 213024 | tf_op jit(solution)/shard_map/ppermute | solution.py:41
  246.7 21.9 %all_to_all.44.x_ref = bf16[8,192,512]{2,1,0:T(8,128)(2,1)} all-to-all(bf16[8,192,512]{2,1,0:T(8,128)(2,1)S(1)} %broadcast_in_dim.11), channel_id=1, replica_groups=mesh['y_lo'=2,'z'=8,'x'=4,'y_hi'=2,'core'=2] {'x','y_hi'}, dimensions={0} | all-to-all | bytes 3145728 | tf_op jit(solution)/shard_map/all_to_all | solution.py:236
  268.7 0.5 slice.41
  269.8 3.1 %shard_map.119.sum_ref = f32[192,640]{1,0:T(8,128)S(1)} custom-call(s32[1]{0:T(128)} %bitcast.core_ref, bf16[8,192,512]{2,1,0:T(8,128)(2,1)} %all_to_all.44.x_ref, f32[16,1,512]{2,1,0:T(1,128)S(1)} %bitcast.28, bf16[16,512,256]{2,1,0:T(8,128)(2,1)} %bitcast.38, bf16[16,512,256]{2,1,0:T(8,128)(2,1)} %bitcast.46, bf16[16,16,512]{2,1,0:T(8,128)(2,1)S(1)} %pad.7.gate_ref), custom_call_target="tpu_custom_call" | custom-call | flops 805306368 | bytes 6291456 | tf_op jit(solution)/shard_map/pallas_call | solution.py:169
  273.0 3.6 %shard_map.120.near_ref = bf16[192,256]{1,0:T(8,128)(2,1)S(1)} custom-call(s32[1]{0:T(128)} %bitcast.core_ref, f32[1,1]{1,0:T(1,128)} %bitcast.18.keep_ref, f32[192,640]{1,0:T(8,128)S(1)} %shard_map.119.sum_ref, bf16[8,192,512]{2,1,0:T(8,128)(2,1)} %collective-permute-done.10.x_ref, f32[16,1,512]{2,1,0:T(1,128)S(1)} %bitcast.29, ...), custom_call_target="tpu_custom_call" | custom-call | flops 805306368 | bytes 6291456 | tf_op jit(solution)/shard_map/pallas_call | solution.py:187
  276.6 0.6 collective-permute-start.11
  277.1 0.9 collective-permute-done.11.far_ref
  278.1 3.3 %shard_map.121 = bf16[8,192,512]{2,1,0:T(8,128)(2,1)S(1)} custom-call(bf16[192,256]{1,0:T(8,128)(2,1)S(1)} %shard_map.120.near_ref, bf16[192,256]{1,0:T(8,128)(2,1)S(1)} %collective-permute-done.11.far_ref, bf16[8,256,512]{2,1,0:T(8,128)(2,1)S(1)} %get-tuple-element.21.keep_ref, bf16[8,256,512]{2,1,0:T(8,128)(2,1)} %collective-permute-done.2.got_ref), custom_call_target="tpu_custom_call" | custom-call | flops 805306368 | bytes 2097152 | tf_op jit(solution)/shard_map/pallas_call | solution.py:215
  281.4 25.9 %all_to_all.45 = bf16[8,192,512]{2,1,0:T(8,128)(2,1)S(1)} all-to-all(bf16[8,192,512]{2,1,0:T(8,128)(2,1)S(1)} %shard_map.121), channel_id=1, replica_groups=mesh['y_lo'=2,'z'=8,'x'=4,'y_hi'=2,'core'=2] {'x','y_hi'}, dimensions={0} | all-to-all | bytes 3145728 | tf_op jit(solution)/shard_map/all_to_all | solution.py:236
  307.3 0.2 convert_reduce_fusion
  307.5 0.7 add_convert_fusion
  (38 shorter events, 0.7 us)
Async XLA Ops:
  2.2 29.8 %all-to-all-start = ((bf16[8,192,512]{2,1,0:T(8,128)(2,1)}), bf16[8,192,512]{2,1,0:T(8,128)(2,1)}, u32[]{:S(2)}, u32[]{:S(2)}) async-start(bf16[8,192,512]{2,1,0:T(8,128)(2,1)} %broadcast_in_dim.8), calls=%async_computation | async-start | bytes 3145728 | tf_op jit(solution)/shard_map/all_to_all | solution.py:236
  8.3 24.5 %copy-start.7 = (bf16[1,8192,2]{1,2,0:T(2,128)(2,1)S(1)}, bf16[1,8192,2]{1,2,0:T(2,128)(2,1)}, u32[]{:S(2)}) copy-start(bf16[1,8192,2]{1,2,0:T(2,128)(2,1)} %param.18) | copy-start | bytes 98308
  8.3 24.5 %copy-start.1 = (f32[1,8192]{1,0:T(1,128)S(1)}, f32[1,8192]{1,0:T(1,128)}, u32[]{:S(2)}) copy-start(f32[1,8192]{1,0:T(1,128)} %param.15) | copy-start | bytes 98308
  14.4 27.0 %collective-permute-start.2 = (bf16[8,256,512]{2,1,0:T(8,128)(2,1)}, bf16[8,256,512]{2,1,0:T(8,128)(2,1)}, u32[]{:S(2)}, u32[]{:S(2)}) collective-permute-start(bf16[8,256,512]{2,1,0:T(8,128)(2,1)} %get-tuple-element.22), channel_id=1, source_target_pairs={{0,1},{1,0},{2,3},{3,2},{4,5},{5,4},{6,7},{7,6},{8,9},{9,8},{10,11... | collective-permute-start | bytes 6291464 | tf_op jit(solution)/shard_map/ppermute | solution.py:37
  32.1 4.0 %collective-permute-start = (bf16[8,192,512]{2,1,0:T(8,128)(2,1)}, bf16[8,192,512]{2,1,0:T(8,128)(2,1)}, u32[]{:S(2)}, u32[]{:S(2)}) collective-permute-start(bf16[8,192,512]{2,1,0:T(8,128)(2,1)} %all-to-all-done.x_ref), channel_id=1, source_target_pairs={{0,1},{1,0},{2,3},{3,2},{4,5},{5,4},{6,7},{7,6},{8,9},{9,8},{10,11... | collective-permute-start | bytes 4718600 | tf_op jit(solution)/shard_map/ppermute | solution.py:37
  32.8 3.3 %copy-start.2 = (f32[1,2,128,128]{3,2,1,0:T(8,128)S(1)}, f32[1,2,128,128]{3,2,1,0:T(8,128)}, u32[]{:S(2)}) copy-start(f32[1,2,128,128]{3,2,1,0:T(8,128)} %param.20) | copy-start | bytes 393220
  32.8 3.3 %copy-start.3 = (f32[1,2,128]{2,1,0:T(2,128)S(1)}, f32[1,2,128]{2,1,0:T(2,128)}, u32[]{:S(2)}) copy-start(f32[1,2,128]{2,1,0:T(2,128)} %param.21) | copy-start | bytes 3076
  40.9 1.5 collective-permute-start.1
  45.7 1.2 copy-start
  46.9 29.5 %all-to-all-start.1 = ((bf16[8,192,512]{2,1,0:T(8,128)(2,1)}), bf16[8,192,512]{2,1,0:T(8,128)(2,1)}, u32[]{:S(2)}, u32[]{:S(2)}) async-start(bf16[8,192,512]{2,1,0:T(8,128)(2,1)} %copy-done), calls=%async_computation.1 | async-start | bytes 3145728 | tf_op jit(solution)/shard_map/all_to_all | solution.py:236
  51.2 26.9 %copy-start.4 = (bf16[192,512]{1,0:T(8,128)(2,1)S(1)}, bf16[192,512]{1,0:T(8,128)(2,1)}, u32[]{:S(2)}) copy-start(bf16[192,512]{1,0:T(8,128)(2,1)} %param.11) | copy-start | bytes 589828
  51.2 40.6 %copy-start.5 = (bf16[64,512]{1,0:T(8,128)(2,1)S(1)}, bf16[64,512]{1,0:T(8,128)(2,1)}, u32[]{:S(2)}) copy-start(bf16[64,512]{1,0:T(8,128)(2,1)} %param.14) | copy-start | bytes 196612
  76.4 5.6 %copy-start.6 = (bf16[384,512]{1,0:T(8,128)(2,1)S(1)}, bf16[384,512]{1,0:T(8,128)(2,1)}, u32[]{:S(2)}) copy-start(bf16[384,512]{1,0:T(8,128)(2,1)} %param.13) | copy-start | bytes 1179652
  78.2 13.6 %collective-permute-start.3 = (bf16[208,512]{1,0:T(8,128)(2,1)S(1)}, bf16[208,512]{1,0:T(8,128)(2,1)S(1)}, u32[]{:S(2)}, u32[]{:S(2)}) collective-permute-start(bf16[208,512]{1,0:T(8,128)(2,1)S(1)} %concatenate.21), channel_id=1, source_target_pairs={{0,16},{16,32},{32,48},{48,64},{64,80},{80,96},{96,112},{112,128},... | collective-permute-start | bytes 638984 | tf_op jit(solution)/shard_map/ppermute | solution.py:41
  117.0 4.4 %collective-permute-start.4 = (bf16[8,192,512]{2,1,0:T(8,128)(2,1)}, bf16[8,192,512]{2,1,0:T(8,128)(2,1)}, u32[]{:S(2)}, u32[]{:S(2)}) collective-permute-start(bf16[8,192,512]{2,1,0:T(8,128)(2,1)} %all_to_all.40.x_ref), channel_id=1, source_target_pairs={{0,1},{1,0},{2,3},{3,2},{4,5},{5,4},{6,7},{7,6},{8,9},{9,8},{10,11... | collective-permute-start | bytes 4718600 | tf_op jit(solution)/shard_map/ppermute | solution.py:37
  126.2 1.5 collective-permute-start.5
  157.2 11.2 %collective-permute-start.6 = (bf16[208,512]{1,0:T(8,128)(2,1)S(1)}, bf16[208,512]{1,0:T(8,128)(2,1)S(1)}, u32[]{:S(2)}, u32[]{:S(2)}) collective-permute-start(bf16[208,512]{1,0:T(8,128)(2,1)S(1)} %concatenate.22), channel_id=1, source_target_pairs={{0,16},{16,32},{32,48},{48,64},{64,80},{80,96},{96,112},{112,128},... | collective-permute-start | bytes 638984 | tf_op jit(solution)/shard_map/ppermute | solution.py:41
  192.5 4.4 %collective-permute-start.7 = (bf16[8,192,512]{2,1,0:T(8,128)(2,1)}, bf16[8,192,512]{2,1,0:T(8,128)(2,1)}, u32[]{:S(2)}, u32[]{:S(2)}) collective-permute-start(bf16[8,192,512]{2,1,0:T(8,128)(2,1)} %all_to_all.42.x_ref), channel_id=1, source_target_pairs={{0,1},{1,0},{2,3},{3,2},{4,5},{5,4},{6,7},{7,6},{8,9},{9,8},{10,11... | collective-permute-start | bytes 4718600 | tf_op jit(solution)/shard_map/ppermute | solution.py:37
  201.6 1.8 collective-permute-start.8
  232.9 13.7 %collective-permute-start.9 = (bf16[208,512]{1,0:T(8,128)(2,1)S(1)}, bf16[208,512]{1,0:T(8,128)(2,1)S(1)}, u32[]{:S(2)}, u32[]{:S(2)}) collective-permute-start(bf16[208,512]{1,0:T(8,128)(2,1)S(1)} %concatenate.23), channel_id=1, source_target_pairs={{0,16},{16,32},{32,48},{48,64},{64,80},{80,96},{96,112},{112,128},... | collective-permute-start | bytes 638984 | tf_op jit(solution)/shard_map/ppermute | solution.py:41
  268.6 4.3 %collective-permute-start.10 = (bf16[8,192,512]{2,1,0:T(8,128)(2,1)}, bf16[8,192,512]{2,1,0:T(8,128)(2,1)}, u32[]{:S(2)}, u32[]{:S(2)}) collective-permute-start(bf16[8,192,512]{2,1,0:T(8,128)(2,1)} %all_to_all.44.x_ref), channel_id=1, source_target_pairs={{0,1},{1,0},{2,3},{3,2},{4,5},{5,4},{6,7},{7,6},{8,9},{9,8},{10,11... | collective-permute-start | bytes 4718600 | tf_op jit(solution)/shard_map/ppermute | solution.py:37
  276.6 1.5 collective-permute-start.11

commit v4 on v3

--- a/solution.py
+++ b/solution.py
@@ -64,7 +64,7 @@
     )(core, f)
 
 
-def project_half(write, offset, x_ref, gain_ref, wk_ref, wv_ref, gate_ref, bufs, sems):
+def project_half(write, offset, x_ref, gain_ref, wk_ref, wv_ref, gate_ref, bufs, sems, extra=None):
     x_buf, k_buf, v_buf = bufs
     rows = x_ref.shape[1]
     copies = []
@@ -82,6 +82,8 @@
             copy.start()
             group.append(copy)
         copies.append(group)
+    if extra is not None:
+        extra.start()
     dot = functools.partial(jnp.dot, preferred_element_type=jnp.float32)
     squares, gates, keys, values = 0.0, 0.0, 0.0, 0.0
     for b in range(N_CHIPS):
@@ -119,21 +121,24 @@
 
 
 def read_kernel(
-    write, core_ref, keep_ref, sum_ref, x_ref, gain_ref, wk_ref, wv_ref, gate_ref, a_ref, z_ref,
-    read_ref, *rest,
+    write, core_ref, entered_ref, sum_ref, x_ref, gain_ref, wk_ref, wv_ref, gate_ref, f_ref,
+    a_ref, z_ref, read_ref, f_next, tile_ref, *rest,
 ):
-    *state, x_buf, k_buf, v_buf, sems = rest
+    *state, x_buf, k_buf, v_buf, sems, f_sem = rest
     rows = x_ref.shape[1]
+    f_copy = pltpu.make_async_copy(f_ref, f_next, f_sem.at[0])
     keys, values, squares, gates = project_half(
         write, 1 - core_ref[0], x_ref, gain_ref, wk_ref, wv_ref, gate_ref,
-        (x_buf, k_buf, v_buf), sems,
+        (x_buf, k_buf, v_buf), sems, f_copy,
     )
     keys += sum_ref[:, :WIDE]
     values += sum_ref[:, WIDE : 2 * WIDE]
     side = sum_ref[:, 2 * WIDE :]
     squares += side[:, GATE_ROWS : GATE_ROWS + 1]
     scale = lax.rsqrt(squares * (1.0 / HIDDEN) + EPS)
-    keep = keep_ref[0, 0]
+    tile = entered_ref[pl.ds(PIECE, FLAG_ROWS)]
+    tile_ref[...] = tile
+    keep = 1.0 - tile.astype(jnp.float32)[0:1, :HD]
     for h in range(HEADS):
         a = a_ref[h] * keep
         z = z_ref[h : h + 1] * keep
@@ -156,6 +161,7 @@
                 preferred_element_type=jnp.float32,
             )
             state[1][h : h + 1] = z + jnp.sum(tail, axis=0, keepdims=True)
+    f_copy.wait()
 
 
 def half_scratch(rows):
@@ -179,34 +185,33 @@
     )(core, own, gain, wk, wv, gate)
 
 
-def read_memory(core, keep, begun, got, gain, wk, wv, gate, a, z, write):
+def read_memory(core, entered, begun, got, gain, wk, wv, gate, f, a, z, write):
     rows = got.shape[1]
-    shapes = [jax.ShapeDtypeStruct((rows, WIDE), jnp.bfloat16)]
+    shapes = [
+        jax.ShapeDtypeStruct((rows, WIDE), jnp.bfloat16),
+        jax.ShapeDtypeStruct(f.shape, f.dtype),
+        jax.ShapeDtypeStruct((FLAG_ROWS, BLOCK), jnp.bfloat16),
+    ]
     if write:
         shapes += [jax.ShapeDtypeStruct(a.shape, a.dtype), jax.ShapeDtypeStruct(z.shape, z.dtype)]
     return pl.pallas_call(
         functools.partial(read_kernel, write),
-        in_specs=[SMEM, SMEM, VMEM, ANY, VMEM, ANY, ANY, VMEM, VMEM, VMEM],
+        in_specs=[SMEM, VMEM, VMEM, ANY, VMEM, ANY, ANY, VMEM, ANY, VMEM, VMEM],
         out_specs=[VMEM] * len(shapes),
         out_shape=shapes,
-        scratch_shapes=half_scratch(rows),
+        scratch_shapes=half_scratch(rows) + [pltpu.SemaphoreType.DMA((1,))],
         compiler_params=pltpu.CompilerParams(vmem_limit_bytes=VMEM_LIMIT),
         cost_estimate=pl.CostEstimate(
             flops=rows * HIDDEN * 2 * WIDE, bytes_accessed=6 * 2**20, transcendentals=0
         ),
-    )(core, keep, begun, got, gain, wk, wv, gate, a, z)
-
-
-def output_kernel(near_ref, far_ref, keep_ref, got_ref, p_ref, got_buf, sems):
-    copies = []
-    for b in range(N_CHIPS):
-        copies.append(pltpu.make_async_copy(got_ref.at[b], got_buf.at[b], sems.at[b]))
-        copies[-1].start()
+    )(core, entered, begun, got, gain, wk, wv, gate, f, a, z)
+
+
+def output_kernel(near_ref, far_ref, keep_ref, got_ref, p_ref):
     near, far = near_ref[...], far_ref[...]
     for b in range(N_CHIPS):
         part = jnp.dot(near, keep_ref[b], preferred_element_type=jnp.float32)
-        copies[b].wait()
-        part += jnp.dot(far, got_buf[b], preferred_element_type=jnp.float32)
+        part += jnp.dot(far, got_ref[b], preferred_element_type=jnp.float32)
         p_ref[b] = part.astype(jnp.bfloat16)
 
 
@@ -214,16 +219,12 @@
     rows = near.shape[0]
     return pl.pallas_call(
         output_kernel,
-        in_specs=[VMEM, VMEM, VMEM, ANY],
+        in_specs=[VMEM] * 4,
         out_specs=VMEM,
         out_shape=jax.ShapeDtypeStruct((N_CHIPS, rows, BLOCK), jnp.bfloat16),
-        scratch_shapes=[
-            pltpu.VMEM((N_CHIPS, WIDE, BLOCK), jnp.bfloat16),
-            pltpu.SemaphoreType.DMA((N_CHIPS,)),
-        ],
         compiler_params=pltpu.CompilerParams(vmem_limit_bytes=VMEM_LIMIT),
         cost_estimate=pl.CostEstimate(
-            flops=2 * rows * 2 * WIDE * 4096, bytes_accessed=2 * 2**20, transcendentals=0
+            flops=2 * rows * 2 * WIDE * 4096, bytes_accessed=6 * 2**20, transcendentals=0
         ),
     )(near, far, keep, got)
 
@@ -254,9 +255,10 @@
     section_zero = (lax.axis_index("y_lo") == 0) & (lax.axis_index("z") == 0)
     steps = arriving_pieces.shape[0] // SEG + 1
 
-    x = initial_stack_inputs
-    outgoing, which = lax.optimization_barrier((copies(x), which))
     flag = (initial_sequence_starts[0] > 0).astype(jnp.bfloat16)
+    tile = jnp.broadcast_to(flag, (FLAG_ROWS, BLOCK))
+    entered = jnp.concatenate([initial_stack_inputs, tile], axis=0)
+    outgoing, which = lax.optimization_barrier((copies(initial_stack_inputs), which))
 
     wk = lookup_projection[0].reshape(2 * N_CHIPS, BLOCK, WIDE)
     wv = content_projection[0].reshape(2 * N_CHIPS, BLOCK, WIDE)
@@ -268,27 +270,32 @@
 
     a = associative_stores[0]
     z = denominator_vectors[0]
+    clear = jnp.zeros((FLAG_ROWS, BLOCK), jnp.bfloat16)
+    entering = [
+        jnp.concatenate(
+            [arriving_pieces[t * SEG : (t + 1) * SEG], recall_embeddings, clear], axis=0
+        )
+        for t in range(steps - 1)
+    ]
     for t in range(steps):
         write = t + 1 < steps
         if t > 0:
-            sent = jnp.concatenate([x, jnp.broadcast_to(flag, (FLAG_ROWS, BLOCK))], axis=0)
-            moved = next_section(sent)
-            entering = jnp.concatenate(
-                [arriving_pieces[(t - 1) * SEG : t * SEG], recall_embeddings], axis=0
-            )
-            x = jnp.where(section_zero, entering, moved[:PIECE])
-            flag = jnp.where(section_zero, jnp.zeros((), jnp.bfloat16), moved[PIECE, 0])
-            outgoing = copies(x)
-        keep = (1.0 - flag.astype(jnp.float32)).reshape(1, 1)
+            moved = next_section(jnp.concatenate([x, tile], axis=0))
+            entered = jnp.where(section_zero, entering[t - 1], moved)
+            outgoing = copies(entered[:PIECE])
         own = exchange(outgoing)
         got = swap(own, "core")
         begun = project_first(which, own, gain, wk, wv, gate, write)
-        read, *state = read_memory(which, keep, begun, got, gain, wk, wv, gate, a, z, write)
+        read, f_near, tile, *state = read_memory(
+            which, entered, begun, got, gain, wk, wv, gate, f_got, a, z, write
+        )
         if write:
             a, z = state
-        p = exchange(output(read, swap(read, "core"), f_keep, f_got))
+        if t == 0:
+            read, entering, section_zero = lax.optimization_barrier((read, entering, section_zero))
+        p = exchange(output(read, swap(read, "core"), f_keep, f_near))
         total = jnp.sum(p.astype(jnp.float32), axis=0)
-        x = (x.astype(jnp.float32) + total).astype(jnp.bfloat16)
+        x = (entered[:PIECE].astype(jnp.float32) + total).astype(jnp.bfloat16)
     return x
 
 

time: 309 us -> 293 us (0.948)
  waiting for transfers between devices: 77.3 us -> 51.9 us
  blocking collectives: 149 us -> 173 us
  starting transfers between devices: 20.6 us -> 16.2 us
  Pallas kernels: 49.9 us -> 45.7 us
    all_to_all x2 -> x1, waiting for transfers between devices: 42.8 us -> 17.6 us  [exchange(): return lax.all_to_all(blocks, CHIPS, 0, 0, tiled=True)]
    all_to_all x6 -> x7, blocking collectives: 149 us -> 173 us  [exchange(): return lax.all_to_all(blocks, CHIPS, 0, 0, tiled=True)]
    pallas_call x8, Pallas kernels: 30.8 us -> 24.4 us  [the longest x4 20.5 us: read_memory(): pl.pallas_call(functools.partial(read_kernel, write), in_specs=[SMEM, VME...]
    all_to_all x2 -> x1, starting transfers between devices: 10.3 us -> 6.03 us  [exchange(): return lax.all_to_all(blocks, CHIPS, 0, 0, tiled=True)]
  transfers between devices with their start and end apart: 14 -> 13, of which waited for: 9 -> 8; matrix products, arithmetic and copies ran while one was open for 1% -> 0% of each run, Pallas kernels for 8% -> 7%
where the time goes in v4:
time: 293 us; the launch traced here: 292 us
  blocking collectives  173 us (59%)
  waiting for transfers between devices  51.9 us (18%)
  Pallas kernels  45.7 us (16%)
  starting transfers between devices  16.2 us (6%)
    all_to_all x7, blocking collectives, exchange(): return lax.all_to_all(blocks, CHIPS, 0, 0, tiled=True)  173 us
    ppermute x3, waiting for transfers between devices, next_section(): return lax.ppermute(value, SECTION, [(i, i + 1) for i in range(15)])  30.6 us
    pallas_call x4, Pallas kernels, read_memory(): pl.pallas_call(functools.partial(read_kernel, write), in_specs=[SMEM, VME...  20.5 us
    all_to_all x1, waiting for transfers between devices, exchange(): return lax.all_to_all(blocks, CHIPS, 0, 0, tiled=True)  17.6 us
    pallas_call x4, Pallas kernels, project_first(): pl.pallas_call(functools.partial(first_kernel, write), in_specs=[SMEM, AN...  15 us
    ppermute x3, starting transfers between devices, next_section(): return lax.ppermute(value, SECTION, [(i, i + 1) for i in range(15)])  7.65 us
    pallas_call x1, Pallas kernels, pick(): pl.pallas_call(pick_kernel, grid=(N_CHIPS,), in_specs=[SMEM, pl.BlockSpec...  6.21 us
    all_to_all x1, starting transfers between devices, exchange(): return lax.all_to_all(blocks, CHIPS, 0, 0, tiled=True)  6.03 us
  transfers between devices with their start and end apart: 13, of which 8 were waited for; matrix products, arithmetic and copies ran while one was open for 0% of the time, Pallas kernels for 7%

profile of v4, /device:TPU:8, one launch (start us, length us, event | category | flops | bytes accessed | tf_op | source)
XLA Modules:
  0.0 292.5 jit_solution(12563386347493374961)
XLA Ops:
  0.0 2.2 broadcast_in_dim.10
  2.2 6.0 %all-to-all-start = ((bf16[8,192,512]{2,1,0:T(8,128)(2,1)}), bf16[8,192,512]{2,1,0:T(8,128)(2,1)}, u32[]{:S(2)}, u32[]{:S(2)}) async-start(bf16[8,192,512]{2,1,0:T(8,128)(2,1)} %broadcast_in_dim.10), calls=%async_computation | async-start | bytes 3145728 | tf_op jit(solution)/shard_map/all_to_all | solution.py:237
  8.3 6.2 %shard_map.110 = (bf16[8,256,512]{2,1,0:T(8,128)(2,1)S(1)}, bf16[8,256,512]{2,1,0:T(8,128)(2,1)}) custom-call(s32[1]{0:T(128)} %bitcast.core_ref, bf16[256,8192]{1,0:T(8,128)(2,1)} %bitcast.41), custom_call_target="tpu_custom_call" | custom-call | tf_op jit(solution)/shard_map/pallas_call | solution.py:56
  14.5 17.6 %all-to-all-done.x_ref = bf16[8,192,512]{2,1,0:T(8,128)(2,1)} async-done(((bf16[8,192,512]{2,1,0:T(8,128)(2,1)}), bf16[8,192,512]{2,1,0:T(8,128)(2,1)}, u32[]{:S(2)}, u32[]{:S(2)}) %all-to-all-start) | async-done | bytes 1572896 | tf_op jit(solution)/shard_map/all_to_all | solution.py:237
  32.8 0.1 pad.20.clone
  33.0 0.2 fusion.2
  33.1 0.0 copy-start.1
  33.1 3.3 %shard_map.109.sum_ref = f32[192,640]{1,0:T(8,128)S(1)} custom-call(s32[1]{0:T(128)} %bitcast.core_ref, bf16[8,192,512]{2,1,0:T(8,128)(2,1)} %all-to-all-done.x_ref, f32[16,1,512]{2,1,0:T(1,128)S(1)} %bitcast.15, bf16[16,512,256]{2,1,0:T(8,128)(2,1)} %bitcast.25, bf16[16,512,256]{2,1,0:T(8,128)(2,1)} %bitcast.33, bf16[16,16,512]{2,1,0:T(8,128)(2,1)S(1)} %pad.5.gate_ref), custom_call_target="tpu_custom_call" | custom-call | flops 805306368 | bytes 6291456 | tf_op jit(solution)/shard_map/pallas_call | solution.py:175
  36.5 4.7 %shard_map.111 = (bf16[192,256]{1,0:T(8,128)(2,1)S(1)}, bf16[8,256,512]{2,1,0:T(8,128)(2,1)S(1)}, bf16[16,512]{1,0:T(8,128)(2,1)S(1)}, f32[2,128,128]{2,1,0:T(8,128)S(1)}, f32[2,128]{1,0:T(2,128)S(1)}) custom-call(s32[1]{0:T(128)} %bitcast.core_ref, bf16[208,512]{1,0:T(8,128)(2,1)S(1)} %concatenate.21.entered_ref, f32[192,640]{1,0:T(8,128)S(1)} %shard_map.109.sum_ref, ...), custom_call_target="tpu_custom_call" | custom-call | flops 805306368 | bytes 6291456 | tf_op jit(solution)/shard_map/pallas_call | solution.py:197
  41.2 0.6 collective-permute-start.2
  41.8 0.9 collective-permute-done.2.far_ref
  42.7 1.0 shard_map.112
  43.7 25.7 %all_to_all.40 = bf16[8,192,512]{2,1,0:T(8,128)(2,1)S(1)} all-to-all(bf16[8,192,512]{2,1,0:T(8,128)(2,1)S(1)} %shard_map.112), channel_id=1, replica_groups=mesh['y_lo'=2,'z'=8,'x'=4,'y_hi'=2,'core'=2] {'x','y_hi'}, dimensions={0} | all-to-all | bytes 3145728 | tf_op jit(solution)/shard_map/all_to_all | solution.py:237
  69.4 0.2 convert_reduce_fusion.3
  69.7 3.8 %collective-permute-start.3 = (bf16[208,512]{1,0:T(8,128)(2,1)S(1)}, bf16[208,512]{1,0:T(8,128)(2,1)S(1)}, u32[]{:S(2)}, u32[]{:S(2)}) collective-permute-start(bf16[208,512]{1,0:T(8,128)(2,1)S(1)} %pad_maximum_fusion.3), channel_id=1, source_target_pairs={{0,16},{16,32},{32,48},{48,64},{64,80},{80,96},{96,112},{112,128},... | collective-permute-start | bytes 638984 | tf_op jit(solution)/shard_map/ppermute | solution.py:41
  73.5 9.8 %collective-permute-done.3 = bf16[208,512]{1,0:T(8,128)(2,1)S(1)} collective-permute-done((bf16[208,512]{1,0:T(8,128)(2,1)S(1)}, bf16[208,512]{1,0:T(8,128)(2,1)S(1)}, u32[]{:S(2)}, u32[]{:S(2)}) %collective-permute-start.3) | collective-permute-done | bytes 213024 | tf_op jit(solution)/shard_map/ppermute | solution.py:41
  83.4 0.1 broadcast_in_dim.12
  83.6 23.8 %all_to_all.41.x_ref = bf16[8,192,512]{2,1,0:T(8,128)(2,1)S(1)} all-to-all(bf16[8,192,512]{2,1,0:T(8,128)(2,1)S(1)} %broadcast_in_dim.12), channel_id=1, replica_groups=mesh['y_lo'=2,'z'=8,'x'=4,'y_hi'=2,'core'=2] {'x','y_hi'}, dimensions={0} | all-to-all | bytes 3145728 | tf_op jit(solution)/shard_map/all_to_all | solution.py:237
  107.3 4.0 %shard_map.113.sum_ref = f32[192,640]{1,0:T(8,128)S(1)} custom-call(s32[1]{0:T(128)} %bitcast.core_ref, bf16[8,192,512]{2,1,0:T(8,128)(2,1)S(1)} %all_to_all.41.x_ref, f32[16,1,512]{2,1,0:T(1,128)S(1)} %bitcast.17, bf16[16,512,256]{2,1,0:T(8,128)(2,1)} %bitcast.27, bf16[16,512,256]{2,1,0:T(8,128)(2,1)} %bitcast.35, bf16[16,16,512]{2,1,0:T(8,128)(2,1)S(1)} %pad.5.gate_ref), custom_call_target="tpu_custom_call" | custom-call | flops 805306368 | bytes 6291456 | tf_op jit(solution)/shard_map/pallas_call | solution.py:175
  111.4 5.5 %shard_map.114 = (bf16[192,256]{1,0:T(8,128)(2,1)S(1)}, bf16[8,256,512]{2,1,0:T(8,128)(2,1)S(1)}, bf16[16,512]{1,0:T(8,128)(2,1)S(1)}, f32[2,128,128]{2,1,0:T(8,128)S(1)}, f32[2,128]{1,0:T(2,128)S(1)}) custom-call(s32[1]{0:T(128)} %bitcast.core_ref, bf16[208,512]{1,0:T(8,128)(2,1)S(1)} %broadcast_select_fusion.2.entered_ref, ...), custom_call_target="tpu_custom_call" | custom-call | flops 805306368 | bytes 6291456 | tf_op jit(solution)/shard_map/pallas_call | solution.py:197
  116.9 0.8 collective-permute-start.5
  117.6 0.9 collective-permute-done.5.far_ref
  118.6 1.0 shard_map.115
  119.6 25.9 %all_to_all.42 = bf16[8,192,512]{2,1,0:T(8,128)(2,1)S(1)} all-to-all(bf16[8,192,512]{2,1,0:T(8,128)(2,1)S(1)} %shard_map.115), channel_id=1, replica_groups=mesh['y_lo'=2,'z'=8,'x'=4,'y_hi'=2,'core'=2] {'x','y_hi'}, dimensions={0} | all-to-all | bytes 3145728 | tf_op jit(solution)/shard_map/all_to_all | solution.py:237
  145.5 0.2 convert_reduce_fusion.2
  145.7 1.9 collective-permute-start.6
  147.7 9.1 %collective-permute-done.6 = bf16[208,512]{1,0:T(8,128)(2,1)S(1)} collective-permute-done((bf16[208,512]{1,0:T(8,128)(2,1)S(1)}, bf16[208,512]{1,0:T(8,128)(2,1)S(1)}, u32[]{:S(2)}, u32[]{:S(2)}) %collective-permute-start.6) | collective-permute-done | bytes 213024 | tf_op jit(solution)/shard_map/ppermute | solution.py:41
  156.9 0.1 broadcast_in_dim.13
  157.0 23.9 %all_to_all.43.x_ref = bf16[8,192,512]{2,1,0:T(8,128)(2,1)S(1)} all-to-all(bf16[8,192,512]{2,1,0:T(8,128)(2,1)S(1)} %broadcast_in_dim.13), channel_id=1, replica_groups=mesh['y_lo'=2,'z'=8,'x'=4,'y_hi'=2,'core'=2] {'x','y_hi'}, dimensions={0} | all-to-all | bytes 3145728 | tf_op jit(solution)/shard_map/all_to_all | solution.py:237
  180.9 4.0 %shard_map.116.sum_ref = f32[192,640]{1,0:T(8,128)S(1)} custom-call(s32[1]{0:T(128)} %bitcast.core_ref, bf16[8,192,512]{2,1,0:T(8,128)(2,1)S(1)} %all_to_all.43.x_ref, f32[16,1,512]{2,1,0:T(1,128)S(1)} %bitcast.19, bf16[16,512,256]{2,1,0:T(8,128)(2,1)} %bitcast.29, bf16[16,512,256]{2,1,0:T(8,128)(2,1)} %bitcast.37, bf16[16,16,512]{2,1,0:T(8,128)(2,1)S(1)} %pad.5.gate_ref), custom_call_target="tpu_custom_call" | custom-call | flops 805306368 | bytes 6291456 | tf_op jit(solution)/shard_map/pallas_call | solution.py:175
  184.9 5.5 %shard_map.117 = (bf16[192,256]{1,0:T(8,128)(2,1)S(1)}, bf16[8,256,512]{2,1,0:T(8,128)(2,1)S(1)}, bf16[16,512]{1,0:T(8,128)(2,1)S(1)}, f32[2,128,128]{2,1,0:T(8,128)S(1)}, f32[2,128]{1,0:T(2,128)S(1)}) custom-call(s32[1]{0:T(128)} %bitcast.core_ref, bf16[208,512]{1,0:T(8,128)(2,1)S(1)} %broadcast_select_fusion.1.entered_ref, ...), custom_call_target="tpu_custom_call" | custom-call | flops 805306368 | bytes 6291456 | tf_op jit(solution)/shard_map/pallas_call | solution.py:197
  190.5 0.6 collective-permute-start.8
  191.1 0.9 collective-permute-done.8.far_ref
  192.0 1.0 shard_map.118
  193.0 25.9 %all_to_all.44 = bf16[8,192,512]{2,1,0:T(8,128)(2,1)S(1)} all-to-all(bf16[8,192,512]{2,1,0:T(8,128)(2,1)S(1)} %shard_map.118), channel_id=1, replica_groups=mesh['y_lo'=2,'z'=8,'x'=4,'y_hi'=2,'core'=2] {'x','y_hi'}, dimensions={0} | all-to-all | bytes 3145728 | tf_op jit(solution)/shard_map/all_to_all | solution.py:237
  218.9 0.2 convert_reduce_fusion.1
  219.2 1.9 collective-permute-start.9
  221.1 11.6 %collective-permute-done.9 = bf16[208,512]{1,0:T(8,128)(2,1)S(1)} collective-permute-done((bf16[208,512]{1,0:T(8,128)(2,1)S(1)}, bf16[208,512]{1,0:T(8,128)(2,1)S(1)}, u32[]{:S(2)}, u32[]{:S(2)}) %collective-permute-start.9) | collective-permute-done | bytes 213024 | tf_op jit(solution)/shard_map/ppermute | solution.py:41
  232.7 0.1 broadcast_in_dim.14
  232.9 21.7 %all_to_all.45.x_ref = bf16[8,192,512]{2,1,0:T(8,128)(2,1)S(1)} all-to-all(bf16[8,192,512]{2,1,0:T(8,128)(2,1)S(1)} %broadcast_in_dim.14), channel_id=1, replica_groups=mesh['y_lo'=2,'z'=8,'x'=4,'y_hi'=2,'core'=2] {'x','y_hi'}, dimensions={0} | all-to-all | bytes 3145728 | tf_op jit(solution)/shard_map/all_to_all | solution.py:237
  254.6 3.7 %shard_map.119.sum_ref = f32[192,640]{1,0:T(8,128)S(1)} custom-call(s32[1]{0:T(128)} %bitcast.core_ref, bf16[8,192,512]{2,1,0:T(8,128)(2,1)S(1)} %all_to_all.45.x_ref, f32[16,1,512]{2,1,0:T(1,128)S(1)} %bitcast.21, bf16[16,512,256]{2,1,0:T(8,128)(2,1)} %bitcast.31, bf16[16,512,256]{2,1,0:T(8,128)(2,1)} %bitcast.39, bf16[16,16,512]{2,1,0:T(8,128)(2,1)S(1)} %pad.5.gate_ref), custom_call_target="tpu_custom_call" | custom-call | flops 805306368 | bytes 6291456 | tf_op jit(solution)/shard_map/pallas_call | solution.py:175
  258.3 4.8 %shard_map.120 = (bf16[192,256]{1,0:T(8,128)(2,1)S(1)}, bf16[8,256,512]{2,1,0:T(8,128)(2,1)S(1)}, bf16[16,512]{1,0:T(8,128)(2,1)}) custom-call(s32[1]{0:T(128)} %bitcast.core_ref, bf16[208,512]{1,0:T(8,128)(2,1)S(1)} %broadcast_select_fusion.entered_ref, f32[192,640]{1,0:T(8,128)S(1)} %shard_map.119.sum_ref, ...), custom_call_target="tpu_custom_call" | custom-call | flops 805306368 | bytes 6291456 | tf_op jit(solution)/shard_map/pallas_call | solution.py:197
  263.1 0.6 collective-permute-start.11
  263.7 0.9 collective-permute-done.11.far_ref
  264.6 1.0 shard_map.121
  265.6 25.9 %all_to_all.46 = bf16[8,192,512]{2,1,0:T(8,128)(2,1)S(1)} all-to-all(bf16[8,192,512]{2,1,0:T(8,128)(2,1)S(1)} %shard_map.121), channel_id=1, replica_groups=mesh['y_lo'=2,'z'=8,'x'=4,'y_hi'=2,'core'=2] {'x','y_hi'}, dimensions={0} | all-to-all | bytes 3145728 | tf_op jit(solution)/shard_map/all_to_all | solution.py:237
  291.5 0.2 convert_reduce_fusion
  291.7 0.7 add_convert_fusion
  (39 shorter events, 0.4 us)
Async XLA Ops:
  2.2 29.8 %all-to-all-start = ((bf16[8,192,512]{2,1,0:T(8,128)(2,1)}), bf16[8,192,512]{2,1,0:T(8,128)(2,1)}, u32[]{:S(2)}, u32[]{:S(2)}) async-start(bf16[8,192,512]{2,1,0:T(8,128)(2,1)} %broadcast_in_dim.10), calls=%async_computation | async-start | bytes 3145728 | tf_op jit(solution)/shard_map/all_to_all | solution.py:237
  8.3 24.5 %copy-start.3 = (bf16[192,512]{1,0:T(8,128)(2,1)S(1)}, bf16[192,512]{1,0:T(8,128)(2,1)}, u32[]{:S(2)}) copy-start(bf16[192,512]{1,0:T(8,128)(2,1)} %param.11) | copy-start | bytes 589828
  8.3 24.5 %copy-start.6 = (bf16[1,8192,2]{1,2,0:T(2,128)(2,1)S(1)}, bf16[1,8192,2]{1,2,0:T(2,128)(2,1)}, u32[]{:S(2)}) copy-start(bf16[1,8192,2]{1,2,0:T(2,128)(2,1)} %param.18) | copy-start | bytes 98308
  8.3 24.6 %copy-start.4 = (bf16[384,512]{1,0:T(8,128)(2,1)S(1)}, bf16[384,512]{1,0:T(8,128)(2,1)}, u32[]{:S(2)}) copy-start(bf16[384,512]{1,0:T(8,128)(2,1)} %param.13) | copy-start | bytes 1179652
  14.5 18.5 %copy-start.5 = (bf16[64,512]{1,0:T(8,128)(2,1)S(1)}, bf16[64,512]{1,0:T(8,128)(2,1)}, u32[]{:S(2)}) copy-start(bf16[64,512]{1,0:T(8,128)(2,1)} %param.14) | copy-start | bytes 196612
  14.5 18.6 %copy-start = (f32[1,8192]{1,0:T(1,128)S(1)}, f32[1,8192]{1,0:T(1,128)}, u32[]{:S(2)}) copy-start(f32[1,8192]{1,0:T(1,128)} %param.15) | copy-start | bytes 98308
  14.5 21.9 %collective-permute-start.1 = (bf16[8,256,512]{2,1,0:T(8,128)(2,1)}, bf16[8,256,512]{2,1,0:T(8,128)(2,1)}, u32[]{:S(2)}, u32[]{:S(2)}) collective-permute-start(bf16[8,256,512]{2,1,0:T(8,128)(2,1)} %get-tuple-element.33), channel_id=1, source_target_pairs={{0,1},{1,0},{2,3},{3,2},{4,5},{5,4},{6,7},{7,6},{8,9},{9,8},{10,11... | collective-permute-start | bytes 6291464 | tf_op jit(solution)/shard_map/ppermute | solution.py:37
  32.1 4.4 %collective-permute-start = (bf16[8,192,512]{2,1,0:T(8,128)(2,1)}, bf16[8,192,512]{2,1,0:T(8,128)(2,1)}, u32[]{:S(2)}, u32[]{:S(2)}) collective-permute-start(bf16[8,192,512]{2,1,0:T(8,128)(2,1)} %all-to-all-done.x_ref), channel_id=1, source_target_pairs={{0,1},{1,0},{2,3},{3,2},{4,5},{5,4},{6,7},{7,6},{8,9},{9,8},{10,11... | collective-permute-start | bytes 4718600 | tf_op jit(solution)/shard_map/ppermute | solution.py:37
  33.1 3.3 %copy-start.1 = (f32[1,2,128,128]{3,2,1,0:T(8,128)S(1)}, f32[1,2,128,128]{3,2,1,0:T(8,128)}, u32[]{:S(2)}) copy-start(f32[1,2,128,128]{3,2,1,0:T(8,128)} %param.20) | copy-start | bytes 393220
  33.1 3.3 %copy-start.2 = (f32[1,2,128]{2,1,0:T(2,128)S(1)}, f32[1,2,128]{2,1,0:T(2,128)}, u32[]{:S(2)}) copy-start(f32[1,2,128]{2,1,0:T(2,128)} %param.21) | copy-start | bytes 3076
  41.2 1.6 collective-permute-start.2
  69.7 13.6 %collective-permute-start.3 = (bf16[208,512]{1,0:T(8,128)(2,1)S(1)}, bf16[208,512]{1,0:T(8,128)(2,1)S(1)}, u32[]{:S(2)}, u32[]{:S(2)}) collective-permute-start(bf16[208,512]{1,0:T(8,128)(2,1)S(1)} %pad_maximum_fusion.3), channel_id=1, source_target_pairs={{0,16},{16,32},{32,48},{48,64},{64,80},{80,96},{96,112},{112,128},... | collective-permute-start | bytes 638984 | tf_op jit(solution)/shard_map/ppermute | solution.py:41
  107.3 4.0 %collective-permute-start.4 = (bf16[8,192,512]{2,1,0:T(8,128)(2,1)S(1)}, bf16[8,192,512]{2,1,0:T(8,128)(2,1)S(1)}, u32[]{:S(2)}, u32[]{:S(2)}) collective-permute-start(bf16[8,192,512]{2,1,0:T(8,128)(2,1)S(1)} %all_to_all.41.x_ref), channel_id=1, source_target_pairs={{0,1},{1,0},{2,3},{3,2},{4,5},{5,4},{6,7},{7,6},{8,9},{9,8},{10,11... | collective-permute-start | bytes 4718600 | tf_op jit(solution)/shard_map/ppermute | solution.py:37
  116.9 1.7 collective-permute-start.5
  145.7 11.1 %collective-permute-start.6 = (bf16[208,512]{1,0:T(8,128)(2,1)S(1)}, bf16[208,512]{1,0:T(8,128)(2,1)S(1)}, u32[]{:S(2)}, u32[]{:S(2)}) collective-permute-start(bf16[208,512]{1,0:T(8,128)(2,1)S(1)} %pad_maximum_fusion.4), channel_id=1, source_target_pairs={{0,16},{16,32},{32,48},{48,64},{64,80},{80,96},{96,112},{112,128},... | collective-permute-start | bytes 638984 | tf_op jit(solution)/shard_map/ppermute | solution.py:41
  180.9 4.0 %collective-permute-start.7 = (bf16[8,192,512]{2,1,0:T(8,128)(2,1)S(1)}, bf16[8,192,512]{2,1,0:T(8,128)(2,1)S(1)}, u32[]{:S(2)}, u32[]{:S(2)}) collective-permute-start(bf16[8,192,512]{2,1,0:T(8,128)(2,1)S(1)} %all_to_all.43.x_ref), channel_id=1, source_target_pairs={{0,1},{1,0},{2,3},{3,2},{4,5},{5,4},{6,7},{7,6},{8,9},{9,8},{10,11... | collective-permute-start | bytes 4718600 | tf_op jit(solution)/shard_map/ppermute | solution.py:37
  190.5 1.5 collective-permute-start.8
  219.2 13.5 %collective-permute-start.9 = (bf16[208,512]{1,0:T(8,128)(2,1)S(1)}, bf16[208,512]{1,0:T(8,128)(2,1)S(1)}, u32[]{:S(2)}, u32[]{:S(2)}) collective-permute-start(bf16[208,512]{1,0:T(8,128)(2,1)S(1)} %pad_maximum_fusion.5), channel_id=1, source_target_pairs={{0,16},{16,32},{32,48},{48,64},{64,80},{80,96},{96,112},{112,128},... | collective-permute-start | bytes 638984 | tf_op jit(solution)/shard_map/ppermute | solution.py:41
  254.6 3.7 %collective-permute-start.10 = (bf16[8,192,512]{2,1,0:T(8,128)(2,1)S(1)}, bf16[8,192,512]{2,1,0:T(8,128)(2,1)S(1)}, u32[]{:S(2)}, u32[]{:S(2)}) collective-permute-start(bf16[8,192,512]{2,1,0:T(8,128)(2,1)S(1)} %all_to_all.45.x_ref), channel_id=1, source_target_pairs={{0,1},{1,0},{2,3},{3,2},{4,5},{5,4},{6,7},{7,6},{8,9},{9,8},{10,11... | collective-permute-start | bytes 4718600 | tf_op jit(solution)/shard_map/ppermute | solution.py:37
  263.1 1.5 collective-permute-start.11

commit v5 on v4

--- a/solution.py
+++ b/solution.py
@@ -65,7 +65,7 @@
 
 
 def project_half(write, offset, x_ref, gain_ref, wk_ref, wv_ref, gate_ref, bufs, sems, extra=None):
-    x_buf, k_buf, v_buf = bufs
+    k_buf, v_buf = bufs
     rows = x_ref.shape[1]
     copies = []
     for b in range(N_CHIPS):
@@ -73,7 +73,6 @@
         group = []
         for i, (source, target) in enumerate(
             (
-                (x_ref.at[b], x_buf.at[b]),
                 (wk_ref.at[place], k_buf.at[b]),
                 (wv_ref.at[place], v_buf.at[b]),
             )
@@ -90,7 +89,7 @@
         place = 2 * b + offset
         for copy in copies[b]:
             copy.wait()
-        wide = x_buf[b].astype(jnp.float32)
+        wide = x_ref[b].astype(jnp.float32)
         squares += wide * wide
         scaled = (wide * gain_ref[place]).astype(jnp.bfloat16)
         keys += dot(scaled, k_buf[b])
@@ -124,12 +123,12 @@
     write, core_ref, entered_ref, sum_ref, x_ref, gain_ref, wk_ref, wv_ref, gate_ref, f_ref,
     a_ref, z_ref, read_ref, f_next, tile_ref, *rest,
 ):
-    *state, x_buf, k_buf, v_buf, sems, f_sem = rest
+    *state, k_buf, v_buf, sems, f_sem = rest
     rows = x_ref.shape[1]
     f_copy = pltpu.make_async_copy(f_ref, f_next, f_sem.at[0])
     keys, values, squares, gates = project_half(
         write, 1 - core_ref[0], x_ref, gain_ref, wk_ref, wv_ref, gate_ref,
-        (x_buf, k_buf, v_buf), sems, f_copy,
+        (k_buf, v_buf), sems, f_copy,
     )
     keys += sum_ref[:, :WIDE]
     values += sum_ref[:, WIDE : 2 * WIDE]
@@ -164,20 +163,19 @@
     f_copy.wait()
 
 
-def half_scratch(rows):
+def half_scratch():
     weights = pltpu.VMEM((N_CHIPS, BLOCK, WIDE), jnp.bfloat16)
-    x = pltpu.VMEM((N_CHIPS, rows, BLOCK), jnp.bfloat16)
-    return [x, weights, weights, pltpu.SemaphoreType.DMA((3, N_CHIPS))]
+    return [weights, weights, pltpu.SemaphoreType.DMA((2, N_CHIPS))]
 
 
 def project_first(core, own, gain, wk, wv, gate, write):
     rows = own.shape[1]
     return pl.pallas_call(
         functools.partial(first_kernel, write),
-        in_specs=[SMEM, ANY, VMEM, ANY, ANY, VMEM],
+        in_specs=[SMEM, VMEM, VMEM, ANY, ANY, VMEM],
         out_specs=VMEM,
         out_shape=jax.ShapeDtypeStruct((rows, 2 * WIDE + SIDE), jnp.float32),
-        scratch_shapes=half_scratch(rows),
+        scratch_shapes=half_scratch(),
         compiler_params=pltpu.CompilerParams(vmem_limit_bytes=VMEM_LIMIT),
         cost_estimate=pl.CostEstimate(
             flops=rows * HIDDEN * 2 * WIDE, bytes_accessed=6 * 2**20, transcendentals=0
@@ -196,10 +194,10 @@
         shapes += [jax.ShapeDtypeStruct(a.shape, a.dtype), jax.ShapeDtypeStruct(z.shape, z.dtype)]
     return pl.pallas_call(
         functools.partial(read_kernel, write),
-        in_specs=[SMEM, VMEM, VMEM, ANY, VMEM, ANY, ANY, VMEM, ANY, VMEM, VMEM],
+        in_specs=[SMEM, VMEM, VMEM, VMEM, VMEM, ANY, ANY, VMEM, ANY, VMEM, VMEM],
         out_specs=[VMEM] * len(shapes),
         out_shape=shapes,
-        scratch_shapes=half_scratch(rows) + [pltpu.SemaphoreType.DMA((1,))],
+        scratch_shapes=half_scratch() + [pltpu.SemaphoreType.DMA((1,))],
         compiler_params=pltpu.CompilerParams(vmem_limit_bytes=VMEM_LIMIT),
         cost_estimate=pl.CostEstimate(
             flops=rows * HIDDEN * 2 * WIDE, bytes_accessed=6 * 2**20, transcendentals=0

time: 293 us -> 290 us (0.990)
  Pallas kernels: 45.7 us -> 41.8 us
  transfers between devices with their start and end apart: 13 -> 13, of which waited for: 8 -> 11; matrix products, arithmetic and copies ran while one was open for 0% -> 0% of each run, Pallas kernels for 7% -> 7%
where the time goes in v5:
time: 290 us
  blocking collectives  175 us (60%)
  waiting for transfers between devices  51.8 us (18%)
  Pallas kernels  41.8 us (14%)
  starting transfers between devices  15.2 us (5%)
    all_to_all x7, blocking collectives, exchange(): return lax.all_to_all(blocks, CHIPS, 0, 0, tiled=True)  175 us
    ppermute x3, waiting for transfers between devices, next_section(): return lax.ppermute(value, SECTION, [(i, i + 1) for i in range(15)])  28.3 us
    pallas_call x4, Pallas kernels, read_memory(): pl.pallas_call(functools.partial(read_kernel, write), in_specs=[SMEM, VME...  18.6 us
    all_to_all x1, waiting for transfers between devices, exchange(): return lax.all_to_all(blocks, CHIPS, 0, 0, tiled=True)  17.6 us
    pallas_call x4, Pallas kernels, project_first(): pl.pallas_call(functools.partial(first_kernel, write), in_specs=[SMEM, VM...  13.1 us
    ppermute x3, starting transfers between devices, next_section(): return lax.ppermute(value, SECTION, [(i, i + 1) for i in range(15)])  7.67 us
    pallas_call x1, Pallas kernels, pick(): pl.pallas_call(pick_kernel, grid=(N_CHIPS,), in_specs=[SMEM, pl.BlockSpec...  6.21 us
    all_to_all x1, starting transfers between devices, exchange(): return lax.all_to_all(blocks, CHIPS, 0, 0, tiled=True)  6.03 us
  transfers between devices with their start and end apart: 13, of which 11 were waited for; matrix products, arithmetic and copies ran while one was open for 0% of the time, Pallas kernels for 7%

profile of v5, /device:TPU:8, one launch (start us, length us, event | category | flops | bytes accessed | tf_op | source)
XLA Modules:
  0.0 289.6 jit_solution(11576733463366181744)
XLA Ops:
  0.0 2.2 broadcast_in_dim.10
  2.2 6.0 %all-to-all-start = ((bf16[8,192,512]{2,1,0:T(8,128)(2,1)}), bf16[8,192,512]{2,1,0:T(8,128)(2,1)}, u32[]{:S(2)}, u32[]{:S(2)}) async-start(bf16[8,192,512]{2,1,0:T(8,128)(2,1)} %broadcast_in_dim.10), calls=%async_computation | async-start | bytes 3145728 | tf_op jit(solution)/shard_map/all_to_all | solution.py:235
  8.3 6.2 %shard_map.110 = (bf16[8,256,512]{2,1,0:T(8,128)(2,1)S(1)}, bf16[8,256,512]{2,1,0:T(8,128)(2,1)}) custom-call(s32[1]{0:T(128)} %bitcast.core_ref, bf16[256,8192]{1,0:T(8,128)(2,1)} %bitcast.41), custom_call_target="tpu_custom_call" | custom-call | tf_op jit(solution)/shard_map/pallas_call | solution.py:56
  14.5 17.6 %all-to-all-done.x_ref = bf16[8,192,512]{2,1,0:T(8,128)(2,1)} async-done(((bf16[8,192,512]{2,1,0:T(8,128)(2,1)}), bf16[8,192,512]{2,1,0:T(8,128)(2,1)}, u32[]{:S(2)}, u32[]{:S(2)}) %all-to-all-start) | async-done | bytes 1572896 | tf_op jit(solution)/shard_map/all_to_all | solution.py:235
  33.0 0.2 fusion.2
  33.1 4.4 %shard_map.109.sum_ref = f32[192,640]{1,0:T(8,128)S(1)} custom-call(s32[1]{0:T(128)} %bitcast.core_ref, bf16[8,192,512]{2,1,0:T(8,128)(2,1)} %all-to-all-done.x_ref, f32[16,1,512]{2,1,0:T(1,128)S(1)} %bitcast.15, bf16[16,512,256]{2,1,0:T(8,128)(2,1)} %bitcast.25, bf16[16,512,256]{2,1,0:T(8,128)(2,1)} %bitcast.33, bf16[16,16,512]{2,1,0:T(8,128)(2,1)S(1)} %pad.5.gate_ref), custom_call_target="tpu_custom_call" | custom-call | flops 805306368 | bytes 6291456 | tf_op jit(solution)/shard_map/pallas_call | solution.py:173
  37.6 5.9 %shard_map.111 = (bf16[192,256]{1,0:T(8,128)(2,1)S(1)}, bf16[8,256,512]{2,1,0:T(8,128)(2,1)S(1)}, bf16[16,512]{1,0:T(8,128)(2,1)S(1)}, f32[2,128,128]{2,1,0:T(8,128)S(1)}, f32[2,128]{1,0:T(2,128)S(1)}) custom-call(s32[1]{0:T(128)} %bitcast.core_ref, bf16[208,512]{1,0:T(8,128)(2,1)S(1)} %concatenate.21.entered_ref, f32[192,640]{1,0:T(8,128)S(1)} %shard_map.109.sum_ref, ...), custom_call_target="tpu_custom_call" | custom-call | flops 805306368 | bytes 6291456 | tf_op jit(solution)/shard_map/pallas_call | solution.py:195
  43.5 0.6 collective-permute-start.2
  44.1 0.9 collective-permute-done.2.far_ref
  45.0 1.0 shard_map.112
  46.0 25.7 %all_to_all.40 = bf16[8,192,512]{2,1,0:T(8,128)(2,1)S(1)} all-to-all(bf16[8,192,512]{2,1,0:T(8,128)(2,1)S(1)} %shard_map.112), channel_id=1, replica_groups=mesh['y_lo'=2,'z'=8,'x'=4,'y_hi'=2,'core'=2] {'x','y_hi'}, dimensions={0} | all-to-all | bytes 3145728 | tf_op jit(solution)/shard_map/all_to_all | solution.py:235
  71.7 0.2 convert_reduce_fusion.3
  72.0 3.8 %collective-permute-start.3 = (bf16[208,512]{1,0:T(8,128)(2,1)S(1)}, bf16[208,512]{1,0:T(8,128)(2,1)S(1)}, u32[]{:S(2)}, u32[]{:S(2)}) collective-permute-start(bf16[208,512]{1,0:T(8,128)(2,1)S(1)} %pad_maximum_fusion.3), channel_id=1, source_target_pairs={{0,16},{16,32},{32,48},{48,64},{64,80},{80,96},{96,112},{112,128},... | collective-permute-start | bytes 638984 | tf_op jit(solution)/shard_map/ppermute | solution.py:41
  75.9 9.8 %collective-permute-done.3 = bf16[208,512]{1,0:T(8,128)(2,1)S(1)} collective-permute-done((bf16[208,512]{1,0:T(8,128)(2,1)S(1)}, bf16[208,512]{1,0:T(8,128)(2,1)S(1)}, u32[]{:S(2)}, u32[]{:S(2)}) %collective-permute-start.3) | collective-permute-done | bytes 213024 | tf_op jit(solution)/shard_map/ppermute | solution.py:41
  85.7 0.1 broadcast_in_dim.12
  85.9 23.7 %all_to_all.41.x_ref = bf16[8,192,512]{2,1,0:T(8,128)(2,1)S(1)} all-to-all(bf16[8,192,512]{2,1,0:T(8,128)(2,1)S(1)} %broadcast_in_dim.12), channel_id=1, replica_groups=mesh['y_lo'=2,'z'=8,'x'=4,'y_hi'=2,'core'=2] {'x','y_hi'}, dimensions={0} | all-to-all | bytes 3145728 | tf_op jit(solution)/shard_map/all_to_all | solution.py:235
  109.6 3.0 %shard_map.113.sum_ref = f32[192,640]{1,0:T(8,128)S(1)} custom-call(s32[1]{0:T(128)} %bitcast.core_ref, bf16[8,192,512]{2,1,0:T(8,128)(2,1)S(1)} %all_to_all.41.x_ref, f32[16,1,512]{2,1,0:T(1,128)S(1)} %bitcast.17, bf16[16,512,256]{2,1,0:T(8,128)(2,1)} %bitcast.27, bf16[16,512,256]{2,1,0:T(8,128)(2,1)} %bitcast.35, bf16[16,16,512]{2,1,0:T(8,128)(2,1)S(1)} %pad.5.gate_ref), custom_call_target="tpu_custom_call" | custom-call | flops 805306368 | bytes 6291456 | tf_op jit(solution)/shard_map/pallas_call | solution.py:173
  112.6 0.4 collective-permute-done.4.x_ref
  113.0 4.5 %shard_map.114 = (bf16[192,256]{1,0:T(8,128)(2,1)S(1)}, bf16[8,256,512]{2,1,0:T(8,128)(2,1)S(1)}, bf16[16,512]{1,0:T(8,128)(2,1)S(1)}, f32[2,128,128]{2,1,0:T(8,128)S(1)}, f32[2,128]{1,0:T(2,128)S(1)}) custom-call(s32[1]{0:T(128)} %bitcast.core_ref, bf16[208,512]{1,0:T(8,128)(2,1)S(1)} %broadcast_select_fusion.2.entered_ref, ...), custom_call_target="tpu_custom_call" | custom-call | flops 805306368 | bytes 6291456 | tf_op jit(solution)/shard_map/pallas_call | solution.py:195
  117.5 0.4 collective-permute-start.5
  117.9 1.2 collective-permute-done.5.far_ref
  119.1 1.0 shard_map.115
  120.1 25.8 %all_to_all.42 = bf16[8,192,512]{2,1,0:T(8,128)(2,1)S(1)} all-to-all(bf16[8,192,512]{2,1,0:T(8,128)(2,1)S(1)} %shard_map.115), channel_id=1, replica_groups=mesh['y_lo'=2,'z'=8,'x'=4,'y_hi'=2,'core'=2] {'x','y_hi'}, dimensions={0} | all-to-all | bytes 3145728 | tf_op jit(solution)/shard_map/all_to_all | solution.py:235
  145.9 0.2 convert_reduce_fusion.2
  146.2 1.9 collective-permute-start.6
  148.1 8.5 %collective-permute-done.6 = bf16[208,512]{1,0:T(8,128)(2,1)S(1)} collective-permute-done((bf16[208,512]{1,0:T(8,128)(2,1)S(1)}, bf16[208,512]{1,0:T(8,128)(2,1)S(1)}, u32[]{:S(2)}, u32[]{:S(2)}) %collective-permute-start.6) | collective-permute-done | bytes 213024 | tf_op jit(solution)/shard_map/ppermute | solution.py:41
  156.8 24.6 %all_to_all.43.x_ref = bf16[8,192,512]{2,1,0:T(8,128)(2,1)S(1)} all-to-all(bf16[8,192,512]{2,1,0:T(8,128)(2,1)S(1)} %broadcast_in_dim.13), channel_id=1, replica_groups=mesh['y_lo'=2,'z'=8,'x'=4,'y_hi'=2,'core'=2] {'x','y_hi'}, dimensions={0} | all-to-all | bytes 3145728 | tf_op jit(solution)/shard_map/all_to_all | solution.py:235
  181.5 3.0 %shard_map.116.sum_ref = f32[192,640]{1,0:T(8,128)S(1)} custom-call(s32[1]{0:T(128)} %bitcast.core_ref, bf16[8,192,512]{2,1,0:T(8,128)(2,1)S(1)} %all_to_all.43.x_ref, f32[16,1,512]{2,1,0:T(1,128)S(1)} %bitcast.19, bf16[16,512,256]{2,1,0:T(8,128)(2,1)} %bitcast.29, bf16[16,512,256]{2,1,0:T(8,128)(2,1)} %bitcast.37, bf16[16,16,512]{2,1,0:T(8,128)(2,1)S(1)} %pad.5.gate_ref), custom_call_target="tpu_custom_call" | custom-call | flops 805306368 | bytes 6291456 | tf_op jit(solution)/shard_map/pallas_call | solution.py:173
  184.5 0.4 collective-permute-done.7.x_ref
  184.9 4.5 %shard_map.117 = (bf16[192,256]{1,0:T(8,128)(2,1)S(1)}, bf16[8,256,512]{2,1,0:T(8,128)(2,1)S(1)}, bf16[16,512]{1,0:T(8,128)(2,1)S(1)}, f32[2,128,128]{2,1,0:T(8,128)S(1)}, f32[2,128]{1,0:T(2,128)S(1)}) custom-call(s32[1]{0:T(128)} %bitcast.core_ref, bf16[208,512]{1,0:T(8,128)(2,1)S(1)} %broadcast_select_fusion.1.entered_ref, ...), custom_call_target="tpu_custom_call" | custom-call | flops 805306368 | bytes 6291456 | tf_op jit(solution)/shard_map/pallas_call | solution.py:195
  189.4 0.2 collective-permute-start.8
  189.6 1.2 collective-permute-done.8.far_ref
  190.8 1.0 shard_map.118
  191.8 25.7 %all_to_all.44 = bf16[8,192,512]{2,1,0:T(8,128)(2,1)S(1)} all-to-all(bf16[8,192,512]{2,1,0:T(8,128)(2,1)S(1)} %shard_map.118), channel_id=1, replica_groups=mesh['y_lo'=2,'z'=8,'x'=4,'y_hi'=2,'core'=2] {'x','y_hi'}, dimensions={0} | all-to-all | bytes 3145728 | tf_op jit(solution)/shard_map/all_to_all | solution.py:235
  217.5 0.2 convert_reduce_fusion.1
  217.8 1.9 collective-permute-start.9
  219.7 10.0 %collective-permute-done.9 = bf16[208,512]{1,0:T(8,128)(2,1)S(1)} collective-permute-done((bf16[208,512]{1,0:T(8,128)(2,1)S(1)}, bf16[208,512]{1,0:T(8,128)(2,1)S(1)}, u32[]{:S(2)}, u32[]{:S(2)}) %collective-permute-start.9) | collective-permute-done | bytes 213024 | tf_op jit(solution)/shard_map/ppermute | solution.py:41
  229.7 0.1 broadcast_in_dim.14
  229.8 23.7 %all_to_all.45.x_ref = bf16[8,192,512]{2,1,0:T(8,128)(2,1)S(1)} all-to-all(bf16[8,192,512]{2,1,0:T(8,128)(2,1)S(1)} %broadcast_in_dim.14), channel_id=1, replica_groups=mesh['y_lo'=2,'z'=8,'x'=4,'y_hi'=2,'core'=2] {'x','y_hi'}, dimensions={0} | all-to-all | bytes 3145728 | tf_op jit(solution)/shard_map/all_to_all | solution.py:235
  253.5 2.7 shard_map.119.sum_ref
  256.2 0.7 collective-permute-done.10.x_ref
  256.9 3.7 %shard_map.120 = (bf16[192,256]{1,0:T(8,128)(2,1)S(1)}, bf16[8,256,512]{2,1,0:T(8,128)(2,1)S(1)}, bf16[16,512]{1,0:T(8,128)(2,1)}) custom-call(s32[1]{0:T(128)} %bitcast.core_ref, bf16[208,512]{1,0:T(8,128)(2,1)S(1)} %broadcast_select_fusion.entered_ref, f32[192,640]{1,0:T(8,128)S(1)} %shard_map.119.sum_ref, ...), custom_call_target="tpu_custom_call" | custom-call | flops 805306368 | bytes 6291456 | tf_op jit(solution)/shard_map/pallas_call | solution.py:195
  260.6 0.2 collective-permute-start.11
  260.8 1.2 collective-permute-done.11.far_ref
  262.0 1.0 shard_map.121
  263.0 25.7 %all_to_all.46 = bf16[8,192,512]{2,1,0:T(8,128)(2,1)S(1)} all-to-all(bf16[8,192,512]{2,1,0:T(8,128)(2,1)S(1)} %shard_map.121), channel_id=1, replica_groups=mesh['y_lo'=2,'z'=8,'x'=4,'y_hi'=2,'core'=2] {'x','y_hi'}, dimensions={0} | all-to-all | bytes 3145728 | tf_op jit(solution)/shard_map/all_to_all | solution.py:235
  288.7 0.2 convert_reduce_fusion
  288.9 0.7 add_convert_fusion
  (39 shorter events, 0.6 us)
Async XLA Ops:
  2.2 29.8 %all-to-all-start = ((bf16[8,192,512]{2,1,0:T(8,128)(2,1)}), bf16[8,192,512]{2,1,0:T(8,128)(2,1)}, u32[]{:S(2)}, u32[]{:S(2)}) async-start(bf16[8,192,512]{2,1,0:T(8,128)(2,1)} %broadcast_in_dim.10), calls=%async_computation | async-start | bytes 3145728 | tf_op jit(solution)/shard_map/all_to_all | solution.py:235
  8.3 24.5 %copy-start.3 = (bf16[192,512]{1,0:T(8,128)(2,1)S(1)}, bf16[192,512]{1,0:T(8,128)(2,1)}, u32[]{:S(2)}) copy-start(bf16[192,512]{1,0:T(8,128)(2,1)} %param.11) | copy-start | bytes 589828
  8.3 24.5 %copy-start.6 = (bf16[1,8192,2]{1,2,0:T(2,128)(2,1)S(1)}, bf16[1,8192,2]{1,2,0:T(2,128)(2,1)}, u32[]{:S(2)}) copy-start(bf16[1,8192,2]{1,2,0:T(2,128)(2,1)} %param.18) | copy-start | bytes 98308
  8.3 24.6 %copy-start.4 = (bf16[384,512]{1,0:T(8,128)(2,1)S(1)}, bf16[384,512]{1,0:T(8,128)(2,1)}, u32[]{:S(2)}) copy-start(bf16[384,512]{1,0:T(8,128)(2,1)} %param.13) | copy-start | bytes 1179652
  14.5 18.5 %copy-start.5 = (bf16[64,512]{1,0:T(8,128)(2,1)S(1)}, bf16[64,512]{1,0:T(8,128)(2,1)}, u32[]{:S(2)}) copy-start(bf16[64,512]{1,0:T(8,128)(2,1)} %param.14) | copy-start | bytes 196612
  14.5 18.6 %copy-start = (f32[1,8192]{1,0:T(1,128)S(1)}, f32[1,8192]{1,0:T(1,128)}, u32[]{:S(2)}) copy-start(f32[1,8192]{1,0:T(1,128)} %param.15) | copy-start | bytes 98308
  14.5 23.1 %collective-permute-start.1 = (bf16[8,256,512]{2,1,0:T(8,128)(2,1)}, bf16[8,256,512]{2,1,0:T(8,128)(2,1)}, u32[]{:S(2)}, u32[]{:S(2)}) collective-permute-start(bf16[8,256,512]{2,1,0:T(8,128)(2,1)} %get-tuple-element.33), channel_id=1, source_target_pairs={{0,1},{1,0},{2,3},{3,2},{4,5},{5,4},{6,7},{7,6},{8,9},{9,8},{10,11... | collective-permute-start | bytes 6291464 | tf_op jit(solution)/shard_map/ppermute | solution.py:37
  32.1 5.5 %collective-permute-start = (bf16[8,192,512]{2,1,0:T(8,128)(2,1)}, bf16[8,192,512]{2,1,0:T(8,128)(2,1)}, u32[]{:S(2)}, u32[]{:S(2)}) collective-permute-start(bf16[8,192,512]{2,1,0:T(8,128)(2,1)} %all-to-all-done.x_ref), channel_id=1, source_target_pairs={{0,1},{1,0},{2,3},{3,2},{4,5},{5,4},{6,7},{7,6},{8,9},{9,8},{10,11... | collective-permute-start | bytes 4718600 | tf_op jit(solution)/shard_map/ppermute | solution.py:37
  33.1 4.5 %copy-start.1 = (f32[1,2,128,128]{3,2,1,0:T(8,128)S(1)}, f32[1,2,128,128]{3,2,1,0:T(8,128)}, u32[]{:S(2)}) copy-start(f32[1,2,128,128]{3,2,1,0:T(8,128)} %param.20) | copy-start | bytes 393220
  33.1 4.5 %copy-start.2 = (f32[1,2,128]{2,1,0:T(2,128)S(1)}, f32[1,2,128]{2,1,0:T(2,128)}, u32[]{:S(2)}) copy-start(f32[1,2,128]{2,1,0:T(2,128)} %param.21) | copy-start | bytes 3076
  43.5 1.5 collective-permute-start.2
  72.0 13.6 %collective-permute-start.3 = (bf16[208,512]{1,0:T(8,128)(2,1)S(1)}, bf16[208,512]{1,0:T(8,128)(2,1)S(1)}, u32[]{:S(2)}, u32[]{:S(2)}) collective-permute-start(bf16[208,512]{1,0:T(8,128)(2,1)S(1)} %pad_maximum_fusion.3), channel_id=1, source_target_pairs={{0,16},{16,32},{32,48},{48,64},{64,80},{80,96},{96,112},{112,128},... | collective-permute-start | bytes 638984 | tf_op jit(solution)/shard_map/ppermute | solution.py:41
  109.6 3.4 %collective-permute-start.4 = (bf16[8,192,512]{2,1,0:T(8,128)(2,1)S(1)}, bf16[8,192,512]{2,1,0:T(8,128)(2,1)S(1)}, u32[]{:S(2)}, u32[]{:S(2)}) collective-permute-start(bf16[8,192,512]{2,1,0:T(8,128)(2,1)S(1)} %all_to_all.41.x_ref), channel_id=1, source_target_pairs={{0,1},{1,0},{2,3},{3,2},{4,5},{5,4},{6,7},{7,6},{8,9},{9,8},{10,11... | collective-permute-start | bytes 4718600 | tf_op jit(solution)/shard_map/ppermute | solution.py:37
  117.5 1.6 collective-permute-start.5
  146.2 10.5 %collective-permute-start.6 = (bf16[208,512]{1,0:T(8,128)(2,1)S(1)}, bf16[208,512]{1,0:T(8,128)(2,1)S(1)}, u32[]{:S(2)}, u32[]{:S(2)}) collective-permute-start(bf16[208,512]{1,0:T(8,128)(2,1)S(1)} %pad_maximum_fusion.4), channel_id=1, source_target_pairs={{0,16},{16,32},{32,48},{48,64},{64,80},{80,96},{96,112},{112,128},... | collective-permute-start | bytes 638984 | tf_op jit(solution)/shard_map/ppermute | solution.py:41
  181.5 3.4 %collective-permute-start.7 = (bf16[8,192,512]{2,1,0:T(8,128)(2,1)S(1)}, bf16[8,192,512]{2,1,0:T(8,128)(2,1)S(1)}, u32[]{:S(2)}, u32[]{:S(2)}) collective-permute-start(bf16[8,192,512]{2,1,0:T(8,128)(2,1)S(1)} %all_to_all.43.x_ref), channel_id=1, source_target_pairs={{0,1},{1,0},{2,3},{3,2},{4,5},{5,4},{6,7},{7,6},{8,9},{9,8},{10,11... | collective-permute-start | bytes 4718600 | tf_op jit(solution)/shard_map/ppermute | solution.py:37
  189.4 1.4 collective-permute-start.8
  217.8 11.9 %collective-permute-start.9 = (bf16[208,512]{1,0:T(8,128)(2,1)S(1)}, bf16[208,512]{1,0:T(8,128)(2,1)S(1)}, u32[]{:S(2)}, u32[]{:S(2)}) collective-permute-start(bf16[208,512]{1,0:T(8,128)(2,1)S(1)} %pad_maximum_fusion.5), channel_id=1, source_target_pairs={{0,16},{16,32},{32,48},{48,64},{64,80},{80,96},{96,112},{112,128},... | collective-permute-start | bytes 638984 | tf_op jit(solution)/shard_map/ppermute | solution.py:41
  253.5 3.4 %collective-permute-start.10 = (bf16[8,192,512]{2,1,0:T(8,128)(2,1)S(1)}, bf16[8,192,512]{2,1,0:T(8,128)(2,1)S(1)}, u32[]{:S(2)}, u32[]{:S(2)}) collective-permute-start(bf16[8,192,512]{2,1,0:T(8,128)(2,1)S(1)} %all_to_all.45.x_ref), channel_id=1, source_target_pairs={{0,1},{1,0},{2,3},{3,2},{4,5},{5,4},{6,7},{7,6},{8,9},{9,8},{10,11... | collective-permute-start | bytes 4718600 | tf_op jit(solution)/shard_map/ppermute | solution.py:37
  260.6 1.4 collective-permute-start.11

commit v6 on v5

--- a/solution.py
+++ b/solution.py
@@ -65,7 +65,7 @@
 
 
 def project_half(write, offset, x_ref, gain_ref, wk_ref, wv_ref, gate_ref, bufs, sems, extra=None):
-    k_buf, v_buf = bufs
+    k_buf, v_buf, *x_buf = bufs
     rows = x_ref.shape[1]
     copies = []
     for b in range(N_CHIPS):
@@ -75,6 +75,7 @@
             (
                 (wk_ref.at[place], k_buf.at[b]),
                 (wv_ref.at[place], v_buf.at[b]),
+                *((x_ref.at[b], buf.at[b]) for buf in x_buf),
             )
         ):
             copy = pltpu.make_async_copy(source, target, sems.at[i, b])
@@ -83,13 +84,14 @@
         copies.append(group)
     if extra is not None:
         extra.start()
+    x_blocks = x_buf[0] if x_buf else x_ref
     dot = functools.partial(jnp.dot, preferred_element_type=jnp.float32)
     squares, gates, keys, values = 0.0, 0.0, 0.0, 0.0
     for b in range(N_CHIPS):
         place = 2 * b + offset
         for copy in copies[b]:
             copy.wait()
-        wide = x_ref[b].astype(jnp.float32)
+        wide = x_blocks[b].astype(jnp.float32)
         squares += wide * wide
         scaled = (wide * gain_ref[place]).astype(jnp.bfloat16)
         keys += dot(scaled, k_buf[b])
@@ -120,15 +122,16 @@
 
 
 def read_kernel(
-    write, core_ref, entered_ref, sum_ref, x_ref, gain_ref, wk_ref, wv_ref, gate_ref, f_ref,
+    write, buffers, core_ref, entered_ref, sum_ref, x_ref, gain_ref, wk_ref, wv_ref, gate_ref, f_ref,
     a_ref, z_ref, read_ref, f_next, tile_ref, *rest,
 ):
-    *state, k_buf, v_buf, sems, f_sem = rest
+    *state, sems, f_sem = rest
+    state, bufs = state[:-buffers], state[-buffers:]
     rows = x_ref.shape[1]
     f_copy = pltpu.make_async_copy(f_ref, f_next, f_sem.at[0])
     keys, values, squares, gates = project_half(
         write, 1 - core_ref[0], x_ref, gain_ref, wk_ref, wv_ref, gate_ref,
-        (k_buf, v_buf), sems, f_copy,
+        bufs, sems, f_copy,
     )
     keys += sum_ref[:, :WIDE]
     values += sum_ref[:, WIDE : 2 * WIDE]
@@ -163,19 +166,20 @@
     f_copy.wait()
 
 
-def half_scratch():
+def half_scratch(rows, stream):
     weights = pltpu.VMEM((N_CHIPS, BLOCK, WIDE), jnp.bfloat16)
-    return [weights, weights, pltpu.SemaphoreType.DMA((2, N_CHIPS))]
-
-
-def project_first(core, own, gain, wk, wv, gate, write):
+    x = [pltpu.VMEM((N_CHIPS, rows, BLOCK), jnp.bfloat16)] if stream else []
+    return [weights, weights, *x, pltpu.SemaphoreType.DMA((3, N_CHIPS))]
+
+
+def project_first(core, own, gain, wk, wv, gate, write, stream):
     rows = own.shape[1]
     return pl.pallas_call(
         functools.partial(first_kernel, write),
-        in_specs=[SMEM, VMEM, VMEM, ANY, ANY, VMEM],
+        in_specs=[SMEM, ANY if stream else VMEM, VMEM, ANY, ANY, VMEM],
         out_specs=VMEM,
         out_shape=jax.ShapeDtypeStruct((rows, 2 * WIDE + SIDE), jnp.float32),
-        scratch_shapes=half_scratch(),
+        scratch_shapes=half_scratch(rows, stream),
         compiler_params=pltpu.CompilerParams(vmem_limit_bytes=VMEM_LIMIT),
         cost_estimate=pl.CostEstimate(
             flops=rows * HIDDEN * 2 * WIDE, bytes_accessed=6 * 2**20, transcendentals=0
@@ -183,7 +187,7 @@
     )(core, own, gain, wk, wv, gate)
 
 
-def read_memory(core, entered, begun, got, gain, wk, wv, gate, f, a, z, write):
+def read_memory(core, entered, begun, got, gain, wk, wv, gate, f, a, z, write, stream):
     rows = got.shape[1]
     shapes = [
         jax.ShapeDtypeStruct((rows, WIDE), jnp.bfloat16),
@@ -193,11 +197,11 @@
     if write:
         shapes += [jax.ShapeDtypeStruct(a.shape, a.dtype), jax.ShapeDtypeStruct(z.shape, z.dtype)]
     return pl.pallas_call(
-        functools.partial(read_kernel, write),
-        in_specs=[SMEM, VMEM, VMEM, VMEM, VMEM, ANY, ANY, VMEM, ANY, VMEM, VMEM],
+        functools.partial(read_kernel, write, 3 if stream else 2),
+        in_specs=[SMEM, VMEM, VMEM, ANY if stream else VMEM, VMEM, ANY, ANY, VMEM, ANY, VMEM, VMEM],
         out_specs=[VMEM] * len(shapes),
         out_shape=shapes,
-        scratch_shapes=half_scratch() + [pltpu.SemaphoreType.DMA((1,))],
+        scratch_shapes=half_scratch(rows, stream) + [pltpu.SemaphoreType.DMA((1,))],
         compiler_params=pltpu.CompilerParams(vmem_limit_bytes=VMEM_LIMIT),
         cost_estimate=pl.CostEstimate(
             flops=rows * HIDDEN * 2 * WIDE, bytes_accessed=6 * 2**20, transcendentals=0
@@ -283,9 +287,9 @@
             outgoing = copies(entered[:PIECE])
         own = exchange(outgoing)
         got = swap(own, "core")
-        begun = project_first(which, own, gain, wk, wv, gate, write)
+        begun = project_first(which, own, gain, wk, wv, gate, write, t == 0)
         read, f_near, tile, *state = read_memory(
-            which, entered, begun, got, gain, wk, wv, gate, f_got, a, z, write
+            which, entered, begun, got, gain, wk, wv, gate, f_got, a, z, write, t == 0
         )
         if write:
             a, z = state

time: 290 us -> 288 us (level)
  transfers between devices with their start and end apart: 13 -> 13, of which waited for: 11 -> 11; matrix products, arithmetic and copies ran while one was open for 0% -> 0% of each run, Pallas kernels for 7% -> 6%
where the time goes in v6:
time: 288 us; the launch traced here: 287 us
  blocking collectives  175 us (61%)
  waiting for transfers between devices  51.3 us (18%)
  Pallas kernels  39.9 us (14%)
  starting transfers between devices  15.3 us (5%)
    all_to_all x7, blocking collectives, exchange(): return lax.all_to_all(blocks, CHIPS, 0, 0, tiled=True)  175 us
    ppermute x3, waiting for transfers between devices, next_section(): return lax.ppermute(value, SECTION, [(i, i + 1) for i in range(15)])  28.2 us
    pallas_call x4, Pallas kernels, read_memory(): pl.pallas_call(functools.partial(read_kernel, write, 3 if stream else 2),...  17.6 us
    all_to_all x1, waiting for transfers between devices, exchange(): return lax.all_to_all(blocks, CHIPS, 0, 0, tiled=True)  17.6 us
    pallas_call x4, Pallas kernels, project_first(): pl.pallas_call(functools.partial(first_kernel, write), in_specs=[SMEM, AN...  12.2 us
    ppermute x3, starting transfers between devices, next_section(): return lax.ppermute(value, SECTION, [(i, i + 1) for i in range(15)])  7.66 us
    pallas_call x1, Pallas kernels, pick(): pl.pallas_call(pick_kernel, grid=(N_CHIPS,), in_specs=[SMEM, pl.BlockSpec...  6.21 us
    all_to_all x1, starting transfers between devices, exchange(): return lax.all_to_all(blocks, CHIPS, 0, 0, tiled=True)  6.03 us
  transfers between devices with their start and end apart: 13, of which 11 were waited for; matrix products, arithmetic and copies ran while one was open for 0% of the time, Pallas kernels for 6%

profile of v6, /device:TPU:8, one launch (start us, length us, event | category | flops | bytes accessed | tf_op | source)
XLA Modules:
  0.0 287.3 jit_solution(10071318401222665070)
XLA Ops:
  0.0 2.2 broadcast_in_dim.10
  2.2 6.0 %all-to-all-start = ((bf16[8,192,512]{2,1,0:T(8,128)(2,1)}), bf16[8,192,512]{2,1,0:T(8,128)(2,1)}, u32[]{:S(2)}, u32[]{:S(2)}) async-start(bf16[8,192,512]{2,1,0:T(8,128)(2,1)} %broadcast_in_dim.10), calls=%async_computation | async-start | bytes 3145728 | tf_op jit(solution)/shard_map/all_to_all | solution.py:239
  8.3 6.2 %shard_map.110 = (bf16[8,256,512]{2,1,0:T(8,128)(2,1)S(1)}, bf16[8,256,512]{2,1,0:T(8,128)(2,1)}) custom-call(s32[1]{0:T(128)} %bitcast.core_ref, bf16[256,8192]{1,0:T(8,128)(2,1)} %bitcast.41), custom_call_target="tpu_custom_call" | custom-call | tf_op jit(solution)/shard_map/pallas_call | solution.py:56
  14.5 17.6 %all-to-all-done.x_ref = bf16[8,192,512]{2,1,0:T(8,128)(2,1)} async-done(((bf16[8,192,512]{2,1,0:T(8,128)(2,1)}), bf16[8,192,512]{2,1,0:T(8,128)(2,1)}, u32[]{:S(2)}, u32[]{:S(2)}) %all-to-all-start) | async-done | bytes 1572896 | tf_op jit(solution)/shard_map/all_to_all | solution.py:239
  33.0 0.2 fusion.2
  33.1 3.2 %shard_map.109.sum_ref = f32[192,640]{1,0:T(8,128)S(1)} custom-call(s32[1]{0:T(128)} %bitcast.core_ref, bf16[8,192,512]{2,1,0:T(8,128)(2,1)} %all-to-all-done.x_ref, f32[16,1,512]{2,1,0:T(1,128)S(1)} %bitcast.15, bf16[16,512,256]{2,1,0:T(8,128)(2,1)} %bitcast.25, bf16[16,512,256]{2,1,0:T(8,128)(2,1)} %bitcast.33, bf16[16,16,512]{2,1,0:T(8,128)(2,1)S(1)} %pad.5.gate_ref), custom_call_target="tpu_custom_call" | custom-call | flops 805306368 | bytes 6291456 | tf_op jit(solution)/shard_map/pallas_call | solution.py:177
  36.4 4.7 %shard_map.111 = (bf16[192,256]{1,0:T(8,128)(2,1)S(1)}, bf16[8,256,512]{2,1,0:T(8,128)(2,1)S(1)}, bf16[16,512]{1,0:T(8,128)(2,1)S(1)}, f32[2,128,128]{2,1,0:T(8,128)S(1)}, f32[2,128]{1,0:T(2,128)S(1)}) custom-call(s32[1]{0:T(128)} %bitcast.core_ref, bf16[208,512]{1,0:T(8,128)(2,1)S(1)} %concatenate.21.entered_ref, f32[192,640]{1,0:T(8,128)S(1)} %shard_map.109.sum_ref, ...), custom_call_target="tpu_custom_call" | custom-call | flops 805306368 | bytes 6291456 | tf_op jit(solution)/shard_map/pallas_call | solution.py:199
  41.1 0.6 collective-permute-start.2
  41.7 0.9 collective-permute-done.2.far_ref
  42.6 1.0 shard_map.112
  43.6 25.7 %all_to_all.40 = bf16[8,192,512]{2,1,0:T(8,128)(2,1)S(1)} all-to-all(bf16[8,192,512]{2,1,0:T(8,128)(2,1)S(1)} %shard_map.112), channel_id=1, replica_groups=mesh['y_lo'=2,'z'=8,'x'=4,'y_hi'=2,'core'=2] {'x','y_hi'}, dimensions={0} | all-to-all | bytes 3145728 | tf_op jit(solution)/shard_map/all_to_all | solution.py:239
  69.3 0.2 convert_reduce_fusion.3
  69.6 3.8 %collective-permute-start.3 = (bf16[208,512]{1,0:T(8,128)(2,1)S(1)}, bf16[208,512]{1,0:T(8,128)(2,1)S(1)}, u32[]{:S(2)}, u32[]{:S(2)}) collective-permute-start(bf16[208,512]{1,0:T(8,128)(2,1)S(1)} %pad_maximum_fusion.3), channel_id=1, source_target_pairs={{0,16},{16,32},{32,48},{48,64},{64,80},{80,96},{96,112},{112,128},... | collective-permute-start | bytes 638984 | tf_op jit(solution)/shard_map/ppermute | solution.py:41
  73.5 9.8 %collective-permute-done.3 = bf16[208,512]{1,0:T(8,128)(2,1)S(1)} collective-permute-done((bf16[208,512]{1,0:T(8,128)(2,1)S(1)}, bf16[208,512]{1,0:T(8,128)(2,1)S(1)}, u32[]{:S(2)}, u32[]{:S(2)}) %collective-permute-start.3) | collective-permute-done | bytes 213024 | tf_op jit(solution)/shard_map/ppermute | solution.py:41
  83.3 0.1 broadcast_in_dim.12
  83.5 23.8 %all_to_all.41.x_ref = bf16[8,192,512]{2,1,0:T(8,128)(2,1)S(1)} all-to-all(bf16[8,192,512]{2,1,0:T(8,128)(2,1)S(1)} %broadcast_in_dim.12), channel_id=1, replica_groups=mesh['y_lo'=2,'z'=8,'x'=4,'y_hi'=2,'core'=2] {'x','y_hi'}, dimensions={0} | all-to-all | bytes 3145728 | tf_op jit(solution)/shard_map/all_to_all | solution.py:239
  107.2 3.1 %shard_map.113.sum_ref = f32[192,640]{1,0:T(8,128)S(1)} custom-call(s32[1]{0:T(128)} %bitcast.core_ref, bf16[8,192,512]{2,1,0:T(8,128)(2,1)S(1)} %all_to_all.41.x_ref, f32[16,1,512]{2,1,0:T(1,128)S(1)} %bitcast.17, bf16[16,512,256]{2,1,0:T(8,128)(2,1)} %bitcast.27, bf16[16,512,256]{2,1,0:T(8,128)(2,1)} %bitcast.35, bf16[16,16,512]{2,1,0:T(8,128)(2,1)S(1)} %pad.5.gate_ref), custom_call_target="tpu_custom_call" | custom-call | flops 805306368 | bytes 6291456 | tf_op jit(solution)/shard_map/pallas_call | solution.py:177
  110.3 0.3 collective-permute-done.4.x_ref
  110.6 4.6 %shard_map.114 = (bf16[192,256]{1,0:T(8,128)(2,1)S(1)}, bf16[8,256,512]{2,1,0:T(8,128)(2,1)S(1)}, bf16[16,512]{1,0:T(8,128)(2,1)S(1)}, f32[2,128,128]{2,1,0:T(8,128)S(1)}, f32[2,128]{1,0:T(2,128)S(1)}) custom-call(s32[1]{0:T(128)} %bitcast.core_ref, bf16[208,512]{1,0:T(8,128)(2,1)S(1)} %broadcast_select_fusion.2.entered_ref, ...), custom_call_target="tpu_custom_call" | custom-call | flops 805306368 | bytes 6291456 | tf_op jit(solution)/shard_map/pallas_call | solution.py:199
  115.2 0.5 collective-permute-start.5
  115.7 1.1 collective-permute-done.5.far_ref
  116.8 1.0 shard_map.115
  117.8 25.7 %all_to_all.42 = bf16[8,192,512]{2,1,0:T(8,128)(2,1)S(1)} all-to-all(bf16[8,192,512]{2,1,0:T(8,128)(2,1)S(1)} %shard_map.115), channel_id=1, replica_groups=mesh['y_lo'=2,'z'=8,'x'=4,'y_hi'=2,'core'=2] {'x','y_hi'}, dimensions={0} | all-to-all | bytes 3145728 | tf_op jit(solution)/shard_map/all_to_all | solution.py:239
  143.5 0.2 convert_reduce_fusion.2
  143.8 1.9 collective-permute-start.6
  145.7 8.4 %collective-permute-done.6 = bf16[208,512]{1,0:T(8,128)(2,1)S(1)} collective-permute-done((bf16[208,512]{1,0:T(8,128)(2,1)S(1)}, bf16[208,512]{1,0:T(8,128)(2,1)S(1)}, u32[]{:S(2)}, u32[]{:S(2)}) %collective-permute-start.6) | collective-permute-done | bytes 213024 | tf_op jit(solution)/shard_map/ppermute | solution.py:41
  154.3 24.7 %all_to_all.43.x_ref = bf16[8,192,512]{2,1,0:T(8,128)(2,1)S(1)} all-to-all(bf16[8,192,512]{2,1,0:T(8,128)(2,1)S(1)} %broadcast_in_dim.13), channel_id=1, replica_groups=mesh['y_lo'=2,'z'=8,'x'=4,'y_hi'=2,'core'=2] {'x','y_hi'}, dimensions={0} | all-to-all | bytes 3145728 | tf_op jit(solution)/shard_map/all_to_all | solution.py:239
  179.1 3.1 %shard_map.116.sum_ref = f32[192,640]{1,0:T(8,128)S(1)} custom-call(s32[1]{0:T(128)} %bitcast.core_ref, bf16[8,192,512]{2,1,0:T(8,128)(2,1)S(1)} %all_to_all.43.x_ref, f32[16,1,512]{2,1,0:T(1,128)S(1)} %bitcast.19, bf16[16,512,256]{2,1,0:T(8,128)(2,1)} %bitcast.29, bf16[16,512,256]{2,1,0:T(8,128)(2,1)} %bitcast.37, bf16[16,16,512]{2,1,0:T(8,128)(2,1)S(1)} %pad.5.gate_ref), custom_call_target="tpu_custom_call" | custom-call | flops 805306368 | bytes 6291456 | tf_op jit(solution)/shard_map/pallas_call | solution.py:177
  182.2 0.3 collective-permute-done.7.x_ref
  182.5 4.6 %shard_map.117 = (bf16[192,256]{1,0:T(8,128)(2,1)S(1)}, bf16[8,256,512]{2,1,0:T(8,128)(2,1)S(1)}, bf16[16,512]{1,0:T(8,128)(2,1)S(1)}, f32[2,128,128]{2,1,0:T(8,128)S(1)}, f32[2,128]{1,0:T(2,128)S(1)}) custom-call(s32[1]{0:T(128)} %bitcast.core_ref, bf16[208,512]{1,0:T(8,128)(2,1)S(1)} %broadcast_select_fusion.1.entered_ref, ...), custom_call_target="tpu_custom_call" | custom-call | flops 805306368 | bytes 6291456 | tf_op jit(solution)/shard_map/pallas_call | solution.py:199
  187.1 0.3 collective-permute-start.8
  187.4 1.1 collective-permute-done.8.far_ref
  188.5 1.0 shard_map.118
  189.5 25.7 %all_to_all.44 = bf16[8,192,512]{2,1,0:T(8,128)(2,1)S(1)} all-to-all(bf16[8,192,512]{2,1,0:T(8,128)(2,1)S(1)} %shard_map.118), channel_id=1, replica_groups=mesh['y_lo'=2,'z'=8,'x'=4,'y_hi'=2,'core'=2] {'x','y_hi'}, dimensions={0} | all-to-all | bytes 3145728 | tf_op jit(solution)/shard_map/all_to_all | solution.py:239
  215.2 0.2 convert_reduce_fusion.1
  215.5 1.9 collective-permute-start.9
  217.4 9.9 %collective-permute-done.9 = bf16[208,512]{1,0:T(8,128)(2,1)S(1)} collective-permute-done((bf16[208,512]{1,0:T(8,128)(2,1)S(1)}, bf16[208,512]{1,0:T(8,128)(2,1)S(1)}, u32[]{:S(2)}, u32[]{:S(2)}) %collective-permute-start.9) | collective-permute-done | bytes 213024 | tf_op jit(solution)/shard_map/ppermute | solution.py:41
  227.4 0.1 broadcast_in_dim.14
  227.5 23.6 %all_to_all.45.x_ref = bf16[8,192,512]{2,1,0:T(8,128)(2,1)S(1)} all-to-all(bf16[8,192,512]{2,1,0:T(8,128)(2,1)S(1)} %broadcast_in_dim.14), channel_id=1, replica_groups=mesh['y_lo'=2,'z'=8,'x'=4,'y_hi'=2,'core'=2] {'x','y_hi'}, dimensions={0} | all-to-all | bytes 3145728 | tf_op jit(solution)/shard_map/all_to_all | solution.py:239
  251.1 2.8 shard_map.119.sum_ref
  253.9 0.6 collective-permute-done.10.x_ref
  254.5 3.8 %shard_map.120 = (bf16[192,256]{1,0:T(8,128)(2,1)S(1)}, bf16[8,256,512]{2,1,0:T(8,128)(2,1)S(1)}, bf16[16,512]{1,0:T(8,128)(2,1)}) custom-call(s32[1]{0:T(128)} %bitcast.core_ref, bf16[208,512]{1,0:T(8,128)(2,1)S(1)} %broadcast_select_fusion.entered_ref, f32[192,640]{1,0:T(8,128)S(1)} %shard_map.119.sum_ref, ...), custom_call_target="tpu_custom_call" | custom-call | flops 805306368 | bytes 6291456 | tf_op jit(solution)/shard_map/pallas_call | solution.py:199
  258.3 0.2 collective-permute-start.11
  258.5 1.2 collective-permute-done.11.far_ref
  259.7 1.0 shard_map.121
  260.7 25.7 %all_to_all.46 = bf16[8,192,512]{2,1,0:T(8,128)(2,1)S(1)} all-to-all(bf16[8,192,512]{2,1,0:T(8,128)(2,1)S(1)} %shard_map.121), channel_id=1, replica_groups=mesh['y_lo'=2,'z'=8,'x'=4,'y_hi'=2,'core'=2] {'x','y_hi'}, dimensions={0} | all-to-all | bytes 3145728 | tf_op jit(solution)/shard_map/all_to_all | solution.py:239
  286.3 0.2 convert_reduce_fusion
  286.6 0.7 add_convert_fusion
  (39 shorter events, 0.6 us)
Async XLA Ops:
  2.2 29.8 %all-to-all-start = ((bf16[8,192,512]{2,1,0:T(8,128)(2,1)}), bf16[8,192,512]{2,1,0:T(8,128)(2,1)}, u32[]{:S(2)}, u32[]{:S(2)}) async-start(bf16[8,192,512]{2,1,0:T(8,128)(2,1)} %broadcast_in_dim.10), calls=%async_computation | async-start | bytes 3145728 | tf_op jit(solution)/shard_map/all_to_all | solution.py:239
  8.3 24.5 %copy-start.3 = (bf16[192,512]{1,0:T(8,128)(2,1)S(1)}, bf16[192,512]{1,0:T(8,128)(2,1)}, u32[]{:S(2)}) copy-start(bf16[192,512]{1,0:T(8,128)(2,1)} %param.11) | copy-start | bytes 589828
  8.3 24.5 %copy-start.6 = (bf16[1,8192,2]{1,2,0:T(2,128)(2,1)S(1)}, bf16[1,8192,2]{1,2,0:T(2,128)(2,1)}, u32[]{:S(2)}) copy-start(bf16[1,8192,2]{1,2,0:T(2,128)(2,1)} %param.18) | copy-start | bytes 98308
  8.3 24.6 %copy-start.4 = (bf16[384,512]{1,0:T(8,128)(2,1)S(1)}, bf16[384,512]{1,0:T(8,128)(2,1)}, u32[]{:S(2)}) copy-start(bf16[384,512]{1,0:T(8,128)(2,1)} %param.13) | copy-start | bytes 1179652
  14.5 18.5 %copy-start.5 = (bf16[64,512]{1,0:T(8,128)(2,1)S(1)}, bf16[64,512]{1,0:T(8,128)(2,1)}, u32[]{:S(2)}) copy-start(bf16[64,512]{1,0:T(8,128)(2,1)} %param.14) | copy-start | bytes 196612
  14.5 18.6 %copy-start = (f32[1,8192]{1,0:T(1,128)S(1)}, f32[1,8192]{1,0:T(1,128)}, u32[]{:S(2)}) copy-start(f32[1,8192]{1,0:T(1,128)} %param.15) | copy-start | bytes 98308
  14.5 21.9 %collective-permute-start.1 = (bf16[8,256,512]{2,1,0:T(8,128)(2,1)}, bf16[8,256,512]{2,1,0:T(8,128)(2,1)}, u32[]{:S(2)}, u32[]{:S(2)}) collective-permute-start(bf16[8,256,512]{2,1,0:T(8,128)(2,1)} %get-tuple-element.33), channel_id=1, source_target_pairs={{0,1},{1,0},{2,3},{3,2},{4,5},{5,4},{6,7},{7,6},{8,9},{9,8},{10,11... | collective-permute-start | bytes 6291464 | tf_op jit(solution)/shard_map/ppermute | solution.py:37
  32.1 4.3 %collective-permute-start = (bf16[8,192,512]{2,1,0:T(8,128)(2,1)}, bf16[8,192,512]{2,1,0:T(8,128)(2,1)}, u32[]{:S(2)}, u32[]{:S(2)}) collective-permute-start(bf16[8,192,512]{2,1,0:T(8,128)(2,1)} %all-to-all-done.x_ref), channel_id=1, source_target_pairs={{0,1},{1,0},{2,3},{3,2},{4,5},{5,4},{6,7},{7,6},{8,9},{9,8},{10,11... | collective-permute-start | bytes 4718600 | tf_op jit(solution)/shard_map/ppermute | solution.py:37
  33.1 3.3 %copy-start.1 = (f32[1,2,128,128]{3,2,1,0:T(8,128)S(1)}, f32[1,2,128,128]{3,2,1,0:T(8,128)}, u32[]{:S(2)}) copy-start(f32[1,2,128,128]{3,2,1,0:T(8,128)} %param.20) | copy-start | bytes 393220
  33.1 3.3 %copy-start.2 = (f32[1,2,128]{2,1,0:T(2,128)S(1)}, f32[1,2,128]{2,1,0:T(2,128)}, u32[]{:S(2)}) copy-start(f32[1,2,128]{2,1,0:T(2,128)} %param.21) | copy-start | bytes 3076
  41.1 1.5 collective-permute-start.2
  69.6 13.6 %collective-permute-start.3 = (bf16[208,512]{1,0:T(8,128)(2,1)S(1)}, bf16[208,512]{1,0:T(8,128)(2,1)S(1)}, u32[]{:S(2)}, u32[]{:S(2)}) collective-permute-start(bf16[208,512]{1,0:T(8,128)(2,1)S(1)} %pad_maximum_fusion.3), channel_id=1, source_target_pairs={{0,16},{16,32},{32,48},{48,64},{64,80},{80,96},{96,112},{112,128},... | collective-permute-start | bytes 638984 | tf_op jit(solution)/shard_map/ppermute | solution.py:41
  107.2 3.4 %collective-permute-start.4 = (bf16[8,192,512]{2,1,0:T(8,128)(2,1)S(1)}, bf16[8,192,512]{2,1,0:T(8,128)(2,1)S(1)}, u32[]{:S(2)}, u32[]{:S(2)}) collective-permute-start(bf16[8,192,512]{2,1,0:T(8,128)(2,1)S(1)} %all_to_all.41.x_ref), channel_id=1, source_target_pairs={{0,1},{1,0},{2,3},{3,2},{4,5},{5,4},{6,7},{7,6},{8,9},{9,8},{10,11... | collective-permute-start | bytes 4718600 | tf_op jit(solution)/shard_map/ppermute | solution.py:37
  115.2 1.6 collective-permute-start.5
  143.8 10.3 %collective-permute-start.6 = (bf16[208,512]{1,0:T(8,128)(2,1)S(1)}, bf16[208,512]{1,0:T(8,128)(2,1)S(1)}, u32[]{:S(2)}, u32[]{:S(2)}) collective-permute-start(bf16[208,512]{1,0:T(8,128)(2,1)S(1)} %pad_maximum_fusion.4), channel_id=1, source_target_pairs={{0,16},{16,32},{32,48},{48,64},{64,80},{80,96},{96,112},{112,128},... | collective-permute-start | bytes 638984 | tf_op jit(solution)/shard_map/ppermute | solution.py:41
  179.1 3.4 %collective-permute-start.7 = (bf16[8,192,512]{2,1,0:T(8,128)(2,1)S(1)}, bf16[8,192,512]{2,1,0:T(8,128)(2,1)S(1)}, u32[]{:S(2)}, u32[]{:S(2)}) collective-permute-start(bf16[8,192,512]{2,1,0:T(8,128)(2,1)S(1)} %all_to_all.43.x_ref), channel_id=1, source_target_pairs={{0,1},{1,0},{2,3},{3,2},{4,5},{5,4},{6,7},{7,6},{8,9},{9,8},{10,11... | collective-permute-start | bytes 4718600 | tf_op jit(solution)/shard_map/ppermute | solution.py:37
  187.1 1.4 collective-permute-start.8
  215.5 11.9 %collective-permute-start.9 = (bf16[208,512]{1,0:T(8,128)(2,1)S(1)}, bf16[208,512]{1,0:T(8,128)(2,1)S(1)}, u32[]{:S(2)}, u32[]{:S(2)}) collective-permute-start(bf16[208,512]{1,0:T(8,128)(2,1)S(1)} %pad_maximum_fusion.5), channel_id=1, source_target_pairs={{0,16},{16,32},{32,48},{48,64},{64,80},{80,96},{96,112},{112,128},... | collective-permute-start | bytes 638984 | tf_op jit(solution)/shard_map/ppermute | solution.py:41
  251.1 3.4 %collective-permute-start.10 = (bf16[8,192,512]{2,1,0:T(8,128)(2,1)S(1)}, bf16[8,192,512]{2,1,0:T(8,128)(2,1)S(1)}, u32[]{:S(2)}, u32[]{:S(2)}) collective-permute-start(bf16[8,192,512]{2,1,0:T(8,128)(2,1)S(1)} %all_to_all.45.x_ref), channel_id=1, source_target_pairs={{0,1},{1,0},{2,3},{3,2},{4,5},{5,4},{6,7},{7,6},{8,9},{9,8},{10,11... | collective-permute-start | bytes 4718600 | tf_op jit(solution)/shard_map/ppermute | solution.py:37
  258.3 1.4 collective-permute-start.11

commit v7 on v6

--- a/solution.py
+++ b/solution.py
@@ -26,7 +26,6 @@
 WIDE = HEADS * HD
 HIDDEN = 8192
 VMEM_LIMIT = 48 * 2**20
-HIGHEST = lax.Precision.HIGHEST
 
 
 VMEM = pl.BlockSpec(memory_space=pltpu.VMEM)
@@ -121,6 +120,18 @@
         sum_ref[rows - MEM :, 2 * WIDE : 2 * WIDE + GATE_ROWS] = gates
 
 
+def split_dot(left, right, contract):
+    dot = functools.partial(
+        lax.dot_general,
+        dimension_numbers=((contract, (0,)), ((), ())),
+        preferred_element_type=jnp.float32,
+    )
+    left_high, right_high = left.astype(jnp.bfloat16), right.astype(jnp.bfloat16)
+    left_low = (left - left_high.astype(jnp.float32)).astype(jnp.bfloat16)
+    right_low = (right - right_high.astype(jnp.float32)).astype(jnp.bfloat16)
+    return dot(left_high, right_high) + (dot(left_high, right_low) + dot(left_low, right_high))
+
+
 def read_kernel(
     write, buffers, core_ref, entered_ref, sum_ref, x_ref, gain_ref, wk_ref, wv_ref, gate_ref, f_ref,
     a_ref, z_ref, read_ref, f_next, tile_ref, *rest,
@@ -146,7 +157,7 @@
         z = z_ref[h : h + 1] * keep
         k = keys[:, h * HD : (h + 1) * HD] * scale
         k = jnp.where(k > 0, k + 1.0, jnp.exp(jnp.minimum(k, 0.0)))
-        top = jnp.dot(k, a, precision=HIGHEST, preferred_element_type=jnp.float32)
+        top = split_dot(k, a, (1,))
         bottom = jnp.sum(k * z, axis=1, keepdims=True) + 1.0
         read = top / bottom
         read_ref[:, h * HD : (h + 1) * HD] = read.astype(jnp.bfloat16)
@@ -155,13 +166,7 @@
             logit = (side[rows - MEM :, h : h + 1] + gates[:, h : h + 1]) * scale[rows - MEM :]
             gate = 1.0 / (1.0 + jnp.exp(-logit))
             tail = k[rows - MEM :]
-            state[0][h] = a + lax.dot_general(
-                tail,
-                (v - read[rows - MEM :]) * gate,
-                (((0,), (0,)), ((), ())),
-                precision=HIGHEST,
-                preferred_element_type=jnp.float32,
-            )
+            state[0][h] = a + split_dot(tail, (v - read[rows - MEM :]) * gate, (0,))
             state[1][h : h + 1] = z + jnp.sum(tail, axis=0, keepdims=True)
     f_copy.wait()
 

time: 288 us -> 287 us (level)
  no operation moved by 1% of the time
where the time goes in v7:
time: 287 us; the launch traced here: 286 us
  blocking collectives  175 us (61%)
  waiting for transfers between devices  51.3 us (18%)
  Pallas kernels  39 us (14%)
  starting transfers between devices  15.3 us (5%)
    all_to_all x7, blocking collectives, exchange(): return lax.all_to_all(blocks, CHIPS, 0, 0, tiled=True)  175 us
    ppermute x3, waiting for transfers between devices, next_section(): return lax.ppermute(value, SECTION, [(i, i + 1) for i in range(15)])  28.1 us
    all_to_all x1, waiting for transfers between devices, exchange(): return lax.all_to_all(blocks, CHIPS, 0, 0, tiled=True)  17.6 us
    pallas_call x4, Pallas kernels, read_memory(): pl.pallas_call(functools.partial(read_kernel, write, 3 if stream else 2),...  16.7 us
    pallas_call x4, Pallas kernels, project_first(): pl.pallas_call(functools.partial(first_kernel, write), in_specs=[SMEM, AN...  12.2 us
    ppermute x3, starting transfers between devices, next_section(): return lax.ppermute(value, SECTION, [(i, i + 1) for i in range(15)])  7.66 us
    pallas_call x1, Pallas kernels, pick(): pl.pallas_call(pick_kernel, grid=(N_CHIPS,), in_specs=[SMEM, pl.BlockSpec...  6.21 us
    all_to_all x1, starting transfers between devices, exchange(): return lax.all_to_all(blocks, CHIPS, 0, 0, tiled=True)  6.03 us
  transfers between devices with their start and end apart: 13, of which 11 were waited for; matrix products, arithmetic and copies ran while one was open for 0% of the time, Pallas kernels for 6%

profile of v7, /device:TPU:8, one launch (start us, length us, event | category | flops | bytes accessed | tf_op | source)
XLA Modules:
  0.0 286.4 jit_solution(17739800446303888181)
XLA Ops:
  0.0 2.2 broadcast_in_dim.10
  2.2 6.0 %all-to-all-start = ((bf16[8,192,512]{2,1,0:T(8,128)(2,1)}), bf16[8,192,512]{2,1,0:T(8,128)(2,1)}, u32[]{:S(2)}, u32[]{:S(2)}) async-start(bf16[8,192,512]{2,1,0:T(8,128)(2,1)} %broadcast_in_dim.10), calls=%async_computation | async-start | bytes 3145728 | tf_op jit(solution)/shard_map/all_to_all | solution.py:244
  8.3 6.2 %shard_map.110 = (bf16[8,256,512]{2,1,0:T(8,128)(2,1)S(1)}, bf16[8,256,512]{2,1,0:T(8,128)(2,1)}) custom-call(s32[1]{0:T(128)} %bitcast.core_ref, bf16[256,8192]{1,0:T(8,128)(2,1)} %bitcast.41), custom_call_target="tpu_custom_call" | custom-call | tf_op jit(solution)/shard_map/pallas_call | solution.py:55
  14.5 17.6 %all-to-all-done.x_ref = bf16[8,192,512]{2,1,0:T(8,128)(2,1)} async-done(((bf16[8,192,512]{2,1,0:T(8,128)(2,1)}), bf16[8,192,512]{2,1,0:T(8,128)(2,1)}, u32[]{:S(2)}, u32[]{:S(2)}) %all-to-all-start) | async-done | bytes 1572896 | tf_op jit(solution)/shard_map/all_to_all | solution.py:244
  33.0 0.2 fusion.2
  33.1 3.2 %shard_map.109.sum_ref = f32[192,640]{1,0:T(8,128)S(1)} custom-call(s32[1]{0:T(128)} %bitcast.core_ref, bf16[8,192,512]{2,1,0:T(8,128)(2,1)} %all-to-all-done.x_ref, f32[16,1,512]{2,1,0:T(1,128)S(1)} %bitcast.15, bf16[16,512,256]{2,1,0:T(8,128)(2,1)} %bitcast.25, bf16[16,512,256]{2,1,0:T(8,128)(2,1)} %bitcast.33, bf16[16,16,512]{2,1,0:T(8,128)(2,1)S(1)} %pad.5.gate_ref), custom_call_target="tpu_custom_call" | custom-call | flops 805306368 | bytes 6291456 | tf_op jit(solution)/shard_map/pallas_call | solution.py:182
  36.4 4.4 %shard_map.111 = (bf16[192,256]{1,0:T(8,128)(2,1)S(1)}, bf16[8,256,512]{2,1,0:T(8,128)(2,1)S(1)}, bf16[16,512]{1,0:T(8,128)(2,1)S(1)}, f32[2,128,128]{2,1,0:T(8,128)S(1)}, f32[2,128]{1,0:T(2,128)S(1)}) custom-call(s32[1]{0:T(128)} %bitcast.core_ref, bf16[208,512]{1,0:T(8,128)(2,1)S(1)} %concatenate.21.entered_ref, f32[192,640]{1,0:T(8,128)S(1)} %shard_map.109.sum_ref, ...), custom_call_target="tpu_custom_call" | custom-call | flops 805306368 | bytes 6291456 | tf_op jit(solution)/shard_map/pallas_call | solution.py:204
  40.8 0.6 collective-permute-start.2
  41.4 0.9 collective-permute-done.2.far_ref
  42.4 1.0 shard_map.112
  43.4 25.7 %all_to_all.40 = bf16[8,192,512]{2,1,0:T(8,128)(2,1)S(1)} all-to-all(bf16[8,192,512]{2,1,0:T(8,128)(2,1)S(1)} %shard_map.112), channel_id=1, replica_groups=mesh['y_lo'=2,'z'=8,'x'=4,'y_hi'=2,'core'=2] {'x','y_hi'}, dimensions={0} | all-to-all | bytes 3145728 | tf_op jit(solution)/shard_map/all_to_all | solution.py:244
  69.1 0.2 convert_reduce_fusion.3
  69.4 3.8 %collective-permute-start.3 = (bf16[208,512]{1,0:T(8,128)(2,1)S(1)}, bf16[208,512]{1,0:T(8,128)(2,1)S(1)}, u32[]{:S(2)}, u32[]{:S(2)}) collective-permute-start(bf16[208,512]{1,0:T(8,128)(2,1)S(1)} %pad_maximum_fusion.3), channel_id=1, source_target_pairs={{0,16},{16,32},{32,48},{48,64},{64,80},{80,96},{96,112},{112,128},... | collective-permute-start | bytes 638984 | tf_op jit(solution)/shard_map/ppermute | solution.py:40
  73.2 9.8 %collective-permute-done.3 = bf16[208,512]{1,0:T(8,128)(2,1)S(1)} collective-permute-done((bf16[208,512]{1,0:T(8,128)(2,1)S(1)}, bf16[208,512]{1,0:T(8,128)(2,1)S(1)}, u32[]{:S(2)}, u32[]{:S(2)}) %collective-permute-start.3) | collective-permute-done | bytes 213024 | tf_op jit(solution)/shard_map/ppermute | solution.py:40
  83.1 0.1 broadcast_in_dim.12
  83.2 23.8 %all_to_all.41.x_ref = bf16[8,192,512]{2,1,0:T(8,128)(2,1)S(1)} all-to-all(bf16[8,192,512]{2,1,0:T(8,128)(2,1)S(1)} %broadcast_in_dim.12), channel_id=1, replica_groups=mesh['y_lo'=2,'z'=8,'x'=4,'y_hi'=2,'core'=2] {'x','y_hi'}, dimensions={0} | all-to-all | bytes 3145728 | tf_op jit(solution)/shard_map/all_to_all | solution.py:244
  106.9 3.1 %shard_map.113.sum_ref = f32[192,640]{1,0:T(8,128)S(1)} custom-call(s32[1]{0:T(128)} %bitcast.core_ref, bf16[8,192,512]{2,1,0:T(8,128)(2,1)S(1)} %all_to_all.41.x_ref, f32[16,1,512]{2,1,0:T(1,128)S(1)} %bitcast.17, bf16[16,512,256]{2,1,0:T(8,128)(2,1)} %bitcast.27, bf16[16,512,256]{2,1,0:T(8,128)(2,1)} %bitcast.35, bf16[16,16,512]{2,1,0:T(8,128)(2,1)S(1)} %pad.5.gate_ref), custom_call_target="tpu_custom_call" | custom-call | flops 805306368 | bytes 6291456 | tf_op jit(solution)/shard_map/pallas_call | solution.py:182
  110.0 0.3 collective-permute-done.4.x_ref
  110.4 4.3 %shard_map.114 = (bf16[192,256]{1,0:T(8,128)(2,1)S(1)}, bf16[8,256,512]{2,1,0:T(8,128)(2,1)S(1)}, bf16[16,512]{1,0:T(8,128)(2,1)S(1)}, f32[2,128,128]{2,1,0:T(8,128)S(1)}, f32[2,128]{1,0:T(2,128)S(1)}) custom-call(s32[1]{0:T(128)} %bitcast.core_ref, bf16[208,512]{1,0:T(8,128)(2,1)S(1)} %broadcast_select_fusion.2.entered_ref, ...), custom_call_target="tpu_custom_call" | custom-call | flops 805306368 | bytes 6291456 | tf_op jit(solution)/shard_map/pallas_call | solution.py:204
  114.7 0.5 collective-permute-start.5
  115.1 1.1 collective-permute-done.5.far_ref
  116.2 1.0 shard_map.115
  117.2 25.7 %all_to_all.42 = bf16[8,192,512]{2,1,0:T(8,128)(2,1)S(1)} all-to-all(bf16[8,192,512]{2,1,0:T(8,128)(2,1)S(1)} %shard_map.115), channel_id=1, replica_groups=mesh['y_lo'=2,'z'=8,'x'=4,'y_hi'=2,'core'=2] {'x','y_hi'}, dimensions={0} | all-to-all | bytes 3145728 | tf_op jit(solution)/shard_map/all_to_all | solution.py:244
  143.0 0.2 convert_reduce_fusion.2
  143.3 1.9 collective-permute-start.6
  145.2 8.4 %collective-permute-done.6 = bf16[208,512]{1,0:T(8,128)(2,1)S(1)} collective-permute-done((bf16[208,512]{1,0:T(8,128)(2,1)S(1)}, bf16[208,512]{1,0:T(8,128)(2,1)S(1)}, u32[]{:S(2)}, u32[]{:S(2)}) %collective-permute-start.6) | collective-permute-done | bytes 213024 | tf_op jit(solution)/shard_map/ppermute | solution.py:40
  153.8 24.8 %all_to_all.43.x_ref = bf16[8,192,512]{2,1,0:T(8,128)(2,1)S(1)} all-to-all(bf16[8,192,512]{2,1,0:T(8,128)(2,1)S(1)} %broadcast_in_dim.13), channel_id=1, replica_groups=mesh['y_lo'=2,'z'=8,'x'=4,'y_hi'=2,'core'=2] {'x','y_hi'}, dimensions={0} | all-to-all | bytes 3145728 | tf_op jit(solution)/shard_map/all_to_all | solution.py:244
  178.5 3.1 %shard_map.116.sum_ref = f32[192,640]{1,0:T(8,128)S(1)} custom-call(s32[1]{0:T(128)} %bitcast.core_ref, bf16[8,192,512]{2,1,0:T(8,128)(2,1)S(1)} %all_to_all.43.x_ref, f32[16,1,512]{2,1,0:T(1,128)S(1)} %bitcast.19, bf16[16,512,256]{2,1,0:T(8,128)(2,1)} %bitcast.29, bf16[16,512,256]{2,1,0:T(8,128)(2,1)} %bitcast.37, bf16[16,16,512]{2,1,0:T(8,128)(2,1)S(1)} %pad.5.gate_ref), custom_call_target="tpu_custom_call" | custom-call | flops 805306368 | bytes 6291456 | tf_op jit(solution)/shard_map/pallas_call | solution.py:182
  181.6 0.3 collective-permute-done.7.x_ref
  181.9 4.3 %shard_map.117 = (bf16[192,256]{1,0:T(8,128)(2,1)S(1)}, bf16[8,256,512]{2,1,0:T(8,128)(2,1)S(1)}, bf16[16,512]{1,0:T(8,128)(2,1)S(1)}, f32[2,128,128]{2,1,0:T(8,128)S(1)}, f32[2,128]{1,0:T(2,128)S(1)}) custom-call(s32[1]{0:T(128)} %bitcast.core_ref, bf16[208,512]{1,0:T(8,128)(2,1)S(1)} %broadcast_select_fusion.1.entered_ref, ...), custom_call_target="tpu_custom_call" | custom-call | flops 805306368 | bytes 6291456 | tf_op jit(solution)/shard_map/pallas_call | solution.py:204
  186.3 0.3 collective-permute-start.8
  186.6 1.1 collective-permute-done.8.far_ref
  187.6 1.0 shard_map.118
  188.6 25.7 %all_to_all.44 = bf16[8,192,512]{2,1,0:T(8,128)(2,1)S(1)} all-to-all(bf16[8,192,512]{2,1,0:T(8,128)(2,1)S(1)} %shard_map.118), channel_id=1, replica_groups=mesh['y_lo'=2,'z'=8,'x'=4,'y_hi'=2,'core'=2] {'x','y_hi'}, dimensions={0} | all-to-all | bytes 3145728 | tf_op jit(solution)/shard_map/all_to_all | solution.py:244
  214.4 0.2 convert_reduce_fusion.1
  214.7 1.9 collective-permute-start.9
  216.6 9.9 %collective-permute-done.9 = bf16[208,512]{1,0:T(8,128)(2,1)S(1)} collective-permute-done((bf16[208,512]{1,0:T(8,128)(2,1)S(1)}, bf16[208,512]{1,0:T(8,128)(2,1)S(1)}, u32[]{:S(2)}, u32[]{:S(2)}) %collective-permute-start.9) | collective-permute-done | bytes 213024 | tf_op jit(solution)/shard_map/ppermute | solution.py:40
  226.6 0.1 broadcast_in_dim.14
  226.7 23.6 %all_to_all.45.x_ref = bf16[8,192,512]{2,1,0:T(8,128)(2,1)S(1)} all-to-all(bf16[8,192,512]{2,1,0:T(8,128)(2,1)S(1)} %broadcast_in_dim.14), channel_id=1, replica_groups=mesh['y_lo'=2,'z'=8,'x'=4,'y_hi'=2,'core'=2] {'x','y_hi'}, dimensions={0} | all-to-all | bytes 3145728 | tf_op jit(solution)/shard_map/all_to_all | solution.py:244
  250.3 2.8 shard_map.119.sum_ref
  253.0 0.6 collective-permute-done.10.x_ref
  253.7 3.7 %shard_map.120 = (bf16[192,256]{1,0:T(8,128)(2,1)S(1)}, bf16[8,256,512]{2,1,0:T(8,128)(2,1)S(1)}, bf16[16,512]{1,0:T(8,128)(2,1)}) custom-call(s32[1]{0:T(128)} %bitcast.core_ref, bf16[208,512]{1,0:T(8,128)(2,1)S(1)} %broadcast_select_fusion.entered_ref, f32[192,640]{1,0:T(8,128)S(1)} %shard_map.119.sum_ref, ...), custom_call_target="tpu_custom_call" | custom-call | flops 805306368 | bytes 6291456 | tf_op jit(solution)/shard_map/pallas_call | solution.py:204
  257.4 0.2 collective-permute-start.11
  257.6 1.2 collective-permute-done.11.far_ref
  258.8 1.0 shard_map.121
  259.8 25.7 %all_to_all.46 = bf16[8,192,512]{2,1,0:T(8,128)(2,1)S(1)} all-to-all(bf16[8,192,512]{2,1,0:T(8,128)(2,1)S(1)} %shard_map.121), channel_id=1, replica_groups=mesh['y_lo'=2,'z'=8,'x'=4,'y_hi'=2,'core'=2] {'x','y_hi'}, dimensions={0} | all-to-all | bytes 3145728 | tf_op jit(solution)/shard_map/all_to_all | solution.py:244
  285.4 0.2 convert_reduce_fusion
  285.7 0.7 add_convert_fusion
  (39 shorter events, 0.6 us)
Async XLA Ops:
  2.2 29.8 %all-to-all-start = ((bf16[8,192,512]{2,1,0:T(8,128)(2,1)}), bf16[8,192,512]{2,1,0:T(8,128)(2,1)}, u32[]{:S(2)}, u32[]{:S(2)}) async-start(bf16[8,192,512]{2,1,0:T(8,128)(2,1)} %broadcast_in_dim.10), calls=%async_computation | async-start | bytes 3145728 | tf_op jit(solution)/shard_map/all_to_all | solution.py:244
  8.3 24.5 %copy-start.3 = (bf16[192,512]{1,0:T(8,128)(2,1)S(1)}, bf16[192,512]{1,0:T(8,128)(2,1)}, u32[]{:S(2)}) copy-start(bf16[192,512]{1,0:T(8,128)(2,1)} %param.11) | copy-start | bytes 589828
  8.3 24.5 %copy-start.6 = (bf16[1,8192,2]{1,2,0:T(2,128)(2,1)S(1)}, bf16[1,8192,2]{1,2,0:T(2,128)(2,1)}, u32[]{:S(2)}) copy-start(bf16[1,8192,2]{1,2,0:T(2,128)(2,1)} %param.18) | copy-start | bytes 98308
  8.3 24.6 %copy-start.4 = (bf16[384,512]{1,0:T(8,128)(2,1)S(1)}, bf16[384,512]{1,0:T(8,128)(2,1)}, u32[]{:S(2)}) copy-start(bf16[384,512]{1,0:T(8,128)(2,1)} %param.13) | copy-start | bytes 1179652
  14.5 18.5 %copy-start.5 = (bf16[64,512]{1,0:T(8,128)(2,1)S(1)}, bf16[64,512]{1,0:T(8,128)(2,1)}, u32[]{:S(2)}) copy-start(bf16[64,512]{1,0:T(8,128)(2,1)} %param.14) | copy-start | bytes 196612
  14.5 18.6 %copy-start = (f32[1,8192]{1,0:T(1,128)S(1)}, f32[1,8192]{1,0:T(1,128)}, u32[]{:S(2)}) copy-start(f32[1,8192]{1,0:T(1,128)} %param.15) | copy-start | bytes 98308
  14.5 21.9 %collective-permute-start.1 = (bf16[8,256,512]{2,1,0:T(8,128)(2,1)}, bf16[8,256,512]{2,1,0:T(8,128)(2,1)}, u32[]{:S(2)}, u32[]{:S(2)}) collective-permute-start(bf16[8,256,512]{2,1,0:T(8,128)(2,1)} %get-tuple-element.33), channel_id=1, source_target_pairs={{0,1},{1,0},{2,3},{3,2},{4,5},{5,4},{6,7},{7,6},{8,9},{9,8},{10,11... | collective-permute-start | bytes 6291464 | tf_op jit(solution)/shard_map/ppermute | solution.py:36
  32.1 4.3 %collective-permute-start = (bf16[8,192,512]{2,1,0:T(8,128)(2,1)}, bf16[8,192,512]{2,1,0:T(8,128)(2,1)}, u32[]{:S(2)}, u32[]{:S(2)}) collective-permute-start(bf16[8,192,512]{2,1,0:T(8,128)(2,1)} %all-to-all-done.x_ref), channel_id=1, source_target_pairs={{0,1},{1,0},{2,3},{3,2},{4,5},{5,4},{6,7},{7,6},{8,9},{9,8},{10,11... | collective-permute-start | bytes 4718600 | tf_op jit(solution)/shard_map/ppermute | solution.py:36
  33.1 3.3 %copy-start.1 = (f32[1,2,128,128]{3,2,1,0:T(8,128)S(1)}, f32[1,2,128,128]{3,2,1,0:T(8,128)}, u32[]{:S(2)}) copy-start(f32[1,2,128,128]{3,2,1,0:T(8,128)} %param.20) | copy-start | bytes 393220
  33.1 3.3 %copy-start.2 = (f32[1,2,128]{2,1,0:T(2,128)S(1)}, f32[1,2,128]{2,1,0:T(2,128)}, u32[]{:S(2)}) copy-start(f32[1,2,128]{2,1,0:T(2,128)} %param.21) | copy-start | bytes 3076
  40.8 1.5 collective-permute-start.2
  69.4 13.6 %collective-permute-start.3 = (bf16[208,512]{1,0:T(8,128)(2,1)S(1)}, bf16[208,512]{1,0:T(8,128)(2,1)S(1)}, u32[]{:S(2)}, u32[]{:S(2)}) collective-permute-start(bf16[208,512]{1,0:T(8,128)(2,1)S(1)} %pad_maximum_fusion.3), channel_id=1, source_target_pairs={{0,16},{16,32},{32,48},{48,64},{64,80},{80,96},{96,112},{112,128},... | collective-permute-start | bytes 638984 | tf_op jit(solution)/shard_map/ppermute | solution.py:40
  106.9 3.4 %collective-permute-start.4 = (bf16[8,192,512]{2,1,0:T(8,128)(2,1)S(1)}, bf16[8,192,512]{2,1,0:T(8,128)(2,1)S(1)}, u32[]{:S(2)}, u32[]{:S(2)}) collective-permute-start(bf16[8,192,512]{2,1,0:T(8,128)(2,1)S(1)} %all_to_all.41.x_ref), channel_id=1, source_target_pairs={{0,1},{1,0},{2,3},{3,2},{4,5},{5,4},{6,7},{7,6},{8,9},{9,8},{10,11... | collective-permute-start | bytes 4718600 | tf_op jit(solution)/shard_map/ppermute | solution.py:36
  114.7 1.6 collective-permute-start.5
  143.3 10.3 %collective-permute-start.6 = (bf16[208,512]{1,0:T(8,128)(2,1)S(1)}, bf16[208,512]{1,0:T(8,128)(2,1)S(1)}, u32[]{:S(2)}, u32[]{:S(2)}) collective-permute-start(bf16[208,512]{1,0:T(8,128)(2,1)S(1)} %pad_maximum_fusion.4), channel_id=1, source_target_pairs={{0,16},{16,32},{32,48},{48,64},{64,80},{80,96},{96,112},{112,128},... | collective-permute-start | bytes 638984 | tf_op jit(solution)/shard_map/ppermute | solution.py:40
  178.5 3.4 %collective-permute-start.7 = (bf16[8,192,512]{2,1,0:T(8,128)(2,1)S(1)}, bf16[8,192,512]{2,1,0:T(8,128)(2,1)S(1)}, u32[]{:S(2)}, u32[]{:S(2)}) collective-permute-start(bf16[8,192,512]{2,1,0:T(8,128)(2,1)S(1)} %all_to_all.43.x_ref), channel_id=1, source_target_pairs={{0,1},{1,0},{2,3},{3,2},{4,5},{5,4},{6,7},{7,6},{8,9},{9,8},{10,11... | collective-permute-start | bytes 4718600 | tf_op jit(solution)/shard_map/ppermute | solution.py:36
  186.3 1.4 collective-permute-start.8
  214.7 11.8 %collective-permute-start.9 = (bf16[208,512]{1,0:T(8,128)(2,1)S(1)}, bf16[208,512]{1,0:T(8,128)(2,1)S(1)}, u32[]{:S(2)}, u32[]{:S(2)}) collective-permute-start(bf16[208,512]{1,0:T(8,128)(2,1)S(1)} %pad_maximum_fusion.5), channel_id=1, source_target_pairs={{0,16},{16,32},{32,48},{48,64},{64,80},{80,96},{96,112},{112,128},... | collective-permute-start | bytes 638984 | tf_op jit(solution)/shard_map/ppermute | solution.py:40
  250.3 3.4 %collective-permute-start.10 = (bf16[8,192,512]{2,1,0:T(8,128)(2,1)S(1)}, bf16[8,192,512]{2,1,0:T(8,128)(2,1)S(1)}, u32[]{:S(2)}, u32[]{:S(2)}) collective-permute-start(bf16[8,192,512]{2,1,0:T(8,128)(2,1)S(1)} %all_to_all.45.x_ref), channel_id=1, source_target_pairs={{0,1},{1,0},{2,3},{3,2},{4,5},{5,4},{6,7},{7,6},{8,9},{9,8},{10,11... | collective-permute-start | bytes 4718600 | tf_op jit(solution)/shard_map/ppermute | solution.py:36
  257.4 1.4 collective-permute-start.11
